TPU v7x, 256 devices: a whole 4x4x8 slice. The times are simulated.
256 devices in a mesh: gx: 16 (over y, x), gy: 8 (over z), gz: 2 (over core).
Axes of the slice: x: 4, y: 4, z: 8, core: 2. Of those that a mesh axis runs over, the one named last changes fastest.
Arguments:
- electric_x: float32 [512, 128, 1024], P('gx', 'gy', 'gz'), may hold values from -32 to 32
- electric_z: float32 [512, 128, 1024], P('gx', 'gy', 'gz'), may hold values from -32 to 32
- magnetic_x: float32 [512, 128, 1024], P('gx', 'gy', 'gz'), may hold values from -3 to 3
- magnetic_y: float32 [512, 128, 1024], P('gx', 'gy', 'gz'), may hold values from -3 to 3
- magnetic_z: float32 [512, 128, 1024], P('gx', 'gy', 'gz'), may hold values from -3 to 3
- material: int32 [512, 128, 1024], P('gx', 'gy', 'gz'), may hold values from 0 to 15
- perm_table: float32 [16], replicated, may hold values from 1 to 12
Outputs:
- electric_x_half: float32 [512, 128, 1024], P('gx', 'gy', 'gz')
- electric_z_half: float32 [512, 128, 1024], P('gx', 'gy', 'gz')
All inputs are finite; a program needn't handle non-finite values.
Results may differ from a plain program's by a relative error of at most 0.00021.
Values sent between devices are 32-bit elements; how exact they have to be, the bound alone decides.
No kernel may reach another device: no remote copies, remote signals or barrier semaphores. Data moves between devices by JAX's collectives and lax.ppermute only.
A program may use at most 192 MiB of HBM per device.

v0:
```python
import jax
import jax.numpy as jnp
from jax import lax
from jax.sharding import PartitionSpec as P

step_ratio = 1600.0
curl_scale = 40.0


def shifted(x, axis, by):
    length = lax.axis_size(axis)
    pairs = [(i, i + by) for i in range(length) if 0 <= i + by < length]
    return lax.ppermute(x, axis, pairs)


def row_of(field_data, position, line_dim):
    return lax.index_in_dim(field_data, position, line_dim, keepdims=False)


def lower_diff(field_data, below_plane, line_dim):
    earlier = jnp.concatenate(
        [
            jnp.expand_dims(below_plane, line_dim),
            lax.slice_in_dim(field_data, 0, field_data.shape[line_dim] - 1, axis=line_dim),
        ],
        axis=line_dim,
    )
    return field_data - earlier


def lookup(material, perm_table):
    looked_up = jnp.zeros(material.shape, jnp.float32)
    for material_id in range(perm_table.shape[0]):
        looked_up = jnp.where(material == material_id, perm_table[material_id], looked_up)
    return looked_up


def partition_solve(line_ratio, source, line_dim, first_device, last_device, from_next, reduced):
    row_count = line_ratio.shape[line_dim]
    interior = row_count - 1
    ratio_rows = [row_of(line_ratio, position, line_dim) for position in range(row_count)]
    source_rows = [row_of(source, position, line_dim) for position in range(row_count)]
    lower_band = [-reduced_row for reduced_row in ratio_rows]
    upper_band = [-reduced_row for reduced_row in ratio_rows]
    lower_band[0] = jnp.where(first_device, 0.0, lower_band[0])
    upper_band[row_count - 1] = jnp.where(last_device, 0.0, upper_band[row_count - 1])
    main_band = [1.0 + 2.0 * reduced_row for reduced_row in ratio_rows]
    zero_row = jnp.zeros_like(ratio_rows[0])
    factors, sweep_g, sweep_u, sweep_w = ([], [], [], [])
    for position in range(interior):
        if position == 0:
            pivot_value = main_band[0]
            part_g = source_rows[0]
            part_u = -lower_band[0]
            part_w = zero_row
        else:
            pivot_value = main_band[position] - lower_band[position] * factors[position - 1]
            part_g = source_rows[position] - lower_band[position] * sweep_g[position - 1]
            part_u = -lower_band[position] * sweep_u[position - 1]
            part_w = -lower_band[position] * sweep_w[position - 1]
        if position == interior - 1:
            part_w = part_w - upper_band[position]
        factors.append(upper_band[position] / pivot_value)
        sweep_g.append(part_g / pivot_value)
        sweep_u.append(part_u / pivot_value)
        sweep_w.append(part_w / pivot_value)
    solve_g = list(sweep_g)
    solve_u = list(sweep_u)
    solve_w = list(sweep_w)
    for position in range(interior - 2, -1, -1):
        solve_g[position] = sweep_g[position] - factors[position] * solve_g[position + 1]
        solve_u[position] = sweep_u[position] - factors[position] * solve_u[position + 1]
        solve_w[position] = sweep_w[position] - factors[position] * solve_w[position + 1]
    head_g, head_u, head_w = from_next((solve_g[0], solve_u[0], solve_w[0]))
    separator = row_count - 1
    reduced_lower = lower_band[separator] * solve_u[interior - 1]
    reduced_main = (
        main_band[separator]
        + lower_band[separator] * solve_w[interior - 1]
        + upper_band[separator] * head_u
    )
    reduced_upper = upper_band[separator] * head_w
    reduced_source = (
        source_rows[separator]
        - lower_band[separator] * solve_g[interior - 1]
        - upper_band[separator] * head_g
    )
    solved_before, solved_here = reduced(reduced_lower, reduced_main, reduced_upper, reduced_source)
    result_rows = [
        solve_g[position] + solved_before * solve_u[position] + solved_here * solve_w[position]
        for position in range(interior)
    ]
    result_rows.append(solved_here)
    return jnp.stack(result_rows, axis=line_dim)


def cyclic_reduce(
    reduced_lower,
    reduced_main,
    reduced_upper,
    reduced_source,
    place,
    device_count,
    from_below,
    from_above,
):
    depth_count = (device_count - 1).bit_length()
    for depth_level in range(depth_count):
        stride = 1 << depth_level
        below_rows = from_below(
            (reduced_lower, reduced_main, reduced_upper, reduced_source), stride
        )
        above_rows = from_above(
            (reduced_lower, reduced_main, reduced_upper, reduced_source), stride
        )
        below_main = jnp.where(place >= stride, below_rows[1], 1.0)
        above_main = jnp.where(place + stride < device_count, above_rows[1], 1.0)
        left_factor = reduced_lower / below_main
        right_factor = reduced_upper / above_main
        reduced_lower, reduced_main, reduced_upper, reduced_source = (
            -left_factor * below_rows[0],
            reduced_main - left_factor * below_rows[2] - right_factor * above_rows[0],
            -right_factor * above_rows[2],
            reduced_source - left_factor * below_rows[3] - right_factor * above_rows[3],
        )
    return reduced_source / reduced_main


def per_device(electric_x, electric_z, magnetic_x, magnetic_y, magnetic_z, material, perm_table):
    permittivity = lookup(material, perm_table)
    curl_factor = curl_scale / permittivity
    line_ratio = step_ratio / permittivity
    rim_along_x = shifted(magnetic_y[-1], "gx", 1)
    rim_mag_z, rim_mag_x = shifted((magnetic_z[:, -1], magnetic_x[:, -1]), "gy", 1)
    rim_along_z = shifted(magnetic_y[:, :, -1], "gz", 1)
    x_source = electric_x + curl_factor * (
        lower_diff(magnetic_z, rim_mag_z, 1) - lower_diff(magnetic_y, rim_along_z, 2)
    )
    z_source = electric_z + curl_factor * (
        lower_diff(magnetic_y, rim_along_x, 0) - lower_diff(magnetic_x, rim_mag_x, 1)
    )
    place_x = lax.axis_index("gx")
    count_x = lax.axis_size("gx")

    def next_along_x(values):
        return shifted(values, "gx", -1)

    def reduced_along_x(reduced_lower, reduced_main, reduced_upper, reduced_source):

        def below_x(values, stride):
            return shifted(values, "gx", stride)

        def above_x(values, stride):
            return shifted(values, "gx", -stride)

        solved_here = cyclic_reduce(
            reduced_lower,
            reduced_main,
            reduced_upper,
            reduced_source,
            place_x,
            count_x,
            below_x,
            above_x,
        )
        solved_before = shifted(solved_here, "gx", 1)
        return (solved_before, solved_here)

    electric_z_half = partition_solve(
        line_ratio, z_source, 0, place_x == 0, place_x == count_x - 1, next_along_x, reduced_along_x
    )
    place_y = lax.axis_index("gy")
    count_y = lax.axis_size("gy")

    def next_along_y(values):
        return shifted(values, "gy", -1)

    def below_y(values, stride):
        return shifted(values, "gy", stride)

    def above_y(values, stride):
        return shifted(values, "gy", -stride)

    def reduced_along_y(reduced_lower, reduced_main, reduced_upper, reduced_source):
        solved_here = cyclic_reduce(
            reduced_lower,
            reduced_main,
            reduced_upper,
            reduced_source,
            place_y,
            count_y,
            below_y,
            above_y,
        )
        solved_before = shifted(solved_here, "gy", 1)
        return (solved_before, solved_here)

    electric_x_half = partition_solve(
        line_ratio, x_source, 1, place_y == 0, place_y == count_y - 1, next_along_y, reduced_along_y
    )
    return (electric_x_half, electric_z_half)


def solution(mesh):
    placed = (
        P("gx", "gy", "gz"),
        P("gx", "gy", "gz"),
        P("gx", "gy", "gz"),
        P("gx", "gy", "gz"),
        P("gx", "gy", "gz"),
        P("gx", "gy", "gz"),
        P(),
    )
    return jax.shard_map(
        per_device,
        mesh=mesh,
        in_specs=placed,
        out_specs=(P("gx", "gy", "gz"), P("gx", "gy", "gz")),
        check_vma=False,
    )
```

profile of v0, /device:TPU:32, one launch (start us, length us, event | category | flops | bytes accessed | tf_op | source)
XLA Modules:
  0.0 274.4 jit_solution(11967642351302392655)
XLA Ops:
  0.6 1.4 slice_bitcast_fusion.62
  2.0 3.4 %collective-permute-start.28 = (f32[16,512]{1,0:T(8,128)}, f32[16,512]{1,0:T(8,128)S(1)}, u32[]{:S(2)}, u32[]{:S(2)}) collective-permute-start(f32[16,512]{1,0:T(8,128)} %slice_bitcast_fusion.62), channel_id=1, source_target_pairs={{0,16},{16,32},{32,48},{48,64},{64,80},{80,96},{96,112},{112,128},... | collective-permute-start | bytes 98312 | tf_op jit(solution)/shard_map/ppermute | solution.py:13
  7.1 3.8 %collective-permute-start.29 = (f32[32,512]{1,0:T(8,128)}, f32[32,512]{1,0:T(8,128)}, u32[]{:S(2)}, u32[]{:S(2)}) collective-permute-start(f32[32,512]{1,0:T(8,128)} %bitcast.1838), channel_id=1, source_target_pairs={{0,2},{2,4},{4,6},{6,8},{8,10},{10,12},{12,14},{1,3},{3,5},{5,7},{... | collective-permute-start | bytes 196616 | tf_op jit(solution)/shard_map/ppermute | solution.py:13
  12.1 3.8 %collective-permute-start = (f32[32,512]{1,0:T(8,128)S(1)}, f32[32,512]{1,0:T(8,128)S(1)}, u32[]{:S(2)}, u32[]{:S(2)}) collective-permute-start(f32[32,512]{1,0:T(8,128)S(1)} %bitcast.1846), channel_id=1, source_target_pairs={{0,2},{2,4},{4,6},{6,8},{8,10},{10,12},{12,14},{1,3},{3,5},{5,7},{... | collective-permute-start | bytes 196616 | tf_op jit(solution)/shard_map/ppermute | solution.py:13
  20.9 12.8 %fusion.4 = (f32[32,16,512]{2,1,0:T(8,128)S(1)}, f32[32,16,512]{2,1,0:T(8,128)S(1)}) fusion(f32[32,16,512]{2,1,0:T(8,128)} %param.8, f32[32,16,512]{2,1,0:T(8,128)S(1)} %copy-done, f32[31,16,512]{2,1,0:T(8,128)S(1)} %slice-done, f32[1,16,512]{2,1,0:T(8,128)S(1)} %bitcast.1847, f32[32,16,512]{2,1,0:T(8,128)S(1)} %copy-done.1, ...), kind=kLoop, calls=%fused_computation.7 | loop fusion | flops 10485760 | bytes 8388672 | tf_op jit(solution)/shard_map/add | solution.py:139
  35.1 1.8 copy_divide_fusion
  43.6 1.4 collective-permute-done.31
  45.0 1.9 collective-permute-done.30
  47.0 1.3 collective-permute-start.36
  48.3 4.5 %collective-permute-start.33 = (f32[16,512]{1,0:T(8,128)S(1)}, f32[16,512]{1,0:T(8,128)S(1)}, u32[]{:S(2)}, u32[]{:S(2)}) collective-permute-start(f32[16,512]{1,0:T(8,128)S(1)} %get-tuple-element.284), channel_id=1, source_target_pairs={{0,16},{16,32},{32,48},{48,64},{64,80},{80,96},{96,112},{112,128},... | collective-permute-start | bytes 98312 | tf_op jit(solution)/shard_map/ppermute | solution.py:13
  54.1 4.6 %collective-permute-start.32 = (f32[16,512]{1,0:T(8,128)S(1)}, f32[16,512]{1,0:T(8,128)S(1)}, u32[]{:S(2)}, u32[]{:S(2)}) collective-permute-start(f32[16,512]{1,0:T(8,128)S(1)} %get-tuple-element.283), channel_id=1, source_target_pairs={{0,16},{16,32},{32,48},{48,64},{64,80},{80,96},{96,112},{112,128},... | collective-permute-start | bytes 98312 | tf_op jit(solution)/shard_map/ppermute | solution.py:13
  61.6 5.3 %collective-permute-start.38 = (f32[16,512]{1,0:T(8,128)S(1)}, f32[16,512]{1,0:T(8,128)S(1)}, u32[]{:S(2)}, u32[]{:S(2)}) collective-permute-start(f32[16,512]{1,0:T(8,128)S(1)} %get-tuple-element.20), channel_id=1, source_target_pairs={{0,16},{16,32},{32,48},{48,64},{64,80},{80,96},{96,112},{112,128},... | collective-permute-start | bytes 98312 | tf_op jit(solution)/shard_map/ppermute | solution.py:13
  68.5 10.8 %collective-permute-start.41 = (f32[16,512]{1,0:T(8,128)S(1)}, f32[16,512]{1,0:T(8,128)S(1)}, u32[]{:S(2)}, u32[]{:S(2)}) collective-permute-start(f32[16,512]{1,0:T(8,128)S(1)} %get-tuple-element.18), channel_id=1, source_target_pairs={{0,32},{16,48},{32,64},{48,80},{64,96},{80,112},{96,128},{112,144}... | collective-permute-start | bytes 98312 | tf_op jit(solution)/shard_map/ppermute | solution.py:13
  80.6 6.4 %collective-permute-start.37 = (f32[16,512]{1,0:T(8,128)S(1)}, f32[16,512]{1,0:T(8,128)S(1)}, u32[]{:S(2)}, u32[]{:S(2)}) collective-permute-start(f32[16,512]{1,0:T(8,128)S(1)} %get-tuple-element.22), channel_id=1, source_target_pairs={{0,16},{16,32},{32,48},{48,64},{64,80},{80,96},{96,112},{112,128},... | collective-permute-start | bytes 98312 | tf_op jit(solution)/shard_map/ppermute | solution.py:13
  88.3 7.6 %collective-permute-start.40 = (f32[16,512]{1,0:T(8,128)S(1)}, f32[16,512]{1,0:T(8,128)S(1)}, u32[]{:S(2)}, u32[]{:S(2)}) collective-permute-start(f32[16,512]{1,0:T(8,128)S(1)} %multiply_subtract_fusion.64), channel_id=1, source_target_pairs={{0,32},{16,48},{32,64},{48,80},{64,96},{80,112},{96,128},{112,144}... | collective-permute-start | bytes 98312 | tf_op jit(solution)/shard_map/ppermute | solution.py:13
  98.8 7.0 %collective-permute-start.46 = (f32[16,512]{1,0:T(8,128)S(1)}, f32[16,512]{1,0:T(8,128)S(1)}, u32[]{:S(2)}, u32[]{:S(2)}) collective-permute-start(f32[16,512]{1,0:T(8,128)S(1)} %get-tuple-element.15), channel_id=1, source_target_pairs={{0,32},{16,48},{32,64},{48,80},{64,96},{80,112},{96,128},{112,144}... | collective-permute-start | bytes 98312 | tf_op jit(solution)/shard_map/ppermute | solution.py:13
  106.1 2.0 collective-permute-start.3
  108.1 1.9 collective-permute-start.2
  110.0 1.3 collective-permute-start.52
  111.4 7.8 %collective-permute-start.49 = (f32[16,512]{1,0:T(8,128)S(1)}, f32[16,512]{1,0:T(8,128)S(1)}, u32[]{:S(2)}, u32[]{:S(2)}) collective-permute-start(f32[16,512]{1,0:T(8,128)S(1)} %get-tuple-element.13), channel_id=1, source_target_pairs={{0,64},{16,80},{32,96},{48,112},{64,128},{80,144},{96,160},{112,17... | collective-permute-start | bytes 98312 | tf_op jit(solution)/shard_map/ppermute | solution.py:13
  120.5 6.1 %collective-permute-start.45 = (f32[16,512]{1,0:T(8,128)S(1)}, f32[16,512]{1,0:T(8,128)S(1)}, u32[]{:S(2)}, u32[]{:S(2)}) collective-permute-start(f32[16,512]{1,0:T(8,128)S(1)} %get-tuple-element.17), channel_id=1, source_target_pairs={{0,32},{16,48},{32,64},{48,80},{64,96},{80,112},{96,128},{112,144}... | collective-permute-start | bytes 98312 | tf_op jit(solution)/shard_map/ppermute | solution.py:13
  127.9 4.6 %collective-permute-start.48 = (f32[16,512]{1,0:T(8,128)S(1)}, f32[16,512]{1,0:T(8,128)S(1)}, u32[]{:S(2)}, u32[]{:S(2)}) collective-permute-start(f32[16,512]{1,0:T(8,128)S(1)} %multiply_subtract_fusion.62), channel_id=1, source_target_pairs={{0,64},{16,80},{32,96},{48,112},{64,128},{80,144},{96,160},{112,17... | collective-permute-start | bytes 98312 | tf_op jit(solution)/shard_map/ppermute | solution.py:13
  132.5 1.9 collective-permute-start.6
  134.5 1.9 collective-permute-start.8
  136.4 4.9 %collective-permute-start.5 = (f32[32,512]{1,0:T(8,128)S(1)}, f32[32,512]{1,0:T(8,128)S(1)}, u32[]{:S(2)}, u32[]{:S(2)}) collective-permute-start(f32[32,512]{1,0:T(8,128)S(1)} %get-tuple-element.276), channel_id=1, source_target_pairs={{0,2},{2,4},{4,6},{6,8},{8,10},{10,12},{12,14},{1,3},{3,5},{5,7},{... | collective-permute-start | bytes 196616 | tf_op jit(solution)/shard_map/ppermute | solution.py:13
  141.4 1.9 collective-permute-start.7
  143.3 3.9 %collective-permute-start.4 = (f32[32,512]{1,0:T(8,128)S(1)}, f32[32,512]{1,0:T(8,128)S(1)}, u32[]{:S(2)}, u32[]{:S(2)}) collective-permute-start(f32[32,512]{1,0:T(8,128)S(1)} %get-tuple-element.275), channel_id=1, source_target_pairs={{0,2},{2,4},{4,6},{6,8},{8,10},{10,12},{12,14},{1,3},{3,5},{5,7},{... | collective-permute-start | bytes 196616 | tf_op jit(solution)/shard_map/ppermute | solution.py:13
  148.6 4.6 %collective-permute-start.54 = (f32[16,512]{1,0:T(8,128)S(1)}, f32[16,512]{1,0:T(8,128)S(1)}, u32[]{:S(2)}, u32[]{:S(2)}) collective-permute-start(f32[16,512]{1,0:T(8,128)S(1)} %get-tuple-element.10), channel_id=1, source_target_pairs={{0,64},{16,80},{32,96},{48,112},{64,128},{80,144},{96,160},{112,17... | collective-permute-start | bytes 98312 | tf_op jit(solution)/shard_map/ppermute | solution.py:13
  154.5 4.6 %collective-permute-start.53 = (f32[16,512]{1,0:T(8,128)S(1)}, f32[16,512]{1,0:T(8,128)S(1)}, u32[]{:S(2)}, u32[]{:S(2)}) collective-permute-start(f32[16,512]{1,0:T(8,128)S(1)} %get-tuple-element.12), channel_id=1, source_target_pairs={{0,64},{16,80},{32,96},{48,112},{64,128},{80,144},{96,160},{112,17... | collective-permute-start | bytes 98312 | tf_op jit(solution)/shard_map/ppermute | solution.py:13
  160.4 1.9 collective-permute-start.11
  162.4 5.8 %collective-permute-start.10 = (f32[32,512]{1,0:T(8,128)S(1)}, f32[32,512]{1,0:T(8,128)S(1)}, u32[]{:S(2)}, u32[]{:S(2)}) collective-permute-start(f32[32,512]{1,0:T(8,128)S(1)} %get-tuple-element.164), channel_id=1, source_target_pairs={{0,2},{2,4},{4,6},{6,8},{8,10},{10,12},{12,14},{1,3},{3,5},{5,7},{... | collective-permute-start | bytes 196616 | tf_op jit(solution)/shard_map/ppermute | solution.py:13
  169.5 6.0 %collective-permute-start.57 = (f32[16,512]{1,0:T(8,128)S(1)}, f32[16,512]{1,0:T(8,128)S(1)}, u32[]{:S(2)}, u32[]{:S(2)}) collective-permute-start(f32[16,512]{1,0:T(8,128)S(1)} %get-tuple-element.8), channel_id=1, source_target_pairs={{0,128},{16,144},{32,160},{48,176},{64,192},{80,208},{96,224},{112... | collective-permute-start | bytes 98312 | tf_op jit(solution)/shard_map/ppermute | solution.py:13
  176.9 6.0 %collective-permute-start.56 = (f32[16,512]{1,0:T(8,128)S(1)}, f32[16,512]{1,0:T(8,128)S(1)}, u32[]{:S(2)}, u32[]{:S(2)}) collective-permute-start(f32[16,512]{1,0:T(8,128)S(1)} %get-tuple-element.281), channel_id=1, source_target_pairs={{0,128},{16,144},{32,160},{48,176},{64,192},{80,208},{96,224},{112... | collective-permute-start | bytes 98312 | tf_op jit(solution)/shard_map/ppermute | solution.py:13
  184.3 6.0 %collective-permute-start.61 = (f32[16,512]{1,0:T(8,128)S(1)}, f32[16,512]{1,0:T(8,128)S(1)}, u32[]{:S(2)}, u32[]{:S(2)}) collective-permute-start(f32[16,512]{1,0:T(8,128)S(1)} %get-tuple-element.280), channel_id=1, source_target_pairs={{0,128},{16,144},{32,160},{48,176},{64,192},{80,208},{96,224},{112... | collective-permute-start | bytes 98312 | tf_op jit(solution)/shard_map/ppermute | solution.py:13
  190.4 7.8 %collective-permute-start.13 = (f32[32,512]{1,0:T(8,128)S(1)}, f32[32,512]{1,0:T(8,128)S(1)}, u32[]{:S(2)}, u32[]{:S(2)}) collective-permute-start(f32[32,512]{1,0:T(8,128)S(1)} %get-tuple-element.162), channel_id=1, source_target_pairs={{0,4},{2,6},{4,8},{6,10},{8,12},{10,14},{1,5},{3,7},{5,9},{7,11},{... | collective-permute-start | bytes 196616 | tf_op jit(solution)/shard_map/ppermute | solution.py:13
  198.2 1.9 collective-permute-start.14
  200.1 3.9 %collective-permute-start.9 = (f32[32,512]{1,0:T(8,128)S(1)}, f32[32,512]{1,0:T(8,128)S(1)}, u32[]{:S(2)}, u32[]{:S(2)}) collective-permute-start(f32[32,512]{1,0:T(8,128)S(1)} %get-tuple-element.166), channel_id=1, source_target_pairs={{0,2},{2,4},{4,6},{6,8},{8,10},{10,12},{12,14},{1,3},{3,5},{5,7},{... | collective-permute-start | bytes 196616 | tf_op jit(solution)/shard_map/ppermute | solution.py:13
  205.4 6.8 %collective-permute-start.12 = (f32[32,512]{1,0:T(8,128)S(1)}, f32[32,512]{1,0:T(8,128)S(1)}, u32[]{:S(2)}, u32[]{:S(2)}) collective-permute-start(f32[32,512]{1,0:T(8,128)S(1)} %multiply_subtract_fusion.2), channel_id=1, source_target_pairs={{0,4},{2,6},{4,8},{6,10},{8,12},{10,14},{1,5},{3,7},{5,9},{7,11},{... | collective-permute-start | bytes 196616 | tf_op jit(solution)/shard_map/ppermute | solution.py:13
  212.3 5.4 %collective-permute-start.63 = (f32[16,512]{1,0:T(8,128)S(1)}, f32[16,512]{1,0:T(8,128)S(1)}, u32[]{:S(2)}, u32[]{:S(2)}) collective-permute-start(f32[16,512]{1,0:T(8,128)S(1)} %subtract_divide_fusion.2), channel_id=1, source_target_pairs={{0,16},{16,32},{32,48},{48,64},{64,80},{80,96},{96,112},{112,128},... | collective-permute-start | bytes 98312 | tf_op jit(solution)/shard_map/ppermute | solution.py:13
  219.1 6.7 %collective-permute-start.18 = (f32[32,512]{1,0:T(8,128)S(1)}, f32[32,512]{1,0:T(8,128)S(1)}, u32[]{:S(2)}, u32[]{:S(2)}) collective-permute-start(f32[32,512]{1,0:T(8,128)S(1)} %get-tuple-element.159), channel_id=1, source_target_pairs={{0,4},{2,6},{4,8},{6,10},{8,12},{10,14},{1,5},{3,7},{5,9},{7,11},{... | collective-permute-start | bytes 196616 | tf_op jit(solution)/shard_map/ppermute | solution.py:13
  227.1 6.7 %collective-permute-start.17 = (f32[32,512]{1,0:T(8,128)S(1)}, f32[32,512]{1,0:T(8,128)S(1)}, u32[]{:S(2)}, u32[]{:S(2)}) collective-permute-start(f32[32,512]{1,0:T(8,128)S(1)} %get-tuple-element.161), channel_id=1, source_target_pairs={{0,4},{2,6},{4,8},{6,10},{8,12},{10,14},{1,5},{3,7},{5,9},{7,11},{... | collective-permute-start | bytes 196616 | tf_op jit(solution)/shard_map/ppermute | solution.py:13
  235.9 8.5 %collective-permute-start.21 = (f32[32,512]{1,0:T(8,128)S(1)}, f32[32,512]{1,0:T(8,128)S(1)}, u32[]{:S(2)}, u32[]{:S(2)}) collective-permute-start(f32[32,512]{1,0:T(8,128)S(1)} %get-tuple-element.157), channel_id=1, source_target_pairs={{0,8},{2,10},{4,12},{6,14},{1,9},{3,11},{5,13},{7,15},{16,24},{18,... | collective-permute-start | bytes 196616 | tf_op jit(solution)/shard_map/ppermute | solution.py:13
  245.7 8.5 %collective-permute-start.20 = (f32[32,512]{1,0:T(8,128)S(1)}, f32[32,512]{1,0:T(8,128)S(1)}, u32[]{:S(2)}, u32[]{:S(2)}) collective-permute-start(f32[32,512]{1,0:T(8,128)S(1)} %get-tuple-element.278), channel_id=1, source_target_pairs={{0,8},{2,10},{4,12},{6,14},{1,9},{3,11},{5,13},{7,15},{16,24},{18,... | collective-permute-start | bytes 196616 | tf_op jit(solution)/shard_map/ppermute | solution.py:13
  255.5 8.5 %collective-permute-start.25 = (f32[32,512]{1,0:T(8,128)S(1)}, f32[32,512]{1,0:T(8,128)S(1)}, u32[]{:S(2)}, u32[]{:S(2)}) collective-permute-start(f32[32,512]{1,0:T(8,128)S(1)} %get-tuple-element.277), channel_id=1, source_target_pairs={{0,8},{2,10},{4,12},{6,14},{1,9},{3,11},{5,13},{7,15},{16,24},{18,... | collective-permute-start | bytes 196616 | tf_op jit(solution)/shard_map/ppermute | solution.py:13
  264.3 1.6 collective-permute-done.25
  265.9 3.4 %collective-permute-start.27 = (f32[32,512]{1,0:T(8,128)S(1)}, f32[32,512]{1,0:T(8,128)S(1)}, u32[]{:S(2)}, u32[]{:S(2)}) collective-permute-start(f32[32,512]{1,0:T(8,128)S(1)} %subtract_divide_fusion), channel_id=1, source_target_pairs={{0,2},{2,4},{4,6},{6,8},{8,10},{10,12},{12,14},{1,3},{3,5},{5,7},{... | collective-permute-start | bytes 196616 | tf_op jit(solution)/shard_map/ppermute | solution.py:13
  269.4 2.8 %collective-permute-done.27 = f32[32,512]{1,0:T(8,128)S(1)} collective-permute-done((f32[32,512]{1,0:T(8,128)S(1)}, f32[32,512]{1,0:T(8,128)S(1)}, u32[]{:S(2)}, u32[]{:S(2)}) %collective-permute-start.27) | collective-permute-done | bytes 65568 | tf_op jit(solution)/shard_map/ppermute | solution.py:13
  272.8 1.6 copy.149
  (181 shorter events, 47.6 us)
Async XLA Ops:
  2.0 18.7 %collective-permute-start.28 = (f32[16,512]{1,0:T(8,128)}, f32[16,512]{1,0:T(8,128)S(1)}, u32[]{:S(2)}, u32[]{:S(2)}) collective-permute-start(f32[16,512]{1,0:T(8,128)} %slice_bitcast_fusion.62), channel_id=1, source_target_pairs={{0,16},{16,32},{32,48},{48,64},{64,80},{80,96},{96,112},{112,128},... | collective-permute-start | bytes 98312 | tf_op jit(solution)/shard_map/ppermute | solution.py:13
  12.1 21.7 %collective-permute-start = (f32[32,512]{1,0:T(8,128)S(1)}, f32[32,512]{1,0:T(8,128)S(1)}, u32[]{:S(2)}, u32[]{:S(2)}) collective-permute-start(f32[32,512]{1,0:T(8,128)S(1)} %bitcast.1846), channel_id=1, source_target_pairs={{0,2},{2,4},{4,6},{6,8},{8,10},{10,12},{12,14},{1,3},{3,5},{5,7},{... | collective-permute-start | bytes 196616 | tf_op jit(solution)/shard_map/ppermute | solution.py:13
  42.3 16.7 %collective-permute-start.34 = (f32[16,512]{1,0:T(8,128)S(1)}, f32[16,512]{1,0:T(8,128)S(1)}, u32[]{:S(2)}, u32[]{:S(2)}) collective-permute-start(f32[16,512]{1,0:T(8,128)S(1)} %get-tuple-element.99), channel_id=1, source_target_pairs={{16,0},{32,16},{48,32},{64,48},{80,64},{96,80},{112,96},{128,112},... | collective-permute-start | bytes 98312 | tf_op jit(solution)/shard_map/ppermute | solution.py:13
  60.3 20.3 %collective-permute-start.39 = (f32[16,512]{1,0:T(8,128)S(1)}, f32[16,512]{1,0:T(8,128)S(1)}, u32[]{:S(2)}, u32[]{:S(2)}) collective-permute-start(f32[16,512]{1,0:T(8,128)S(1)} %get-tuple-element.22), channel_id=1, source_target_pairs={{16,0},{32,16},{48,32},{64,48},{80,64},{96,80},{112,96},{128,112},... | collective-permute-start | bytes 98312 | tf_op jit(solution)/shard_map/ppermute | solution.py:13
  61.6 25.4 %collective-permute-start.38 = (f32[16,512]{1,0:T(8,128)S(1)}, f32[16,512]{1,0:T(8,128)S(1)}, u32[]{:S(2)}, u32[]{:S(2)}) collective-permute-start(f32[16,512]{1,0:T(8,128)S(1)} %get-tuple-element.20), channel_id=1, source_target_pairs={{0,16},{16,32},{32,48},{48,64},{64,80},{80,96},{96,112},{112,128},... | collective-permute-start | bytes 98312 | tf_op jit(solution)/shard_map/ppermute | solution.py:13
  67.2 21.1 %collective-permute-start.44 = (f32[16,512]{1,0:T(8,128)S(1)}, f32[16,512]{1,0:T(8,128)S(1)}, u32[]{:S(2)}, u32[]{:S(2)}) collective-permute-start(f32[16,512]{1,0:T(8,128)S(1)} %get-tuple-element.18), channel_id=1, source_target_pairs={{32,0},{48,16},{64,32},{80,48},{96,64},{112,80},{128,96},{144,112}... | collective-permute-start | bytes 98312 | tf_op jit(solution)/shard_map/ppermute | solution.py:13
  68.5 27.8 %collective-permute-start.41 = (f32[16,512]{1,0:T(8,128)S(1)}, f32[16,512]{1,0:T(8,128)S(1)}, u32[]{:S(2)}, u32[]{:S(2)}) collective-permute-start(f32[16,512]{1,0:T(8,128)S(1)} %get-tuple-element.18), channel_id=1, source_target_pairs={{0,32},{16,48},{32,64},{48,80},{64,96},{80,112},{96,128},{112,144}... | collective-permute-start | bytes 98312 | tf_op jit(solution)/shard_map/ppermute | solution.py:13
  79.3 16.9 %collective-permute-start.42 = (f32[16,512]{1,0:T(8,128)S(1)}, f32[16,512]{1,0:T(8,128)S(1)}, u32[]{:S(2)}, u32[]{:S(2)}) collective-permute-start(f32[16,512]{1,0:T(8,128)S(1)} %get-tuple-element.20), channel_id=1, source_target_pairs={{16,0},{32,16},{48,32},{64,48},{80,64},{96,80},{112,96},{128,112},... | collective-permute-start | bytes 98312 | tf_op jit(solution)/shard_map/ppermute | solution.py:13
  80.6 15.6 %collective-permute-start.37 = (f32[16,512]{1,0:T(8,128)S(1)}, f32[16,512]{1,0:T(8,128)S(1)}, u32[]{:S(2)}, u32[]{:S(2)}) collective-permute-start(f32[16,512]{1,0:T(8,128)S(1)} %get-tuple-element.22), channel_id=1, source_target_pairs={{0,16},{16,32},{32,48},{48,64},{64,80},{80,96},{96,112},{112,128},... | collective-permute-start | bytes 98312 | tf_op jit(solution)/shard_map/ppermute | solution.py:13
  97.5 13.9 %collective-permute-start.47 = (f32[16,512]{1,0:T(8,128)S(1)}, f32[16,512]{1,0:T(8,128)S(1)}, u32[]{:S(2)}, u32[]{:S(2)}) collective-permute-start(f32[16,512]{1,0:T(8,128)S(1)} %get-tuple-element.17), channel_id=1, source_target_pairs={{32,0},{48,16},{64,32},{80,48},{96,64},{112,80},{128,96},{144,112}... | collective-permute-start | bytes 98312 | tf_op jit(solution)/shard_map/ppermute | solution.py:13
  98.8 20.4 %collective-permute-start.46 = (f32[16,512]{1,0:T(8,128)S(1)}, f32[16,512]{1,0:T(8,128)S(1)}, u32[]{:S(2)}, u32[]{:S(2)}) collective-permute-start(f32[16,512]{1,0:T(8,128)S(1)} %get-tuple-element.15), channel_id=1, source_target_pairs={{0,32},{16,48},{32,64},{48,80},{64,96},{80,112},{96,128},{112,144}... | collective-permute-start | bytes 98312 | tf_op jit(solution)/shard_map/ppermute | solution.py:13
  106.1 14.4 %collective-permute-start.3 = (f32[32,512]{1,0:T(8,128)S(1)}, f32[32,512]{1,0:T(8,128)S(1)}, u32[]{:S(2)}, u32[]{:S(2)}) collective-permute-start(f32[32,512]{1,0:T(8,128)S(1)} %get-tuple-element.228), channel_id=1, source_target_pairs={{2,0},{4,2},{6,4},{8,6},{10,8},{12,10},{14,12},{3,1},{5,3},{7,5},{... | collective-permute-start | bytes 196616 | tf_op jit(solution)/shard_map/ppermute | solution.py:13
  108.1 18.5 %collective-permute-start.2 = (f32[32,512]{1,0:T(8,128)S(1)}, f32[32,512]{1,0:T(8,128)S(1)}, u32[]{:S(2)}, u32[]{:S(2)}) collective-permute-start(f32[32,512]{1,0:T(8,128)S(1)} %get-tuple-element.167), channel_id=1, source_target_pairs={{2,0},{4,2},{6,4},{8,6},{10,8},{12,10},{14,12},{3,1},{5,3},{7,5},{... | collective-permute-start | bytes 196616 | tf_op jit(solution)/shard_map/ppermute | solution.py:13
  110.0 17.8 %collective-permute-start.52 = (f32[16,512]{1,0:T(8,128)S(1)}, f32[16,512]{1,0:T(8,128)S(1)}, u32[]{:S(2)}, u32[]{:S(2)}) collective-permute-start(f32[16,512]{1,0:T(8,128)S(1)} %get-tuple-element.13), channel_id=1, source_target_pairs={{64,0},{80,16},{96,32},{112,48},{128,64},{144,80},{160,96},{176,11... | collective-permute-start | bytes 98312 | tf_op jit(solution)/shard_map/ppermute | solution.py:13
  111.4 21.2 %collective-permute-start.49 = (f32[16,512]{1,0:T(8,128)S(1)}, f32[16,512]{1,0:T(8,128)S(1)}, u32[]{:S(2)}, u32[]{:S(2)}) collective-permute-start(f32[16,512]{1,0:T(8,128)S(1)} %get-tuple-element.13), channel_id=1, source_target_pairs={{0,64},{16,80},{32,96},{48,112},{64,128},{80,144},{96,160},{112,17... | collective-permute-start | bytes 98312 | tf_op jit(solution)/shard_map/ppermute | solution.py:13
  119.2 15.3 %collective-permute-start.50 = (f32[16,512]{1,0:T(8,128)S(1)}, f32[16,512]{1,0:T(8,128)S(1)}, u32[]{:S(2)}, u32[]{:S(2)}) collective-permute-start(f32[16,512]{1,0:T(8,128)S(1)} %get-tuple-element.15), channel_id=1, source_target_pairs={{32,0},{48,16},{64,32},{80,48},{96,64},{112,80},{128,96},{144,112}... | collective-permute-start | bytes 98312 | tf_op jit(solution)/shard_map/ppermute | solution.py:13
  120.5 15.9 %collective-permute-start.45 = (f32[16,512]{1,0:T(8,128)S(1)}, f32[16,512]{1,0:T(8,128)S(1)}, u32[]{:S(2)}, u32[]{:S(2)}) collective-permute-start(f32[16,512]{1,0:T(8,128)S(1)} %get-tuple-element.17), channel_id=1, source_target_pairs={{0,32},{16,48},{32,64},{48,80},{64,96},{80,112},{96,128},{112,144}... | collective-permute-start | bytes 98312 | tf_op jit(solution)/shard_map/ppermute | solution.py:13
  126.6 14.8 %collective-permute-start.51 = (f32[16,512]{1,0:T(8,128)S(1)}, f32[16,512]{1,0:T(8,128)S(1)}, u32[]{:S(2)}, u32[]{:S(2)}) collective-permute-start(f32[16,512]{1,0:T(8,128)S(1)} %multiply_subtract_fusion.62), channel_id=1, source_target_pairs={{64,0},{80,16},{96,32},{112,48},{128,64},{144,80},{160,96},{176,11... | collective-permute-start | bytes 98312 | tf_op jit(solution)/shard_map/ppermute | solution.py:13
  127.9 15.4 %collective-permute-start.48 = (f32[16,512]{1,0:T(8,128)S(1)}, f32[16,512]{1,0:T(8,128)S(1)}, u32[]{:S(2)}, u32[]{:S(2)}) collective-permute-start(f32[16,512]{1,0:T(8,128)S(1)} %multiply_subtract_fusion.62), channel_id=1, source_target_pairs={{0,64},{16,80},{32,96},{48,112},{64,128},{80,144},{96,160},{112,17... | collective-permute-start | bytes 98312 | tf_op jit(solution)/shard_map/ppermute | solution.py:13
  132.5 14.8 %collective-permute-start.6 = (f32[32,512]{1,0:T(8,128)S(1)}, f32[32,512]{1,0:T(8,128)S(1)}, u32[]{:S(2)}, u32[]{:S(2)}) collective-permute-start(f32[32,512]{1,0:T(8,128)S(1)} %get-tuple-element.214), channel_id=1, source_target_pairs={{2,0},{4,2},{6,4},{8,6},{10,8},{12,10},{14,12},{3,1},{5,3},{7,5},{... | collective-permute-start | bytes 196616 | tf_op jit(solution)/shard_map/ppermute | solution.py:13
  134.5 14.1 %collective-permute-start.8 = (f32[32,512]{1,0:T(8,128)S(1)}, f32[32,512]{1,0:T(8,128)S(1)}, u32[]{:S(2)}, u32[]{:S(2)}) collective-permute-start(f32[32,512]{1,0:T(8,128)S(1)} %get-tuple-element.276), channel_id=1, source_target_pairs={{2,0},{4,2},{6,4},{8,6},{10,8},{12,10},{14,12},{3,1},{5,3},{7,5},{... | collective-permute-start | bytes 196616 | tf_op jit(solution)/shard_map/ppermute | solution.py:13
  136.4 16.8 %collective-permute-start.5 = (f32[32,512]{1,0:T(8,128)S(1)}, f32[32,512]{1,0:T(8,128)S(1)}, u32[]{:S(2)}, u32[]{:S(2)}) collective-permute-start(f32[32,512]{1,0:T(8,128)S(1)} %get-tuple-element.276), channel_id=1, source_target_pairs={{0,2},{2,4},{4,6},{6,8},{8,10},{10,12},{12,14},{1,3},{3,5},{5,7},{... | collective-permute-start | bytes 196616 | tf_op jit(solution)/shard_map/ppermute | solution.py:13
  143.3 15.7 %collective-permute-start.4 = (f32[32,512]{1,0:T(8,128)S(1)}, f32[32,512]{1,0:T(8,128)S(1)}, u32[]{:S(2)}, u32[]{:S(2)}) collective-permute-start(f32[32,512]{1,0:T(8,128)S(1)} %get-tuple-element.275), channel_id=1, source_target_pairs={{0,2},{2,4},{4,6},{6,8},{8,10},{10,12},{12,14},{1,3},{3,5},{5,7},{... | collective-permute-start | bytes 196616 | tf_op jit(solution)/shard_map/ppermute | solution.py:13
  147.3 13.1 %collective-permute-start.58 = (f32[16,512]{1,0:T(8,128)S(1)}, f32[16,512]{1,0:T(8,128)S(1)}, u32[]{:S(2)}, u32[]{:S(2)}) collective-permute-start(f32[16,512]{1,0:T(8,128)S(1)} %get-tuple-element.10), channel_id=1, source_target_pairs={{64,0},{80,16},{96,32},{112,48},{128,64},{144,80},{160,96},{176,11... | collective-permute-start | bytes 98312 | tf_op jit(solution)/shard_map/ppermute | solution.py:13
  148.6 19.6 %collective-permute-start.54 = (f32[16,512]{1,0:T(8,128)S(1)}, f32[16,512]{1,0:T(8,128)S(1)}, u32[]{:S(2)}, u32[]{:S(2)}) collective-permute-start(f32[16,512]{1,0:T(8,128)S(1)} %get-tuple-element.10), channel_id=1, source_target_pairs={{0,64},{16,80},{32,96},{48,112},{64,128},{80,144},{96,160},{112,17... | collective-permute-start | bytes 98312 | tf_op jit(solution)/shard_map/ppermute | solution.py:13
  154.5 15.0 %collective-permute-start.53 = (f32[16,512]{1,0:T(8,128)S(1)}, f32[16,512]{1,0:T(8,128)S(1)}, u32[]{:S(2)}, u32[]{:S(2)}) collective-permute-start(f32[16,512]{1,0:T(8,128)S(1)} %get-tuple-element.12), channel_id=1, source_target_pairs={{0,64},{16,80},{32,96},{48,112},{64,128},{80,144},{96,160},{112,17... | collective-permute-start | bytes 98312 | tf_op jit(solution)/shard_map/ppermute | solution.py:13
  159.1 16.4 %collective-permute-start.16 = (f32[32,512]{1,0:T(8,128)S(1)}, f32[32,512]{1,0:T(8,128)S(1)}, u32[]{:S(2)}, u32[]{:S(2)}) collective-permute-start(f32[32,512]{1,0:T(8,128)S(1)} %get-tuple-element.162), channel_id=1, source_target_pairs={{4,0},{6,2},{8,4},{10,6},{12,8},{14,10},{5,1},{7,3},{9,5},{11,7},{... | collective-permute-start | bytes 196616 | tf_op jit(solution)/shard_map/ppermute | solution.py:13
  160.4 16.4 %collective-permute-start.11 = (f32[32,512]{1,0:T(8,128)S(1)}, f32[32,512]{1,0:T(8,128)S(1)}, u32[]{:S(2)}, u32[]{:S(2)}) collective-permute-start(f32[32,512]{1,0:T(8,128)S(1)} %get-tuple-element.166), channel_id=1, source_target_pairs={{2,0},{4,2},{6,4},{8,6},{10,8},{12,10},{14,12},{3,1},{5,3},{7,5},{... | collective-permute-start | bytes 196616 | tf_op jit(solution)/shard_map/ppermute | solution.py:13
  162.4 20.6 %collective-permute-start.10 = (f32[32,512]{1,0:T(8,128)S(1)}, f32[32,512]{1,0:T(8,128)S(1)}, u32[]{:S(2)}, u32[]{:S(2)}) collective-permute-start(f32[32,512]{1,0:T(8,128)S(1)} %get-tuple-element.164), channel_id=1, source_target_pairs={{0,2},{2,4},{4,6},{6,8},{8,10},{10,12},{12,14},{1,3},{3,5},{5,7},{... | collective-permute-start | bytes 196616 | tf_op jit(solution)/shard_map/ppermute | solution.py:13
  168.2 16.1 %collective-permute-start.60 = (f32[16,512]{1,0:T(8,128)S(1)}, f32[16,512]{1,0:T(8,128)S(1)}, u32[]{:S(2)}, u32[]{:S(2)}) collective-permute-start(f32[16,512]{1,0:T(8,128)S(1)} %get-tuple-element.8), channel_id=1, source_target_pairs={{128,0},{144,16},{160,32},{176,48},{192,64},{208,80},{224,96},{240... | collective-permute-start | bytes 98312 | tf_op jit(solution)/shard_map/ppermute | solution.py:13
  169.5 20.9 %collective-permute-start.57 = (f32[16,512]{1,0:T(8,128)S(1)}, f32[16,512]{1,0:T(8,128)S(1)}, u32[]{:S(2)}, u32[]{:S(2)}) collective-permute-start(f32[16,512]{1,0:T(8,128)S(1)} %get-tuple-element.8), channel_id=1, source_target_pairs={{0,128},{16,144},{32,160},{48,176},{64,192},{80,208},{96,224},{112... | collective-permute-start | bytes 98312 | tf_op jit(solution)/shard_map/ppermute | solution.py:13
  175.6 28.5 %collective-permute-start.59 = (f32[16,512]{1,0:T(8,128)S(1)}, f32[16,512]{1,0:T(8,128)S(1)}, u32[]{:S(2)}, u32[]{:S(2)}) collective-permute-start(f32[16,512]{1,0:T(8,128)S(1)} %get-tuple-element.281), channel_id=1, source_target_pairs={{128,0},{144,16},{160,32},{176,48},{192,64},{208,80},{224,96},{240... | collective-permute-start | bytes 98312 | tf_op jit(solution)/shard_map/ppermute | solution.py:13
  176.9 28.5 %collective-permute-start.56 = (f32[16,512]{1,0:T(8,128)S(1)}, f32[16,512]{1,0:T(8,128)S(1)}, u32[]{:S(2)}, u32[]{:S(2)}) collective-permute-start(f32[16,512]{1,0:T(8,128)S(1)} %get-tuple-element.281), channel_id=1, source_target_pairs={{0,128},{16,144},{32,160},{48,176},{64,192},{80,208},{96,224},{112... | collective-permute-start | bytes 98312 | tf_op jit(solution)/shard_map/ppermute | solution.py:13
  182.9 15.2 %collective-permute-start.62 = (f32[16,512]{1,0:T(8,128)S(1)}, f32[16,512]{1,0:T(8,128)S(1)}, u32[]{:S(2)}, u32[]{:S(2)}) collective-permute-start(f32[16,512]{1,0:T(8,128)S(1)} %get-tuple-element.282), channel_id=1, source_target_pairs={{128,0},{144,16},{160,32},{176,48},{192,64},{208,80},{224,96},{240... | collective-permute-start | bytes 98312 | tf_op jit(solution)/shard_map/ppermute | solution.py:13
  184.3 15.8 %collective-permute-start.61 = (f32[16,512]{1,0:T(8,128)S(1)}, f32[16,512]{1,0:T(8,128)S(1)}, u32[]{:S(2)}, u32[]{:S(2)}) collective-permute-start(f32[16,512]{1,0:T(8,128)S(1)} %get-tuple-element.280), channel_id=1, source_target_pairs={{0,128},{16,144},{32,160},{48,176},{64,192},{80,208},{96,224},{112... | collective-permute-start | bytes 98312 | tf_op jit(solution)/shard_map/ppermute | solution.py:13
  190.4 21.9 %collective-permute-start.13 = (f32[32,512]{1,0:T(8,128)S(1)}, f32[32,512]{1,0:T(8,128)S(1)}, u32[]{:S(2)}, u32[]{:S(2)}) collective-permute-start(f32[32,512]{1,0:T(8,128)S(1)} %get-tuple-element.162), channel_id=1, source_target_pairs={{0,4},{2,6},{4,8},{6,10},{8,12},{10,14},{1,5},{3,7},{5,9},{7,11},{... | collective-permute-start | bytes 196616 | tf_op jit(solution)/shard_map/ppermute | solution.py:13
  198.2 19.5 %collective-permute-start.14 = (f32[32,512]{1,0:T(8,128)S(1)}, f32[32,512]{1,0:T(8,128)S(1)}, u32[]{:S(2)}, u32[]{:S(2)}) collective-permute-start(f32[32,512]{1,0:T(8,128)S(1)} %get-tuple-element.164), channel_id=1, source_target_pairs={{2,0},{4,2},{6,4},{8,6},{10,8},{12,10},{14,12},{3,1},{5,3},{7,5},{... | collective-permute-start | bytes 196616 | tf_op jit(solution)/shard_map/ppermute | solution.py:13
  200.1 17.6 %collective-permute-start.9 = (f32[32,512]{1,0:T(8,128)S(1)}, f32[32,512]{1,0:T(8,128)S(1)}, u32[]{:S(2)}, u32[]{:S(2)}) collective-permute-start(f32[32,512]{1,0:T(8,128)S(1)} %get-tuple-element.166), channel_id=1, source_target_pairs={{0,2},{2,4},{4,6},{6,8},{8,10},{10,12},{12,14},{1,3},{3,5},{5,7},{... | collective-permute-start | bytes 196616 | tf_op jit(solution)/shard_map/ppermute | solution.py:13
  204.0 13.7 %collective-permute-start.15 = (f32[32,512]{1,0:T(8,128)S(1)}, f32[32,512]{1,0:T(8,128)S(1)}, u32[]{:S(2)}, u32[]{:S(2)}) collective-permute-start(f32[32,512]{1,0:T(8,128)S(1)} %multiply_subtract_fusion.2), channel_id=1, source_target_pairs={{4,0},{6,2},{8,4},{10,6},{12,8},{14,10},{5,1},{7,3},{9,5},{11,7},{... | collective-permute-start | bytes 196616 | tf_op jit(solution)/shard_map/ppermute | solution.py:13
  212.3 21.5 %collective-permute-start.63 = (f32[16,512]{1,0:T(8,128)S(1)}, f32[16,512]{1,0:T(8,128)S(1)}, u32[]{:S(2)}, u32[]{:S(2)}) collective-permute-start(f32[16,512]{1,0:T(8,128)S(1)} %subtract_divide_fusion.2), channel_id=1, source_target_pairs={{0,16},{16,32},{32,48},{48,64},{64,80},{80,96},{96,112},{112,128},... | collective-permute-start | bytes 98312 | tf_op jit(solution)/shard_map/ppermute | solution.py:13
  217.8 18.1 %collective-permute-start.22 = (f32[32,512]{1,0:T(8,128)S(1)}, f32[32,512]{1,0:T(8,128)S(1)}, u32[]{:S(2)}, u32[]{:S(2)}) collective-permute-start(f32[32,512]{1,0:T(8,128)S(1)} %get-tuple-element.159), channel_id=1, source_target_pairs={{4,0},{6,2},{8,4},{10,6},{12,8},{14,10},{5,1},{7,3},{9,5},{11,7},{... | collective-permute-start | bytes 196616 | tf_op jit(solution)/shard_map/ppermute | solution.py:13
  219.1 25.3 %collective-permute-start.18 = (f32[32,512]{1,0:T(8,128)S(1)}, f32[32,512]{1,0:T(8,128)S(1)}, u32[]{:S(2)}, u32[]{:S(2)}) collective-permute-start(f32[32,512]{1,0:T(8,128)S(1)} %get-tuple-element.159), channel_id=1, source_target_pairs={{0,4},{2,6},{4,8},{6,10},{8,12},{10,14},{1,5},{3,7},{5,9},{7,11},{... | collective-permute-start | bytes 196616 | tf_op jit(solution)/shard_map/ppermute | solution.py:13
  225.8 18.6 %collective-permute-start.19 = (f32[32,512]{1,0:T(8,128)S(1)}, f32[32,512]{1,0:T(8,128)S(1)}, u32[]{:S(2)}, u32[]{:S(2)}) collective-permute-start(f32[32,512]{1,0:T(8,128)S(1)} %get-tuple-element.161), channel_id=1, source_target_pairs={{4,0},{6,2},{8,4},{10,6},{12,8},{14,10},{5,1},{7,3},{9,5},{11,7},{... | collective-permute-start | bytes 196616 | tf_op jit(solution)/shard_map/ppermute | solution.py:13
  227.1 17.3 %collective-permute-start.17 = (f32[32,512]{1,0:T(8,128)S(1)}, f32[32,512]{1,0:T(8,128)S(1)}, u32[]{:S(2)}, u32[]{:S(2)}) collective-permute-start(f32[32,512]{1,0:T(8,128)S(1)} %get-tuple-element.161), channel_id=1, source_target_pairs={{0,4},{2,6},{4,8},{6,10},{8,12},{10,14},{1,5},{3,7},{5,9},{7,11},{... | collective-permute-start | bytes 196616 | tf_op jit(solution)/shard_map/ppermute | solution.py:13
  233.7 21.8 %collective-permute-start.24 = (f32[32,512]{1,0:T(8,128)S(1)}, f32[32,512]{1,0:T(8,128)S(1)}, u32[]{:S(2)}, u32[]{:S(2)}) collective-permute-start(f32[32,512]{1,0:T(8,128)S(1)} %get-tuple-element.157), channel_id=1, source_target_pairs={{8,0},{10,2},{12,4},{14,6},{9,1},{11,3},{13,5},{15,7},{24,16},{26,... | collective-permute-start | bytes 196616 | tf_op jit(solution)/shard_map/ppermute | solution.py:13
  235.9 28.1 %collective-permute-start.21 = (f32[32,512]{1,0:T(8,128)S(1)}, f32[32,512]{1,0:T(8,128)S(1)}, u32[]{:S(2)}, u32[]{:S(2)}) collective-permute-start(f32[32,512]{1,0:T(8,128)S(1)} %get-tuple-element.157), channel_id=1, source_target_pairs={{0,8},{2,10},{4,12},{6,14},{1,9},{3,11},{5,13},{7,15},{16,24},{18,... | collective-permute-start | bytes 196616 | tf_op jit(solution)/shard_map/ppermute | solution.py:13
  244.4 21.4 %collective-permute-start.23 = (f32[32,512]{1,0:T(8,128)S(1)}, f32[32,512]{1,0:T(8,128)S(1)}, u32[]{:S(2)}, u32[]{:S(2)}) collective-permute-start(f32[32,512]{1,0:T(8,128)S(1)} %get-tuple-element.278), channel_id=1, source_target_pairs={{8,0},{10,2},{12,4},{14,6},{9,1},{11,3},{13,5},{15,7},{24,16},{26,... | collective-permute-start | bytes 196616 | tf_op jit(solution)/shard_map/ppermute | solution.py:13
  245.7 20.1 %collective-permute-start.20 = (f32[32,512]{1,0:T(8,128)S(1)}, f32[32,512]{1,0:T(8,128)S(1)}, u32[]{:S(2)}, u32[]{:S(2)}) collective-permute-start(f32[32,512]{1,0:T(8,128)S(1)} %get-tuple-element.278), channel_id=1, source_target_pairs={{0,8},{2,10},{4,12},{6,14},{1,9},{3,11},{5,13},{7,15},{16,24},{18,... | collective-permute-start | bytes 196616 | tf_op jit(solution)/shard_map/ppermute | solution.py:13
  (23 other events, 173.0 us)
where the time goes:
time: 280 us; the launch traced here: 274 us
  starting transfers between devices  231 us (82%)
  other arithmetic  21.2 us (8%)
  waiting for transfers between devices  10.4 us (4%)
  local copies, waits for them, and re-layouts  10.2 us (4%)
    ppermute x64, starting transfers between devices, shifted(): return lax.ppermute(x, axis, pairs)  231 us
    add x1, other arithmetic, per_device(): electric_z + curl_factor * (lower_diff(magnetic_y, rim_along_x, 0) - lowe...  12.8 us
    ppermute x64, waiting for transfers between devices, shifted(): return lax.ppermute(x, axis, pairs)  10.4 us
  transfers between devices with their start and end apart: 64, of which 7 were waited for; matrix products, arithmetic and copies ran while one was open for 8% of the time, Pallas kernels for 0%

commit v1 on v0

v1 whole, which is shorter than its diff:
```python
import functools

import jax
import jax.numpy as jnp
from jax import lax
from jax.experimental import pallas as pl
from jax.experimental.pallas import tpu as pltpu
from jax.sharding import PartitionSpec as P

ground_scale = 1.0 / 1600.0
drive_scale = 1.0 / 40.0
lane = 128
rows = 8
f32 = jnp.float32


def inverse(x):
    guess = pl.reciprocal(x, approx=True)
    return guess * (2.0 - x * guess)


def table_lookup(table, index):
    return jnp.take_along_axis(
        jnp.broadcast_to(table, index.shape), index, axis=1, mode="promise_in_bounds"
    )


def eliminate(state, ground, drive):
    link, left, here, left_drive, here_drive = state
    t = inverse(link + here + 1.0)
    next_link = link * t
    return (
        next_link,
        left + next_link * here,
        ground + here * t,
        left_drive + next_link * here_drive,
        drive + here_drive * t,
    ), t


def close_block(state, rim):
    link, left, here, left_drive, here_drive = state
    return (
        link,
        left,
        here,
        left_drive + link * rim,
        here_drive - (link + here + 1.0) * rim,
    )


def y_forward_kernel(
    table_ref, material_ref, ex_ref, my_ref, mz_ref, edge_ref,
    t_ref, drive_ref, rim_ref, reduced_ref, ground_s, drive_s, mz_s,
):
    xs, ys, zs = material_ref.shape
    tiles = zs // lane
    table = table_ref[...] * ground_scale
    lanes = lax.broadcasted_iota(jnp.int32, (xs * ys, lane), 1)
    before = pltpu.roll(edge_ref[...].reshape(xs * ys, lane), 1, 1)
    for k in range(tiles):
        cut = pl.ds(k * lane, lane)
        ground = table_lookup(table, material_ref[:, :, cut].reshape(xs * ys, lane))
        my = my_ref[:, :, cut].reshape(xs * ys, lane)
        rolled = pltpu.roll(my, 1, 1)
        lower = jnp.where(lanes == 0, before, rolled)
        before = rolled
        ground_s[k] = ground
        drive_s[k] = ground * ex_ref[:, :, cut].reshape(xs * ys, lane) - drive_scale * (my - lower)
        mz_s[k] = mz_ref[:, :, cut].reshape(xs * ys, lane)
    for k in range(tiles):
        cut = pl.ds(k * lane, lane)
        state = None
        last_mz = None
        for j in range(ys):
            pick = pl.ds(j, xs, stride=ys)
            ground = ground_s[k, pick, :]
            mz = drive_scale * mz_s[k, pick, :]
            drive = drive_s[k, pick, :] + mz
            if j == 0:
                state = (jnp.ones_like(ground), jnp.zeros_like(ground), ground, jnp.zeros_like(ground), drive)
            else:
                state, t = eliminate(state, ground, drive - last_mz)
                t_ref[j - 1, :, cut] = t
            drive_ref[j, :, cut] = state[4]
            last_mz = mz
        rim_ref[:, cut] = last_mz
        for v, value in enumerate(close_block(state, last_mz)):
            reduced_ref[k // 2, v, pl.ds((k % 2) * rows, rows), :] = value


def y_reduced_kernel(blocks_ref, ends_ref):
    count = blocks_ref.shape[0]
    block = [[blocks_ref[b, v] for v in range(5)] for b in range(count)]
    here = block[0][2] + block[0][0]
    drive = block[0][4]
    kept = []
    for b in range(1, count):
        link, left, right, left_drive, right_drive = block[b]
        total = here + left
        t = inverse(total + link)
        pull = link * t
        push = drive + left_drive
        kept.append((pull, push * t))
        here = right + pull * total
        drive = right_drive + pull * push
    value = drive * inverse(here + 1.0)
    ends_ref[count - 1, 1] = value
    for b in range(count - 1, 0, -1):
        pull, push = kept[b - 1]
        value = push + pull * value
        ends_ref[b, 0] = value
        ends_ref[b - 1, 1] = value
    ends_ref[0, 0] = jnp.zeros_like(value)


def y_back_kernel(t_ref, drive_ref, rim_ref, ends_ref, out_ref, out_s):
    ys, xs, zs = t_ref.shape
    for k in range(zs // lane):
        cut = pl.ds(k * lane, lane)
        half = pl.ds((k % 2) * rows, rows)
        before = ends_ref[k // 2, 0, half, :]
        value = ends_ref[k // 2, 1, half, :] + rim_ref[:, cut]
        reach = before
        parts = []
        for j in range(ys - 1):
            t = t_ref[j, :, cut]
            reach_t = reach * t
            parts.append((t, drive_ref[j, :, cut] * t + reach_t))
            reach = reach_t
        out_s[pl.ds(ys - 1, xs, stride=ys), :] = value
        for j in range(ys - 2, -1, -1):
            t, part = parts[j]
            value = part + t * value
            out_s[pl.ds(j, xs, stride=ys), :] = value
        out_ref[:, :, cut] = out_s[...].reshape(xs, ys, lane)


def x_forward_kernel(
    table_ref, material_ref, ez_ref, mx_ref, my_ref, edge_ref,
    t_ref, drive_ref, rim_ref, reduced_ref, state_s, last_my_s,
):
    xs, ys, zs = material_ref.shape
    step = pl.program_id(0)
    table = table_ref[...] * ground_scale
    row = lax.broadcasted_iota(jnp.int32, (ys, zs), 0)

    @pl.when(step == 0)
    def _():
        state_s[0] = jnp.zeros((ys, zs), f32)
        state_s[1] = jnp.zeros((ys, zs), f32)
        state_s[2] = jnp.zeros((ys, zs), f32)
        state_s[3] = jnp.zeros((ys, zs), f32)
        state_s[4] = jnp.zeros((ys, zs), f32)
        last_my_s[...] = jnp.zeros((ys, zs), f32)

    state = tuple(state_s[v] for v in range(5))
    last_my = last_my_s[...]
    for i in range(xs):
        index = material_ref[i]
        ground = jnp.concatenate(
            [table_lookup(table, index[:, k * lane:(k + 1) * lane]) for k in range(zs // lane)], axis=1
        )
        mx = mx_ref[i]
        lower_mx = jnp.where(row == 0, edge_ref[pl.ds(i, 1), :], pltpu.roll(mx, 1, 0))
        my = my_ref[i]
        drive = ground * ez_ref[i] + drive_scale * ((my - last_my) - (mx - lower_mx))
        last_my = my
        state, t = eliminate(state, ground, drive)
        if i == 0:
            first = step == 0
            link, left, here, left_drive, here_drive = state
            state = (jnp.where(first, 1.0, link), left, here, left_drive, here_drive)
        t_ref[i] = t
        drive_ref[i] = state[4]
    for v in range(5):
        state_s[v] = state[v]
    last_my_s[...] = last_my

    @pl.when(step == pl.num_programs(0) - 1)
    def _():
        rim = drive_scale * last_my
        rim_ref[...] = rim
        for v, value in enumerate(close_block(state, rim)):
            reduced_ref[v] = value


def x_back_kernel(t_ref, drive_ref, rim_ref, before_ref, here_ref, out_ref):
    xs = t_ref.shape[0]
    reach = before_ref[...]
    for i in range(xs - 1):
        t = t_ref[i + 1]
        reach = reach * t
        out_ref[i] = drive_ref[i] * t + reach
    value = here_ref[...] + rim_ref[...]
    out_ref[xs - 1] = value
    for i in range(xs - 2, -1, -1):
        value = out_ref[i] + t_ref[i + 1] * value
        out_ref[i] = value


def cost(elements, ops, arrays):
    return pl.CostEstimate(flops=elements * ops, bytes_accessed=elements * 4 * arrays, transcendentals=0)


def merge(a, b):
    total = a[2] + b[1]
    t = 1.0 / (total + a[0] + b[0])
    a_link, b_link = a[0] * t, b[0] * t
    push = a[4] + b[3]
    merged = jnp.stack(
        [
            a[0] * b_link,
            a[1] + a_link * total,
            b[2] + b_link * total,
            a[3] + a_link * push,
            b[4] + b_link * push,
        ]
    )
    return merged, (t * push, a_link, b_link)


def solve_along_x(own, axis):
    count = lax.axis_size(axis)
    place = lax.axis_index(axis)
    levels = []
    bit = 1
    while bit < count:
        mask = 3 * (bit // 2) if bit in (2, 8) else bit
        other = lax.ppermute(own, axis, [(i, i ^ mask) for i in range(count)])
        low = (place & bit) == 0
        own, solved = merge(jnp.where(low, own, other), jnp.where(low, other, own))
        levels.append((low, solved))
        bit *= 2
    before = jnp.zeros_like(own[0])
    here = own[4] / (own[2] + own[0] + 1.0)
    for low, (push, from_low, from_high) in reversed(levels):
        middle = push + from_low * before + from_high * here
        before, here = jnp.where(low, before, middle), jnp.where(low, middle, here)
    return before, here


def shift_up(x, axis):
    return lax.ppermute(x, axis, [(i, i + 1) for i in range(lax.axis_size(axis) - 1)])


def per_device(electric_x, electric_z, magnetic_x, magnetic_y, magnetic_z, material, perm_table):
    xs, ys, zs = material.shape
    chunks = xs // rows
    cells = xs * ys * zs
    sds = jax.ShapeDtypeStruct
    table = jnp.pad(perm_table, (0, lane - perm_table.shape[0])).reshape(1, lane)

    edge_z = shift_up(magnetic_y[:, :, zs - lane:], "gz")
    edge_y = shift_up(magnetic_x[:, ys - 1], "gy")

    slab = pl.BlockSpec((rows, ys, zs), lambda c: (c, 0, 0))
    turned = pl.BlockSpec((ys, rows, zs), lambda c: (0, c, 0))
    whole_table = pl.BlockSpec((1, lane), lambda c: (0, 0))
    vmem = pltpu.CompilerParams(vmem_limit_bytes=40 * 2**20)

    y_t, y_drive, y_rim, y_reduced = pl.pallas_call(
        y_forward_kernel,
        grid=(chunks,),
        in_specs=[whole_table, slab, slab, slab, slab, pl.BlockSpec((rows, ys, lane), lambda c: (c, 0, 0))],
        out_specs=[
            turned,
            turned,
            pl.BlockSpec((rows, zs), lambda c: (c, 0)),
            pl.BlockSpec((2, 5, 2 * rows, lane), lambda c: (c, 0, 0, 0)),
        ],
        out_shape=[
            sds((ys, xs, zs), f32),
            sds((ys, xs, zs), f32),
            sds((xs, zs), f32),
            sds((2 * chunks, 5, 2 * rows, lane), f32),
        ],
        scratch_shapes=[pltpu.VMEM((zs // lane, rows * ys, lane), f32)] * 3,
        compiler_params=vmem,
        cost_estimate=cost(cells, 30, 6),
        name="y_forward",
    )(table, material, electric_x, magnetic_y, magnetic_z, edge_z)

    y_blocks = lax.all_to_all(y_reduced, "gy", 0, 0, tiled=True)

    x_t, x_drive, x_rim, x_reduced = pl.pallas_call(
        x_forward_kernel,
        grid=(chunks,),
        in_specs=[whole_table, slab, slab, slab, slab, pl.BlockSpec((rows, zs), lambda c: (c, 0))],
        out_specs=[
            slab,
            slab,
            pl.BlockSpec((ys, zs), lambda c: (0, 0)),
            pl.BlockSpec((5, ys, zs), lambda c: (0, 0, 0)),
        ],
        out_shape=[
            sds((xs, ys, zs), f32),
            sds((xs, ys, zs), f32),
            sds((ys, zs), f32),
            sds((5, ys, zs), f32),
        ],
        scratch_shapes=[pltpu.VMEM((5, ys, zs), f32), pltpu.VMEM((ys, zs), f32)],
        compiler_params=vmem,
        cost_estimate=cost(cells, 30, 6),
        name="x_forward",
    )(table, material, electric_z, magnetic_x, magnetic_y, edge_y)

    x_before, x_here = solve_along_x(x_reduced, "gx")

    y_ends = pl.pallas_call(
        y_reduced_kernel,
        out_shape=sds((2 * chunks, 2, 2 * rows, lane), f32),
        compiler_params=vmem,
        cost_estimate=cost(y_blocks.size // 5, 20, 7),
        name="y_reduced",
    )(y_blocks)
    y_ends = lax.all_to_all(y_ends, "gy", 0, 0, tiled=True)

    electric_z_half = pl.pallas_call(
        x_back_kernel,
        out_shape=sds((xs, ys, zs), f32),
        compiler_params=vmem,
        cost_estimate=cost(cells, 5, 3),
        name="x_back",
    )(x_t, x_drive, x_rim, x_before, x_here)

    electric_x_half = pl.pallas_call(
        y_back_kernel,
        grid=(chunks,),
        in_specs=[
            turned,
            turned,
            pl.BlockSpec((rows, zs), lambda c: (c, 0)),
            pl.BlockSpec((2, 2, 2 * rows, lane), lambda c: (c, 0, 0, 0)),
        ],
        out_specs=slab,
        out_shape=sds((xs, ys, zs), f32),
        scratch_shapes=[pltpu.VMEM((rows * ys, lane), f32)],
        compiler_params=vmem,
        cost_estimate=cost(cells, 5, 3),
        name="y_back",
    )(y_t, y_drive, y_rim, y_ends)
    return (electric_x_half, electric_z_half)


def solution(mesh):
    field = P("gx", "gy", "gz")
    return jax.shard_map(
        per_device,
        mesh=mesh,
        in_specs=(field,) * 6 + (P(),),
        out_specs=(field, field),
        check_vma=False,
    )
```

time: 280 us -> 90 us (0.32)
  the two profiles are of different devices: /device:TPU:32 before, /device:TPU:6 now
where the time goes in v1:
time: 90 us; the launch traced here: 89.2 us
  waiting for transfers between devices  29.6 us (33%)
  starting transfers between devices  24.6 us (27%)
  local copies, waits for them, and re-layouts  15.2 us (17%)
  other arithmetic  10.6 us (12%)
  Pallas kernels  8.27 us (9%)
  between operations  0.97 us (1%)
    unnamed x59, local copies, waits for them, and re-layouts  13.3 us
    ppermute x4, waiting for transfers between devices, solve_along_x(): other = lax.ppermute(own, axis, [(i, i ^ mask) for i in range(count)])  12.6 us
    all_to_all x1, starting transfers between devices, per_device(): y_blocks = lax.all_to_all(y_reduced, 'gy', 0, 0, tiled=True)  10.1 us
    all_to_all x1, waiting for transfers between devices, per_device(): y_blocks = lax.all_to_all(y_reduced, 'gy', 0, 0, tiled=True)  9.07 us
    all_to_all x1, waiting for transfers between devices, per_device(): y_ends = lax.all_to_all(y_ends, 'gy', 0, 0, tiled=True)  6.1 us
    ppermute x4, starting transfers between devices, solve_along_x(): other = lax.ppermute(own, axis, [(i, i ^ mask) for i in range(count)])  5.98 us
    unnamed x12, other arithmetic  5.24 us
    ppermute x2, starting transfers between devices, shift_up(): lax.ppermute(x, axis, [(i, i + 1) for i in range(lax.axis_size(axis) - 1)])  5.12 us
  transfers between devices with their start and end apart: 8, of which 6 were waited for; matrix products, arithmetic and copies ran while one was open for 9% of the time, Pallas kernels for 5%

profile of v1, /device:TPU:6, one launch (start us, length us, event | category | flops | bytes accessed | tf_op | source)
XLA Modules:
  0.0 89.2 jit_solution(8687278372489166559)
XLA Ops:
  0.6 1.1 %slice.133 = f32[32,1,512]{2,1,0:T(1,128)S(1)} slice(f32[32,16,512]{2,1,0:T(8,128)} %mx_ref.1), slice={[0:32], [15:16], [0:512]} | slice | bytes 131072 | tf_op jit(solution)/shard_map/slice | solution.py:255
  1.8 3.8 %collective-permute-start.1 = (f32[32,512]{1,0:T(8,128)S(1)}, f32[32,512]{1,0:T(8,128)S(1)}, u32[]{:S(2)}, u32[]{:S(2)}) collective-permute-start(f32[32,512]{1,0:T(8,128)S(1)} %bitcast.159), channel_id=1, source_target_pairs={{0,2},{2,4},{4,6},{6,8},{8,10},{10,12},{12,14},{1,3},{3,5},{5,7},{... | collective-permute-start | bytes 196616 | tf_op jit(solution)/shard_map/ppermute | solution.py:244
  5.6 1.9 %collective-permute-done.1.edge_ref = f32[32,512]{1,0:T(8,128)S(1)} collective-permute-done((f32[32,512]{1,0:T(8,128)S(1)}, f32[32,512]{1,0:T(8,128)S(1)}, u32[]{:S(2)}, u32[]{:S(2)}) %collective-permute-start.1) | collective-permute-done | bytes 65568 | tf_op jit(solution)/shard_map/ppermute | solution.py:244
  7.5 1.2 %copy-done = f32[32,16,512]{2,1,0:T(8,128)S(1)} copy-done((f32[32,16,512]{2,1,0:T(8,128)S(1)}, f32[32,16,512]{2,1,0:T(8,128)}, u32[]{:S(2)}) %copy-start) | copy-done | bytes 1048600
  8.7 1.2 %copy-done.2 = s32[32,16,512]{2,1,0:T(8,128)S(1)} copy-done((s32[32,16,512]{2,1,0:T(8,128)S(1)}, s32[32,16,512]{2,1,0:T(8,128)}, u32[]{:S(2)}) %copy-start.2) | copy-done | bytes 1048600
  9.9 1.2 %copy-done.4 = f32[32,16,512]{2,1,0:T(8,128)S(1)} copy-done((f32[32,16,512]{2,1,0:T(8,128)S(1)}, f32[32,16,512]{2,1,0:T(8,128)}, u32[]{:S(2)}) %copy-start.4) | copy-done | bytes 1048600
  11.2 1.2 %copy-done.5 = f32[32,16,512]{2,1,0:T(8,128)S(1)} copy-done((f32[32,16,512]{2,1,0:T(8,128)S(1)}, f32[32,16,512]{2,1,0:T(8,128)}, u32[]{:S(2)}) %copy-start.5) | copy-done | bytes 1048600
  12.4 1.2 %x_forward.1 = (f32[32,16,512]{2,1,0:T(8,128)S(1)}, f32[32,16,512]{2,1,0:T(8,128)S(1)}, f32[16,512]{1,0:T(8,128)S(1)}, f32[5,16,512]{2,1,0:T(8,128)S(1)}) custom-call(f32[1,128]{1,0:T(1,128)S(1)} %pad_bitcast_fusion.table_ref, s32[32,16,512]{2,1,0:T(8,128)S(1)} %copy-done.2, f32[32,16,512]{2,1,0:T(8,128)S(1)} %copy-done.5, f32[32,16,512]{2,1,0:T(8,128)S(1)} %copy-done.4, ...), custom_call_target="tpu_custom_call" | custom-call | flops 7864320 | bytes 6291456 | tf_op jit(solution)/shard_map/x_forward/pallas_call | solution.py:286
  13.6 1.0 %copy-done.8 = f32[32,16,512]{2,1,0:T(8,128)} copy-done((f32[32,16,512]{2,1,0:T(8,128)}, f32[32,16,512]{2,1,0:T(8,128)S(1)}, u32[]{:S(2)}) %copy-start.8) | copy-done | bytes 1048600
  14.5 1.0 %copy-done.10 = f32[32,16,512]{2,1,0:T(8,128)} copy-done((f32[32,16,512]{2,1,0:T(8,128)}, f32[32,16,512]{2,1,0:T(8,128)S(1)}, u32[]{:S(2)}) %copy-start.10) | copy-done | bytes 1048600
  15.5 0.6 copy-done.16
  16.1 0.8 collective-permute-start.2
  17.0 4.5 %collective-permute-done.2 = f32[5,16,512]{2,1,0:T(8,128)S(1)} collective-permute-done((f32[5,16,512]{2,1,0:T(8,128)S(1)}, f32[5,16,512]{2,1,0:T(8,128)S(1)}, u32[]{:S(2)}, u32[]{:S(2)}) %collective-permute-start.2) | collective-permute-done | bytes 163872 | tf_op jit(solution)/shard_map/ppermute | solution.py:230
  21.6 0.7 copy-done.24
  22.3 0.6 collective-permute-start.3
  22.9 6.1 %collective-permute-done.3 = f32[5,16,512]{2,1,0:T(8,128)S(1)} collective-permute-done((f32[5,16,512]{2,1,0:T(8,128)S(1)}, f32[5,16,512]{2,1,0:T(8,128)S(1)}, u32[]{:S(2)}, u32[]{:S(2)}) %collective-permute-start.3) | collective-permute-done | bytes 163872 | tf_op jit(solution)/shard_map/ppermute | solution.py:230
  29.0 0.7 constant_dynamic-update-slice_fusion.1
  29.7 0.6 fusion.14
  30.3 0.6 fusion.13
  31.0 0.6 fusion.12
  31.6 0.6 fusion.11
  32.2 1.6 %collective-permute-start.4 = (f32[5,16,512]{2,1,0:T(8,128)}, f32[5,16,512]{2,1,0:T(8,128)}, u32[]{:S(2)}, u32[]{:S(2)}) collective-permute-start(f32[5,16,512]{2,1,0:T(8,128)} %fusion.11), channel_id=1, source_target_pairs={{0,64},{16,80},{32,96},{48,112},{64,0},{80,16},{96,32},{112,48},{1... | collective-permute-start | bytes 491528 | tf_op jit(solution)/shard_map/ppermute | solution.py:230
  33.8 0.7 slice.132
  34.5 1.3 %collective-permute-start = (f32[32,16,128]{2,1,0:T(8,128)}, f32[32,16,128]{2,1,0:T(8,128)S(1)}, u32[]{:S(2)}, u32[]{:S(2)}) collective-permute-start(f32[32,16,128]{2,1,0:T(8,128)} %slice.132), channel_id=1, source_target_pairs={{0,1},{2,3},{4,5},{6,7},{8,9},{10,11},{12,13},{14,15},{16,17},{18,... | collective-permute-start | bytes 786440 | tf_op jit(solution)/shard_map/ppermute | solution.py:244
  35.9 2.0 %collective-permute-done.4 = f32[5,16,512]{2,1,0:T(8,128)} collective-permute-done((f32[5,16,512]{2,1,0:T(8,128)}, f32[5,16,512]{2,1,0:T(8,128)}, u32[]{:S(2)}, u32[]{:S(2)}) %collective-permute-start.4) | collective-permute-done | bytes 163872 | tf_op jit(solution)/shard_map/ppermute | solution.py:230
  37.9 1.0 %broadcast_select_fusion.4 = (f32[5,16,512]{2,1,0:T(8,128)S(1)}, f32[5,16,512]{2,1,0:T(8,128)S(1)}) fusion(f32[5,16,512]{2,1,0:T(8,128)} %collective-permute-done.4, f32[5,16,512]{2,1,0:T(8,128)} %fusion.11, pred[]{:T(512)S(6)} %eq.14), kind=kLoop, calls=%fused_computation.4 | loop fusion | flops 81920 | bytes 655361 | tf_op jit(solution)/shard_map/jit(_where)/select_n | solution.py:232
  38.9 0.7 constant_dynamic-update-slice_fusion.2
  39.6 0.6 fusion.10
  40.3 0.6 fusion.9
  40.9 0.6 fusion.8
  41.5 0.6 fusion.7
  42.1 3.0 %collective-permute-start.5 = (f32[5,16,512]{2,1,0:T(8,128)}, f32[5,16,512]{2,1,0:T(8,128)}, u32[]{:S(2)}, u32[]{:S(2)}) collective-permute-start(f32[5,16,512]{2,1,0:T(8,128)} %fusion.7), channel_id=1, source_target_pairs={{0,192},{16,208},{32,224},{48,240},{64,128},{80,144},{96,160},{112... | collective-permute-start | bytes 491528 | tf_op jit(solution)/shard_map/ppermute | solution.py:230
  45.2 1.2 %copy-done.7 = f32[32,16,512]{2,1,0:T(8,128)S(1)} copy-done((f32[32,16,512]{2,1,0:T(8,128)S(1)}, f32[32,16,512]{2,1,0:T(8,128)}, u32[]{:S(2)}) %copy-start.7) | copy-done | bytes 1048600
  46.4 3.2 %y_forward.1 = (f32[16,32,512]{2,1,0:T(8,128)S(1)}, f32[16,32,512]{2,1,0:T(8,128)S(1)}, f32[32,512]{1,0:T(8,128)S(1)}, f32[8,5,16,128]{3,2,1,0:T(8,128)}) custom-call(f32[1,128]{1,0:T(1,128)S(1)} %pad_bitcast_fusion.table_ref, s32[32,16,512]{2,1,0:T(8,128)S(1)} %copy-done.3, f32[32,16,512]{2,1,0:T(8,128)S(1)} %copy-done.6, f32[32,16,512]{2,1,0:T(8,128)S(1)} %copy-done.1, ...), custom_call_target="tpu_custom_call" | custom-call | flops 7864320 | bytes 6291456 | tf_op jit(solution)/shard_map/y_forward/pallas_call | solution.py:262
  49.6 1.0 %copy-done.12 = f32[16,32,512]{2,1,0:T(8,128)} copy-done((f32[16,32,512]{2,1,0:T(8,128)}, f32[16,32,512]{2,1,0:T(8,128)S(1)}, u32[]{:S(2)}) %copy-start.12) | copy-done | bytes 1048600
  50.5 1.0 %copy-done.14 = f32[16,32,512]{2,1,0:T(8,128)} copy-done((f32[16,32,512]{2,1,0:T(8,128)}, f32[16,32,512]{2,1,0:T(8,128)S(1)}, u32[]{:S(2)}) %copy-start.14) | copy-done | bytes 1048600
  51.5 10.1 %all-to-all-start = ((f32[8,5,16,128]{3,2,1,0:T(8,128)}), f32[8,5,16,128]{3,2,1,0:T(8,128)S(1)}, u32[]{:S(2)}, u32[]{:S(2)}) async-start(f32[8,5,16,128]{3,2,1,0:T(8,128)} %get-tuple-element.13), calls=%async_computation | async-start | bytes 655360 | tf_op jit(solution)/shard_map/all_to_all | solution.py:284
  61.7 1.0 %broadcast_select_fusion.7 = (f32[5,16,512]{2,1,0:T(8,128)S(1)}, f32[5,16,512]{2,1,0:T(8,128)S(1)}) fusion(f32[5,16,512]{2,1,0:T(8,128)} %fusion.7, f32[5,16,512]{2,1,0:T(8,128)} %collective-permute-done.5, pred[]{:T(512)S(6)} %eq.15), kind=kLoop, calls=%fused_computation.7 | loop fusion | flops 81920 | bytes 655361 | tf_op jit(solution)/shard_map/jit(_where)/select_n | solution.py:232
  62.8 1.0 %fusion.35 = (f32[16,512]{1,0:T(8,128)S(1)}, f32[16,512]{1,0:T(8,128)S(1)}, f32[16,512]{1,0:T(8,128)S(1)}) fusion(f32[16,512]{1,0:T(8,128)S(1)} %get-tuple-element.25, pred[]{:T(512)S(6)} %eq.15, pred[]{:T(512)S(6)} %eq.14, f32[5,16,512]{2,1,0:T(8,128)} %copy-done.22, f32[5,16,512]{2,1,0:T(8,128)} %copy-done.23, f32[1,16,512]{2,1,0:T(8,128)S(1)} %get-tuple-element.29, ...), kind=kLoop, calls=%fused_computation.99 | loop fusion | flops 180224 | bytes 458754 | tf_op jit(solution)/shard_map/jit(_where)/select_n | solution.py:239
  63.8 9.1 %all-to-all-done.blocks_ref = f32[8,5,16,128]{3,2,1,0:T(8,128)S(1)} async-done(((f32[8,5,16,128]{3,2,1,0:T(8,128)}), f32[8,5,16,128]{3,2,1,0:T(8,128)S(1)}, u32[]{:S(2)}, u32[]{:S(2)}) %all-to-all-start) | async-done | bytes 327712 | tf_op jit(solution)/shard_map/all_to_all | solution.py:284
  72.8 0.8 y_reduced.1
  73.6 3.4 %all-to-all-start.1 = ((f32[8,2,16,128]{3,2,1,0:T(8,128)}), f32[8,2,16,128]{3,2,1,0:T(8,128)S(1)}, u32[]{:S(2)}, u32[]{:S(2)}) async-start(f32[8,2,16,128]{3,2,1,0:T(8,128)} %y_reduced.1), calls=%async_computation.1 | async-start | bytes 262144 | tf_op jit(solution)/shard_map/all_to_all | solution.py:317
  77.0 0.9 %broadcast_select_fusion.11 = (f32[16,512]{1,0:T(8,128)S(1)}, f32[16,512]{1,0:T(8,128)S(1)}, f32[16,512]{1,0:T(8,128)S(1)}, f32[16,512]{1,0:T(8,128)S(1)}) fusion(pred[]{:T(512)S(6)} %eq.12, f32[16,512]{1,0:T(8,128)S(1)} %get-tuple-element.22, pred[]{:T(512)S(6)} %eq.13, f32[5,16,512]{2,1,0:T(8,128)} %copy-done.18, f32[5,16,512]{2,1,0:T(8,128)} %copy-done.19, ...), kind=kLoop, calls=%fused_computation.102 | loop fusion | flops 221184 | bytes 557060 | tf_op jit(solution)/shard_map/jit(_where)/select_n | solution.py:239
  78.0 0.7 copy-done.17
  78.7 1.2 %x_back.1 = f32[32,16,512]{2,1,0:T(8,128)} custom-call(f32[32,16,512]{2,1,0:T(8,128)S(1)} %copy-done.9, f32[32,16,512]{2,1,0:T(8,128)S(1)} %copy-done.11, f32[16,512]{1,0:T(8,128)S(1)} %copy-done.17, f32[16,512]{1,0:T(8,128)S(1)} %broadcast_select_fusion.12.before_ref, f32[16,512]{1,0:T(8,128)S(1)} %get-tuple-element.18.here_ref), custom_call_target="tpu_custom_call" | custom-call | flops 1310720 | bytes 3145728 | tf_op jit(solution)/shard_map/x_back/pallas_call | solution.py:319
  79.9 6.1 %all-to-all-done.1.ends_ref = f32[8,2,16,128]{3,2,1,0:T(8,128)S(1)} async-done(((f32[8,2,16,128]{3,2,1,0:T(8,128)}), f32[8,2,16,128]{3,2,1,0:T(8,128)S(1)}, u32[]{:S(2)}, u32[]{:S(2)}) %all-to-all-start.1) | async-done | bytes 131104 | tf_op jit(solution)/shard_map/all_to_all | solution.py:317
  86.0 1.2 %copy-done.15 = f32[16,32,512]{2,1,0:T(8,128)S(1)} copy-done((f32[16,32,512]{2,1,0:T(8,128)S(1)}, f32[16,32,512]{2,1,0:T(8,128)}, u32[]{:S(2)}) %copy-start.15) | copy-done | bytes 1048600
  87.2 1.9 %y_back.1 = f32[32,16,512]{2,1,0:T(8,128)} custom-call(f32[16,32,512]{2,1,0:T(8,128)S(1)} %copy-done.13, f32[16,32,512]{2,1,0:T(8,128)S(1)} %copy-done.15, f32[32,512]{1,0:T(8,128)S(1)} %get-tuple-element.12.rim_ref, f32[8,2,16,128]{3,2,1,0:T(8,128)S(1)} %all-to-all-done.1.ends_ref), custom_call_target="tpu_custom_call" | custom-call | flops 1310720 | bytes 3145728 | tf_op jit(solution)/shard_map/y_back/pallas_call | solution.py:327
  (58 shorter events, 0.3 us)
Async XLA Ops:
  1.8 3.8 %copy-start.28 = (f32[16]{0:T(128)S(1)}, f32[16]{0:T(128)}, u32[]{:S(2)}) copy-start(f32[16]{0:T(128)} %param.13) | copy-start | bytes 196
  1.8 5.7 %collective-permute-start.1 = (f32[32,512]{1,0:T(8,128)S(1)}, f32[32,512]{1,0:T(8,128)S(1)}, u32[]{:S(2)}, u32[]{:S(2)}) collective-permute-start(f32[32,512]{1,0:T(8,128)S(1)} %bitcast.159), channel_id=1, source_target_pairs={{0,2},{2,4},{4,6},{6,8},{8,10},{10,12},{12,14},{1,3},{3,5},{5,7},{... | collective-permute-start | bytes 196616 | tf_op jit(solution)/shard_map/ppermute | solution.py:244
  7.5 1.2 %copy-start = (f32[32,16,512]{2,1,0:T(8,128)S(1)}, f32[32,16,512]{2,1,0:T(8,128)}, u32[]{:S(2)}) copy-start(f32[32,16,512]{2,1,0:T(8,128)} %my_ref.3) | copy-start | bytes 3145732
  8.7 1.2 %copy-start.2 = (s32[32,16,512]{2,1,0:T(8,128)S(1)}, s32[32,16,512]{2,1,0:T(8,128)}, u32[]{:S(2)}) copy-start(s32[32,16,512]{2,1,0:T(8,128)} %material_ref.3) | copy-start | bytes 3145732
  9.9 1.2 %copy-start.4 = (f32[32,16,512]{2,1,0:T(8,128)S(1)}, f32[32,16,512]{2,1,0:T(8,128)}, u32[]{:S(2)}) copy-start(f32[32,16,512]{2,1,0:T(8,128)} %mx_ref.1) | copy-start | bytes 3145732
  11.2 1.2 %copy-start.5 = (f32[32,16,512]{2,1,0:T(8,128)S(1)}, f32[32,16,512]{2,1,0:T(8,128)}, u32[]{:S(2)}) copy-start(f32[32,16,512]{2,1,0:T(8,128)} %ez_ref.1) | copy-start | bytes 3145732
  13.6 1.0 %copy-start.8 = (f32[32,16,512]{2,1,0:T(8,128)}, f32[32,16,512]{2,1,0:T(8,128)S(1)}, u32[]{:S(2)}) copy-start(f32[32,16,512]{2,1,0:T(8,128)S(1)} %get-tuple-element.14.t_ref) | copy-start | bytes 3145732
  14.5 1.0 %copy-start.10 = (f32[32,16,512]{2,1,0:T(8,128)}, f32[32,16,512]{2,1,0:T(8,128)S(1)}, u32[]{:S(2)}) copy-start(f32[32,16,512]{2,1,0:T(8,128)S(1)} %get-tuple-element.15.drive_ref) | copy-start | bytes 3145732
  15.5 0.6 copy-start.16
  16.1 5.3 %collective-permute-start.2 = (f32[5,16,512]{2,1,0:T(8,128)S(1)}, f32[5,16,512]{2,1,0:T(8,128)S(1)}, u32[]{:S(2)}, u32[]{:S(2)}) collective-permute-start(f32[5,16,512]{2,1,0:T(8,128)S(1)} %get-tuple-element.17), channel_id=1, source_target_pairs={{0,16},{16,0},{32,48},{48,32},{64,80},{80,64},{96,112},{112,96},{1... | collective-permute-start | bytes 491528 | tf_op jit(solution)/shard_map/ppermute | solution.py:230
  21.5 0.8 copy-start.18
  21.5 0.8 copy-start.19
  21.5 0.7 copy-start.24
  22.2 11.6 %copy-start.1 = (f32[32,16,512]{2,1,0:T(8,128)S(1)}, f32[32,16,512]{2,1,0:T(8,128)}, u32[]{:S(2)}) copy-start(f32[32,16,512]{2,1,0:T(8,128)} %my_ref.3) | copy-start | bytes 3145732
  22.3 6.6 %collective-permute-start.3 = (f32[5,16,512]{2,1,0:T(8,128)S(1)}, f32[5,16,512]{2,1,0:T(8,128)S(1)}, u32[]{:S(2)}, u32[]{:S(2)}) collective-permute-start(f32[5,16,512]{2,1,0:T(8,128)S(1)} %fusion.15), channel_id=1, source_target_pairs={{0,48},{16,32},{32,16},{48,0},{64,112},{80,96},{96,80},{112,64},{1... | collective-permute-start | bytes 491528 | tf_op jit(solution)/shard_map/ppermute | solution.py:230
  29.0 2.6 %copy-start.20 = (f32[5,16,512]{2,1,0:T(8,128)}, f32[5,16,512]{2,1,0:T(8,128)S(1)}, u32[]{:S(2)}) copy-start(f32[5,16,512]{2,1,0:T(8,128)S(1)} %get-tuple-element.40) | copy-start | bytes 491524
  29.0 2.6 %copy-start.21 = (f32[5,16,512]{2,1,0:T(8,128)}, f32[5,16,512]{2,1,0:T(8,128)S(1)}, u32[]{:S(2)}) copy-start(f32[5,16,512]{2,1,0:T(8,128)S(1)} %get-tuple-element.41) | copy-start | bytes 491524
  29.7 0.6 copy-start.26
  32.2 12.9 %copy-start.3 = (s32[32,16,512]{2,1,0:T(8,128)S(1)}, s32[32,16,512]{2,1,0:T(8,128)}, u32[]{:S(2)}) copy-start(s32[32,16,512]{2,1,0:T(8,128)} %material_ref.3) | copy-start | bytes 3145732
  32.2 12.9 %copy-start.6 = (f32[32,16,512]{2,1,0:T(8,128)S(1)}, f32[32,16,512]{2,1,0:T(8,128)}, u32[]{:S(2)}) copy-start(f32[32,16,512]{2,1,0:T(8,128)} %ex_ref.1) | copy-start | bytes 3145732
  32.2 5.6 %collective-permute-start.4 = (f32[5,16,512]{2,1,0:T(8,128)}, f32[5,16,512]{2,1,0:T(8,128)}, u32[]{:S(2)}, u32[]{:S(2)}) collective-permute-start(f32[5,16,512]{2,1,0:T(8,128)} %fusion.11), channel_id=1, source_target_pairs={{0,64},{16,80},{32,96},{48,112},{64,0},{80,16},{96,32},{112,48},{1... | collective-permute-start | bytes 491528 | tf_op jit(solution)/shard_map/ppermute | solution.py:230
  34.5 10.6 %collective-permute-start = (f32[32,16,128]{2,1,0:T(8,128)}, f32[32,16,128]{2,1,0:T(8,128)S(1)}, u32[]{:S(2)}, u32[]{:S(2)}) collective-permute-start(f32[32,16,128]{2,1,0:T(8,128)} %slice.132), channel_id=1, source_target_pairs={{0,1},{2,3},{4,5},{6,7},{8,9},{10,11},{12,13},{14,15},{16,17},{18,... | collective-permute-start | bytes 786440 | tf_op jit(solution)/shard_map/ppermute | solution.py:244
  38.9 2.6 %copy-start.22 = (f32[5,16,512]{2,1,0:T(8,128)}, f32[5,16,512]{2,1,0:T(8,128)S(1)}, u32[]{:S(2)}) copy-start(f32[5,16,512]{2,1,0:T(8,128)S(1)} %get-tuple-element.38) | copy-start | bytes 491524
  38.9 2.6 %copy-start.23 = (f32[5,16,512]{2,1,0:T(8,128)}, f32[5,16,512]{2,1,0:T(8,128)S(1)}, u32[]{:S(2)}) copy-start(f32[5,16,512]{2,1,0:T(8,128)S(1)} %get-tuple-element.39) | copy-start | bytes 491524
  42.1 19.5 %collective-permute-start.5 = (f32[5,16,512]{2,1,0:T(8,128)}, f32[5,16,512]{2,1,0:T(8,128)}, u32[]{:S(2)}, u32[]{:S(2)}) collective-permute-start(f32[5,16,512]{2,1,0:T(8,128)} %fusion.7), channel_id=1, source_target_pairs={{0,192},{16,208},{32,224},{48,240},{64,128},{80,144},{96,160},{112... | collective-permute-start | bytes 491528 | tf_op jit(solution)/shard_map/ppermute | solution.py:230
  45.2 1.2 %copy-start.7 = (f32[32,16,512]{2,1,0:T(8,128)S(1)}, f32[32,16,512]{2,1,0:T(8,128)}, u32[]{:S(2)}) copy-start(f32[32,16,512]{2,1,0:T(8,128)} %mz_ref.1) | copy-start | bytes 3145732
  49.6 1.0 %copy-start.12 = (f32[16,32,512]{2,1,0:T(8,128)}, f32[16,32,512]{2,1,0:T(8,128)S(1)}, u32[]{:S(2)}) copy-start(f32[16,32,512]{2,1,0:T(8,128)S(1)} %get-tuple-element.10.t_ref) | copy-start | bytes 3145732
  50.5 1.0 %copy-start.14 = (f32[16,32,512]{2,1,0:T(8,128)}, f32[16,32,512]{2,1,0:T(8,128)S(1)}, u32[]{:S(2)}) copy-start(f32[16,32,512]{2,1,0:T(8,128)S(1)} %get-tuple-element.11.drive_ref) | copy-start | bytes 3145732
  51.5 21.3 %all-to-all-start = ((f32[8,5,16,128]{3,2,1,0:T(8,128)}), f32[8,5,16,128]{3,2,1,0:T(8,128)S(1)}, u32[]{:S(2)}, u32[]{:S(2)}) async-start(f32[8,5,16,128]{3,2,1,0:T(8,128)} %get-tuple-element.13), calls=%async_computation | async-start | bytes 655360 | tf_op jit(solution)/shard_map/all_to_all | solution.py:284
  61.7 15.3 %copy-start.25 = (f32[1,16,512]{2,1,0:T(8,128)S(1)}, f32[1,16,512]{2,1,0:T(8,128)}, u32[]{:S(2)}) copy-start(f32[1,16,512]{2,1,0:T(8,128)} %copy-done.24) | copy-start | bytes 98308
  61.7 15.3 %copy-start.27 = (f32[1,16,512]{2,1,0:T(8,128)S(1)}, f32[1,16,512]{2,1,0:T(8,128)}, u32[]{:S(2)}) copy-start(f32[1,16,512]{2,1,0:T(8,128)} %copy-done.26) | copy-start | bytes 98308
  62.7 15.3 %copy-start.9 = (f32[32,16,512]{2,1,0:T(8,128)S(1)}, f32[32,16,512]{2,1,0:T(8,128)}, u32[]{:S(2)}) copy-start(f32[32,16,512]{2,1,0:T(8,128)} %copy-done.8) | copy-start | bytes 3145732
  62.7 15.3 %copy-start.11 = (f32[32,16,512]{2,1,0:T(8,128)S(1)}, f32[32,16,512]{2,1,0:T(8,128)}, u32[]{:S(2)}) copy-start(f32[32,16,512]{2,1,0:T(8,128)} %copy-done.10) | copy-start | bytes 3145732
  73.6 12.4 %all-to-all-start.1 = ((f32[8,2,16,128]{3,2,1,0:T(8,128)}), f32[8,2,16,128]{3,2,1,0:T(8,128)S(1)}, u32[]{:S(2)}, u32[]{:S(2)}) async-start(f32[8,2,16,128]{3,2,1,0:T(8,128)} %y_reduced.1), calls=%async_computation.1 | async-start | bytes 262144 | tf_op jit(solution)/shard_map/all_to_all | solution.py:317
  78.0 0.8 copy-start.17
  78.7 7.3 %copy-start.13 = (f32[16,32,512]{2,1,0:T(8,128)S(1)}, f32[16,32,512]{2,1,0:T(8,128)}, u32[]{:S(2)}) copy-start(f32[16,32,512]{2,1,0:T(8,128)} %copy-done.12) | copy-start | bytes 3145732
  86.0 1.2 %copy-start.15 = (f32[16,32,512]{2,1,0:T(8,128)S(1)}, f32[16,32,512]{2,1,0:T(8,128)}, u32[]{:S(2)}) copy-start(f32[16,32,512]{2,1,0:T(8,128)} %copy-done.14) | copy-start | bytes 3145732

commit v2 on v1

v2 whole, which is shorter than its diff:
```python
import functools

import jax
import jax.numpy as jnp
from jax import lax
from jax.experimental import pallas as pl
from jax.experimental.pallas import tpu as pltpu
from jax.sharding import PartitionSpec as P

ground_scale = 1.0 / 1600.0
drive_scale = 1.0 / 40.0
lane = 128
rows = 8
pair = 2
long = 8
hold_bit = 2
f32 = jnp.float32


def inverse(x):
    return pltpu.reciprocal(x, approx=True)


def table_lookup(table, index):
    return jnp.take_along_axis(
        jnp.broadcast_to(table, index.shape), index, axis=1, mode="promise_in_bounds"
    )


def eliminate(state, ground, drive):
    link, left, here, left_drive, here_drive = state
    t = inverse(link + here + 1.0)
    next_link = link * t
    return (
        next_link,
        left + next_link * here,
        ground + here * t,
        left_drive + next_link * here_drive,
        drive + here_drive * t,
    ), t


def close_block(state, rim):
    link, left, here, left_drive, here_drive = state
    return (
        link,
        left,
        here,
        left_drive + link * rim,
        here_drive - (link + here + 1.0) * rim,
    )


def forward_kernel(
    table_ref, material_ref, ex_ref, ez_ref, mx_ref, my_ref, mz_ref, edge_ref,
    yt_ref, ydrive_ref, yreduced_ref, xt_ref, xdrive_ref, xreduced_ref, t_edge_ref,
    ground_s, drive_s, state_s, my_s,
):
    xs, ys, zs = material_ref.shape
    step = pl.program_id(0)
    tiles = zs // lane
    flat = (xs * ys, lane)
    table = table_ref[...] * ground_scale
    first_lane = lax.broadcasted_iota(jnp.int32, flat, 1) == 0
    first_y = lax.broadcasted_iota(jnp.int32, (xs, ys, lane), 1) == 0
    first_cell = step == 0

    @pl.when(first_cell)
    def _():
        state_s[...] = jnp.zeros_like(state_s)
        my_s[...] = jnp.zeros_like(my_s)

    before = pltpu.roll(edge_ref[...].reshape(flat), 1, 1)
    for k in range(tiles):
        cut = pl.ds(k * lane, lane)
        ground = table_lookup(table, material_ref[:, :, cut].reshape(flat))
        my = my_ref[:, :, cut]
        rolled = pltpu.roll(my.reshape(flat), 1, 1)
        my_step = my.reshape(flat) - jnp.where(first_lane, before, rolled)
        before = rolled
        mz = mz_ref[:, :, cut]
        mz_step = mz - jnp.where(first_y, 0.0, pltpu.roll(mz, 1, 1))
        ground_s[k] = ground
        drive_s[k] = ground * ex_ref[:, :, cut].reshape(flat) + drive_scale * (mz_step.reshape(flat) - my_step)
        mx = mx_ref[:, :, cut]
        mx_step = mx - jnp.where(first_y, 0.0, pltpu.roll(mx, 1, 1))

        state = tuple(state_s[v, :, cut] for v in range(5))
        last_my = my_s[:, cut]
        ground = ground.reshape(xs, ys, lane)
        for i in range(xs):
            drive = ground[i] * ez_ref[i, :, cut] + drive_scale * ((my[i] - last_my) - mx_step[i])
            last_my = my[i]
            state, t = eliminate(state, ground[i], drive)
            if i == 0:
                state = (jnp.where(first_cell, 1.0, state[0]),) + state[1:]
            xt_ref[i, :, cut] = t
            t_edge_ref[pl.ds(i, 1), cut] = t[0:1]
            xdrive_ref[i, :, cut] = state[4]
        for v in range(5):
            state_s[v, :, cut] = state[v]
        my_s[:, cut] = last_my
        rim = drive_scale * last_my

        @pl.when(step == pl.num_programs(0) - 1)
        def _(rim=rim, cut=cut):
            xdrive_ref[xs - 1, :, cut] = rim

        for v, value in enumerate(close_block(state, rim)):
            xreduced_ref[v, :, cut] = value
        if k % pair == pair - 1:
            y_eliminate(range(k - pair + 1, k + 1), mz_ref, yt_ref, ydrive_ref, yreduced_ref, ground_s, drive_s)


kept_count = 13


def x_edge_kernel(edge_ref, t_ref, reduced_ref, reduced_out, kept_ref):
    xs = t_ref.shape[0]
    row = pl.ds(0, 1)
    here = drive_scale * edge_ref[row, :]
    link = jnp.ones_like(here)
    left = jnp.zeros_like(here)
    kept_ref[11, row, :] = here
    for i in range(1, xs):
        t = t_ref[pl.ds(i, 1), :]
        link = link * t
        left = left + link * here
        here = drive_scale * edge_ref[pl.ds(i, 1), :] + here * t
        kept_ref[11 + i // 16, pl.ds(i % 16, 1), :] = here
    for v in range(5):
        reduced_out[v] = reduced_ref[v]
    reduced_out[3, row, :] = reduced_ref[3, row, :] + left
    reduced_out[4, row, :] = reduced_ref[4, row, :] + here


def y_eliminate(tiles, mz_ref, t_ref, drive_ref, reduced_ref, ground_s, drive_s):
    xs, ys, _ = mz_ref.shape
    for c in range(xs // rows):
        here = (pl.ds(c * rows, rows), pl.ds(tiles[0] * lane, pair * lane))
        state = None
        for j in range(ys):
            pick = pl.ds(c * rows * ys + j, rows, stride=ys)
            ground = jnp.concatenate([ground_s[k, pick, :] for k in tiles], axis=1)
            drive = jnp.concatenate([drive_s[k, pick, :] for k in tiles], axis=1)
            if j == 0:
                zero = jnp.zeros_like(ground)
                state = (jnp.ones_like(ground), zero, ground, zero, drive)
            else:
                state, t = eliminate(state, ground, drive)
                t_ref[(j - 1,) + here] = t
            if j < ys - 1:
                drive_ref[(j,) + here] = state[4]
        rim = drive_scale * mz_ref[here[0], ys - 1, here[1]]
        drive_ref[(ys - 1,) + here] = rim
        for v, value in enumerate(close_block(state, rim)):
            for n, k in enumerate(tiles):
                reduced_ref[2 * c + k // 2, v, pl.ds((k % 2) * rows, rows), :] = value[:, n * lane:(n + 1) * lane]


def y_reduced_kernel(blocks_ref, ends_ref):
    count = blocks_ref.shape[0]
    block = [[blocks_ref[b, v] for v in range(5)] for b in range(count)]
    here = block[0][2] + block[0][0]
    drive = block[0][4]
    kept = []
    for b in range(1, count):
        link, left, right, left_drive, right_drive = block[b]
        total = here + left
        t = inverse(total + link)
        pull = link * t
        push = drive + left_drive
        kept.append((pull, push * t))
        here = right + pull * total
        drive = right_drive + pull * push
    value = drive * inverse(here + 1.0)
    ends_ref[count - 1, 1] = value
    for b in range(count - 1, 0, -1):
        pull, push = kept[b - 1]
        value = push + pull * value
        ends_ref[b, 0] = value
        ends_ref[b - 1, 1] = value
    ends_ref[0, 0] = jnp.zeros_like(value)


def y_back_kernel(t_ref, drive_ref, ends_ref, out_ref, out_s):
    ys, xs, zs = t_ref.shape
    for k in range(zs // lane):
        cut = pl.ds(k * lane, lane)
        half = pl.ds((k % 2) * rows, rows)
        before = ends_ref[k // 2, 0, half, :]
        value = ends_ref[k // 2, 1, half, :] + drive_ref[ys - 1, :, cut]
        reach = before
        parts = []
        for j in range(ys - 1):
            t = t_ref[j, :, cut]
            reach_t = reach * t
            parts.append((t, drive_ref[j, :, cut] * t + reach_t))
            reach = reach_t
        out_s[pl.ds(ys - 1, xs, stride=ys), :] = value
        for j in range(ys - 2, -1, -1):
            t, part = parts[j]
            value = part + t * value
            out_s[pl.ds(j, xs, stride=ys), :] = value
        out_ref[:, :, cut] = out_s[...].reshape(xs, ys, lane)


def x_back_kernel(low_ref, t_ref, drive_ref, kept_ref, side_ref, other_ref, out_ref):
    xs, ys, zs = t_ref.shape
    top = low_ref[3] == 1
    middle = (side_ref[1] + other_ref[1]) * inverse(side_ref[0] + other_ref[0])
    before = jnp.where(top, 0.0, middle)
    here = jnp.where(top, middle, kept_ref[9] + kept_ref[10] * middle)
    for level in (2, 1, 0):
        low = low_ref[level] == 1
        middle = kept_ref[3 * level] + kept_ref[3 * level + 1] * before + kept_ref[3 * level + 2] * here
        before, here = jnp.where(low, before, middle), jnp.where(low, middle, here)
    first_y = lax.broadcasted_iota(jnp.int32, (ys, zs), 0) == 0
    reach = before
    for i in range(xs - 1):
        t = t_ref[i + 1]
        edge = jnp.where(first_y, kept_ref[11 + i // 16, pl.ds(i % 16, 1), :], 0.0)
        reach = reach * t
        out_ref[i] = (drive_ref[i] + edge) * t + reach
    value = here + drive_ref[xs - 1]
    out_ref[xs - 1] = value
    for i in range(xs - 2, -1, -1):
        value = out_ref[i] + t_ref[i + 1] * value
        out_ref[i] = value


def cost(elements, ops, arrays):
    return pl.CostEstimate(flops=elements * ops, bytes_accessed=elements * 4 * arrays, transcendentals=0)


def merge(low, own_ref, other_ref, kept_ref, slot):
    own = [own_ref[v] for v in range(5)]
    other = [other_ref[v] for v in range(5)]
    a = [jnp.where(low, p, q) for p, q in zip(own, other)]
    b = [jnp.where(low, q, p) for p, q in zip(own, other)]
    total = a[2] + b[1]
    t = inverse(total + a[0] + b[0])
    a_link, b_link = a[0] * t, b[0] * t
    push = a[4] + b[3]
    kept_ref[slot] = push * t
    kept_ref[slot + 1] = a_link
    kept_ref[slot + 2] = b_link
    return (
        a[0] * b_link,
        a[1] + a_link * total,
        b[2] + b_link * total,
        a[3] + a_link * push,
        b[4] + b_link * push,
    )


def merge_kernel(level, low_ref, own_ref, other_ref, _, merged_ref, kept_ref):
    merged = merge(low_ref[level] == 1, own_ref, other_ref, kept_ref, 3 * level)
    for v in range(5):
        merged_ref[v] = merged[v]


def last_merge_kernel(low_ref, own_ref, other_ref, _, side_ref, kept_ref):
    link, left, right, left_drive, right_drive = merge(low_ref[2] == 1, own_ref, other_ref, kept_ref, 6)
    closed = inverse(right + link + 1.0)
    share = link * closed
    top = low_ref[3] == 1
    side_ref[0] = jnp.where(top, right + link, left + share * (right + 1.0))
    side_ref[1] = jnp.where(top, right_drive, left_drive + share * right_drive)
    kept_ref[9] = closed * right_drive
    kept_ref[10] = share


def exchange(x, axis, mask):
    return lax.ppermute(x, axis, [(i, i ^ mask) for i in range(lax.axis_size(axis))])


def in_vmem(a):
    return pltpu.with_memory_space_constraint(a, pltpu.VMEM)


def merge_call(kernel, low, own, other, kept, size):
    _, ys, zs = own.shape
    whole = pl.BlockSpec(memory_space=pltpu.VMEM)
    return pl.pallas_call(
        kernel,
        in_specs=[pl.BlockSpec(memory_space=pltpu.SMEM)] + [whole] * 3,
        out_specs=[whole] * 2,
        out_shape=[pltpu.VMEM((size, ys, zs), f32), pltpu.VMEM(kept.shape, f32)],
        input_output_aliases={3: 1},
        compiler_params=pltpu.CompilerParams(vmem_limit_bytes=8 * 2**20),
        cost_estimate=cost(own.size, 10, 3),
        name="x_merge",
    )(low, in_vmem(own), in_vmem(other), in_vmem(kept))


def load_kernel(t_ref, drive_ref, _, t_out, drive_out, sems):
    copies = [
        pltpu.make_async_copy(t_ref, t_out, sems.at[0]),
        pltpu.make_async_copy(drive_ref, drive_out, sems.at[1]),
    ]
    for copy in copies:
        copy.start()
    for copy in copies:
        copy.wait()


def load(t, drive, after):
    in_hbm_spec = pl.BlockSpec(memory_space=pltpu.HBM)
    whole = pl.BlockSpec(memory_space=pltpu.VMEM)
    return pl.pallas_call(
        load_kernel,
        in_specs=[in_hbm_spec] * 2 + [pl.BlockSpec(memory_space=pl.ANY)],
        out_specs=[whole] * 2,
        out_shape=[pltpu.VMEM(t.shape, f32)] * 2,
        scratch_shapes=[pltpu.SemaphoreType.DMA((2,))],
        compiler_params=pltpu.CompilerParams(vmem_limit_bytes=8 * 2**20),
        cost_estimate=cost(t.size, 1, 4),
        name="load",
    )(*(pltpu.with_memory_space_constraint(a, pltpu.HBM) for a in (t, drive)), after)


def shift_up(x, axis):
    return lax.ppermute(x, axis, [(i, i + 1) for i in range(lax.axis_size(axis) - 1)])


def per_device(electric_x, electric_z, magnetic_x, magnetic_y, magnetic_z, material, perm_table):
    xs, ys, zs = material.shape
    chunks = xs // rows
    cells = xs * ys * zs
    sds = jax.ShapeDtypeStruct
    table = jnp.pad(perm_table, (0, lane - perm_table.shape[0])).reshape(1, lane)

    edge_z = shift_up(magnetic_y[:, :, zs - lane:], "gz")
    edge_y = shift_up(magnetic_x[:, ys - 1], "gy")

    def in_hbm(a):
        return pltpu.with_memory_space_constraint(a, pltpu.HBM)

    slab = pl.BlockSpec((rows, ys, zs), lambda c: (c, 0, 0))
    turned = pl.BlockSpec((ys, rows, zs), lambda c: (0, c, 0))
    long_slab = pl.BlockSpec((long, ys, zs), lambda c: (c, 0, 0))
    long_turned = pl.BlockSpec((ys, long, zs), lambda c: (0, c, 0))
    whole_table = pl.BlockSpec((1, lane), lambda c: (0, 0))
    vmem = pltpu.CompilerParams(vmem_limit_bytes=24 * 2**20)

    y_t, y_drive, y_reduced, x_t, x_drive, x_reduced, t_edge = pl.pallas_call(
        forward_kernel,
        grid=(xs // long,),
        in_specs=[whole_table] + [long_slab] * 6 + [pl.BlockSpec((long, ys, lane), lambda c: (c, 0, 0))],
        out_specs=[
            long_turned,
            long_turned,
            pl.BlockSpec((long // 4, 5, 2 * rows, lane), lambda c: (c, 0, 0, 0)),
            long_slab,
            long_slab,
            pl.BlockSpec((5, ys, zs), lambda c: (0, 0, 0)),
            pl.BlockSpec((long, zs), lambda c: (c, 0)),
        ],
        out_shape=[
            pltpu.HBM((ys, xs, zs), f32),
            pltpu.HBM((ys, xs, zs), f32),
            pltpu.HBM((2 * chunks, 5, 2 * rows, lane), f32),
            pltpu.HBM((xs, ys, zs), f32),
            pltpu.HBM((xs, ys, zs), f32),
            pltpu.VMEM((5, ys, zs), f32),
            pltpu.VMEM((xs, zs), f32),
        ],
        scratch_shapes=[pltpu.VMEM((zs // lane, long * ys, lane), f32)] * 2
        + [pltpu.VMEM((5, ys, zs), f32), pltpu.VMEM((ys, zs), f32)],
        compiler_params=vmem,
        cost_estimate=cost(cells, 60, 10),
        name="forward",
    )(
        table, in_hbm(material), in_hbm(electric_x), in_hbm(electric_z), in_hbm(magnetic_x),
        in_hbm(magnetic_y), in_hbm(magnetic_z), edge_z,
    )

    y_reduced, edge_y = lax.optimization_barrier((y_reduced, edge_y))
    y_blocks = lax.all_to_all(y_reduced, "gy", 0, 0, tiled=True)

    in_place = pl.BlockSpec(memory_space=pltpu.VMEM)
    x_reduced, kept = pl.pallas_call(
        x_edge_kernel,
        in_specs=[in_place] * 3,
        out_specs=[in_place] * 2,
        out_shape=[pltpu.VMEM((5, ys, zs), f32), pltpu.VMEM((kept_count, ys, zs), f32)],
        compiler_params=vmem,
        cost_estimate=cost(cells // ys, 10, 3),
        name="x_edge",
    )(edge_y, t_edge, x_reduced)

    y_ends = pl.pallas_call(
        y_reduced_kernel,
        out_shape=pltpu.HBM((2 * chunks, 2, 2 * rows, lane), f32),
        compiler_params=vmem,
        cost_estimate=cost(y_blocks.size // 5, 20, 7),
        name="y_reduced",
    )(y_blocks)

    hold_level = 1
    place = lax.axis_index("gx")
    low = jnp.stack([((place & bit) == 0).astype(jnp.int32) for bit in (1, 2, 4, 8)])
    own = x_reduced
    for level, mask in enumerate((1, 3, 4)):
        other = exchange(own, "gx", mask)
        if level == hold_level:
            other, y_ends = lax.optimization_barrier((other, y_ends))
        kernel = functools.partial(merge_kernel, level) if level < 2 else last_merge_kernel
        own, kept = merge_call(kernel, low, own, other, kept, 5 if level < 2 else 2)
    x_t, x_drive = load(x_t, x_drive, own)
    side_other = exchange(own, "gx", 12)
    y_t, y_drive = load(y_t, y_drive, y_ends)
    y_ends = lax.all_to_all(y_ends, "gy", 0, 0, tiled=True)

    electric_z_half = pl.pallas_call(
        x_back_kernel,
        in_specs=[pl.BlockSpec(memory_space=pltpu.SMEM)] + [pl.BlockSpec(memory_space=pltpu.VMEM)] * 5,
        out_shape=sds((xs, ys, zs), f32),
        compiler_params=vmem,
        cost_estimate=cost(cells, 5, 3),
        name="x_back",
    )(low, *map(in_vmem, (x_t, x_drive, kept, own, side_other)))

    electric_x_half = pl.pallas_call(
        y_back_kernel,
        grid=(chunks,),
        in_specs=[
            turned,
            turned,
            pl.BlockSpec((2, 2, 2 * rows, lane), lambda c: (c, 0, 0, 0)),
        ],
        out_specs=slab,
        out_shape=sds((xs, ys, zs), f32),
        scratch_shapes=[pltpu.VMEM((rows * ys, lane), f32)],
        compiler_params=vmem,
        cost_estimate=cost(cells, 5, 3),
        name="y_back",
    )(in_vmem(y_t), in_vmem(y_drive), y_ends)
    return (electric_x_half, electric_z_half)


def solution(mesh):
    field = P("gx", "gy", "gz")
    return jax.shard_map(
        per_device,
        mesh=mesh,
        in_specs=(field,) * 6 + (P(),),
        out_specs=(field, field),
        check_vma=False,
    )
```

time: 90 us -> 61.7 us (0.69)
  the two profiles are of different devices: /device:TPU:6 before, /device:TPU:32 now
where the time goes in v2:
time: 61.7 us; the launch traced here: 61.1 us
  starting transfers between devices  29.7 us (48%)
  Pallas kernels  16.1 us (26%)
  waiting for transfers between devices  10.5 us (17%)
  local copies, waits for them, and re-layouts  4.07 us (7%)
  between operations  0.76 us (1%)
    ppermute x4, starting transfers between devices, exchange(): lax.ppermute(x, axis, [(i, i ^ mask) for i in range(lax.axis_size(axis))])  9.18 us
    ppermute x4, waiting for transfers between devices, exchange(): lax.ppermute(x, axis, [(i, i ^ mask) for i in range(lax.axis_size(axis))])  8.33 us
    all_to_all x1, starting transfers between devices, per_device(): y_blocks = lax.all_to_all(y_reduced, 'gy', 0, 0, tiled=True)  7.68 us
    all_to_all x1, starting transfers between devices, per_device(): y_ends = lax.all_to_all(y_ends, 'gy', 0, 0, tiled=True)  7.21 us
    pallas_call x1, Pallas kernels, per_device(): pl.pallas_call(forward_kernel, grid=(xs // long,), in_specs=[whole_table]...  6.61 us
    ppermute x2, starting transfers between devices, shift_up(): lax.ppermute(x, axis, [(i, i + 1) for i in range(lax.axis_size(axis) - 1)])  5.58 us
    pallas_call x2, Pallas kernels, load(): pl.pallas_call(load_kernel, in_specs=[in_hbm_spec] * 2 + [pl.BlockSpec(me...  3.12 us
    all_to_all x1, waiting for transfers between devices, per_device(): y_blocks = lax.all_to_all(y_reduced, 'gy', 0, 0, tiled=True)  2.18 us
  transfers between devices with their start and end apart: 8, of which 4 were waited for; matrix products, arithmetic and copies ran while one was open for 2% of the time, Pallas kernels for 23%

profile of v2, /device:TPU:32, one launch (start us, length us, event | category | flops | bytes accessed | tf_op | source)
XLA Modules:
  0.0 61.1 jit_solution(818255463755322350)
XLA Ops:
  0.6 1.0 %slice.6 = f32[32,16,128]{2,1,0:T(8,128)S(1)} slice(f32[32,16,512]{2,1,0:T(8,128)} %my_ref.1), slice={[0:32], [0:16], [384:512]} | slice | bytes 524288 | tf_op jit(solution)/shard_map/slice | solution.py:334
  1.6 1.8 %collective-permute-start = (f32[32,16,128]{2,1,0:T(8,128)S(1)}, f32[32,16,128]{2,1,0:T(8,128)S(1)}, u32[]{:S(2)}, u32[]{:S(2)}) collective-permute-start(f32[32,16,128]{2,1,0:T(8,128)S(1)} %slice.6), channel_id=1, source_target_pairs={{0,1},{2,3},{4,5},{6,7},{8,9},{10,11},{12,13},{14,15},{16,17},{18,... | collective-permute-start | bytes 786440 | tf_op jit(solution)/shard_map/ppermute | solution.py:324
  3.4 1.1 %slice.7 = f32[32,1,512]{2,1,0:T(1,128)S(1)} slice(f32[32,16,512]{2,1,0:T(8,128)} %mx_ref.1), slice={[0:32], [15:16], [0:512]} | slice | bytes 131072 | tf_op jit(solution)/shard_map/slice | solution.py:335
  4.5 0.0 copy-start.5
  4.5 3.8 %collective-permute-start.1 = (f32[32,512]{1,0:T(8,128)S(1)}, f32[32,512]{1,0:T(8,128)S(1)}, u32[]{:S(2)}, u32[]{:S(2)}) collective-permute-start(f32[32,512]{1,0:T(8,128)S(1)} %bitcast.9), channel_id=1, source_target_pairs={{0,2},{2,4},{4,6},{6,8},{8,10},{10,12},{12,14},{1,3},{3,5},{5,7},{... | collective-permute-start | bytes 196616 | tf_op jit(solution)/shard_map/ppermute | solution.py:324
  8.3 0.0 copy-done.5
  8.4 0.0 collective-permute-done.edge_ref
  8.4 6.6 %forward.1 = (f32[16,32,512]{2,1,0:T(8,128)}, f32[16,32,512]{2,1,0:T(8,128)}, f32[8,5,16,128]{3,2,1,0:T(8,128)}, f32[32,16,512]{2,1,0:T(8,128)}, f32[32,16,512]{...) custom-call(f32[1,128]{1,0:T(1,128)S(1)} %pad_bitcast_fusion.table_ref, s32[32,16,512]{2,1,0:T(8,128)} %material_ref.1, ...), custom_call_target="tpu_custom_call" | custom-call | flops 15728640 | bytes 10485760 | tf_op jit(solution)/shard_map/forward/pallas_call | solution.py:347
  15.0 0.0 collective-permute-done.1.edge_ref
  15.0 7.7 %all-to-all-start = ((f32[8,5,16,128]{3,2,1,0:T(8,128)}), f32[8,5,16,128]{3,2,1,0:T(8,128)S(1)}, u32[]{:S(2)}, u32[]{:S(2)}) async-start(f32[8,5,16,128]{3,2,1,0:T(8,128)} %get-tuple-element.34), calls=%async_computation | async-start | bytes 655360 | tf_op jit(solution)/shard_map/all_to_all | solution.py:380
  22.7 0.1 x_edge.1
  22.7 1.6 %collective-permute-start.2 = (f32[5,16,512]{2,1,0:T(8,128)S(1)}, f32[5,16,512]{2,1,0:T(8,128)S(1)}, u32[]{:S(2)}, u32[]{:S(2)}) collective-permute-start(f32[5,16,512]{2,1,0:T(8,128)S(1)} %get-tuple-element.31.own_ref), channel_id=1, source_target_pairs={{0,16},{16,0},{32,48},{48,32},{64,80},{80,64},{96,112},{112,96},{1... | collective-permute-start | bytes 491528 | tf_op jit(solution)/shard_map/ppermute | solution.py:275
  24.3 0.1 add_convert_fusion.low_ref
  24.4 3.8 %collective-permute-done.2.other_ref = f32[5,16,512]{2,1,0:T(8,128)S(1)} collective-permute-done((f32[5,16,512]{2,1,0:T(8,128)S(1)}, f32[5,16,512]{2,1,0:T(8,128)S(1)}, u32[]{:S(2)}, u32[]{:S(2)}) %collective-permute-start.2) | collective-permute-done | bytes 163872 | tf_op jit(solution)/shard_map/ppermute | solution.py:275
  28.1 0.6 x_merge.3
  28.7 2.8 %collective-permute-start.3 = (f32[5,16,512]{2,1,0:T(8,128)S(1)}, f32[5,16,512]{2,1,0:T(8,128)S(1)}, u32[]{:S(2)}, u32[]{:S(2)}) collective-permute-start(f32[5,16,512]{2,1,0:T(8,128)S(1)} %get-tuple-element.33.own_ref), channel_id=1, source_target_pairs={{0,48},{16,32},{32,16},{48,0},{64,112},{80,96},{96,80},{112,64},{1... | collective-permute-start | bytes 491528 | tf_op jit(solution)/shard_map/ppermute | solution.py:275
  31.6 2.2 %all-to-all-done.blocks_ref = f32[8,5,16,128]{3,2,1,0:T(8,128)S(1)} async-done(((f32[8,5,16,128]{3,2,1,0:T(8,128)}), f32[8,5,16,128]{3,2,1,0:T(8,128)S(1)}, u32[]{:S(2)}, u32[]{:S(2)}) %all-to-all-start) | async-done | bytes 327712 | tf_op jit(solution)/shard_map/all_to_all | solution.py:380
  33.8 0.8 %y_reduced.1._ = f32[8,2,16,128]{3,2,1,0:T(8,128)} custom-call(f32[8,5,16,128]{3,2,1,0:T(8,128)S(1)} %all-to-all-done.blocks_ref), custom_call_target="tpu_custom_call" | custom-call | flops 327680 | bytes 458752 | tf_op jit(solution)/shard_map/y_reduced/pallas_call | solution.py:393
  34.5 0.8 %collective-permute-done.3.other_ref = f32[5,16,512]{2,1,0:T(8,128)S(1)} collective-permute-done((f32[5,16,512]{2,1,0:T(8,128)S(1)}, f32[5,16,512]{2,1,0:T(8,128)S(1)}, u32[]{:S(2)}, u32[]{:S(2)}) %collective-permute-start.3) | collective-permute-done | bytes 163872 | tf_op jit(solution)/shard_map/ppermute | solution.py:275
  35.4 7.2 %all-to-all-start.1 = ((f32[8,2,16,128]{3,2,1,0:T(8,128)}), f32[8,2,16,128]{3,2,1,0:T(8,128)S(1)}, u32[]{:S(2)}, u32[]{:S(2)}) async-start(f32[8,2,16,128]{3,2,1,0:T(8,128)} %y_reduced.1._), calls=%async_computation.1 | async-start | bytes 262144 | tf_op jit(solution)/shard_map/all_to_all | solution.py:414
  42.6 0.6 x_merge.4
  43.1 1.7 %collective-permute-start.4 = (f32[5,16,512]{2,1,0:T(8,128)S(1)}, f32[5,16,512]{2,1,0:T(8,128)S(1)}, u32[]{:S(2)}, u32[]{:S(2)}) collective-permute-start(f32[5,16,512]{2,1,0:T(8,128)S(1)} %get-tuple-element.42.own_ref), channel_id=1, source_target_pairs={{0,64},{16,80},{32,96},{48,112},{64,0},{80,16},{96,32},{112,48},{1... | collective-permute-start | bytes 491528 | tf_op jit(solution)/shard_map/ppermute | solution.py:275
  44.8 3.7 %collective-permute-done.4.other_ref = f32[5,16,512]{2,1,0:T(8,128)S(1)} collective-permute-done((f32[5,16,512]{2,1,0:T(8,128)S(1)}, f32[5,16,512]{2,1,0:T(8,128)S(1)}, u32[]{:S(2)}, u32[]{:S(2)}) %collective-permute-start.4) | collective-permute-done | bytes 163872 | tf_op jit(solution)/shard_map/ppermute | solution.py:275
  48.6 0.0 copy-start
  48.6 0.6 x_merge.5
  49.2 3.1 %collective-permute-start.5 = (f32[2,16,512]{2,1,0:T(8,128)S(1)}, f32[2,16,512]{2,1,0:T(8,128)S(1)}, u32[]{:S(2)}, u32[]{:S(2)}) collective-permute-start(f32[2,16,512]{2,1,0:T(8,128)S(1)} %get-tuple-element.44._.side_ref), channel_id=1, source_target_pairs={{0,192},{16,208},{32,224},{48,240},{64,128},{80,144},{96,160},{112... | collective-permute-start | bytes 196616 | tf_op jit(solution)/shard_map/ppermute | solution.py:275
  52.3 0.0 copy-done
  52.3 1.6 %load.2 = (f32[16,32,512]{2,1,0:T(8,128)S(1)}, f32[16,32,512]{2,1,0:T(8,128)S(1)}) custom-call(f32[16,32,512]{2,1,0:T(8,128)} %get-tuple-element.25.t_ref, f32[16,32,512]{2,1,0:T(8,128)} %get-tuple-element.26.drive_ref, f32[8,2,16,128]{3,2,1,0:T(8,128)S(1)} %copy-done), custom_call_target="tpu_custom_call" | custom-call | flops 262144 | bytes 4194304 | tf_op jit(solution)/shard_map/load/pallas_call | solution.py:311
  53.8 1.6 %load.3 = (f32[32,16,512]{2,1,0:T(8,128)S(1)}, f32[32,16,512]{2,1,0:T(8,128)S(1)}) custom-call(f32[32,16,512]{2,1,0:T(8,128)} %get-tuple-element.38.t_ref, f32[32,16,512]{2,1,0:T(8,128)} %get-tuple-element.39.drive_ref, f32[2,16,512]{2,1,0:T(8,128)S(1)} %get-tuple-element.44._.side_ref), custom_call_target="tpu_custom_call" | custom-call | flops 262144 | bytes 4194304 | tf_op jit(solution)/shard_map/load/pallas_call | solution.py:311
  55.4 0.0 copy-start.1
  55.4 1.0 %copy-done.1 = f32[32,16,512]{2,1,0:T(8,128)} copy-done((f32[32,16,512]{2,1,0:T(8,128)}, f32[32,16,512]{2,1,0:T(8,128)S(1)}, u32[]{:S(2)}) %copy-start.1) | copy-done | bytes 1048600
  56.4 0.0 copy-start.3
  56.4 1.0 %copy-done.3 = f32[32,16,512]{2,1,0:T(8,128)} copy-done((f32[32,16,512]{2,1,0:T(8,128)}, f32[32,16,512]{2,1,0:T(8,128)S(1)}, u32[]{:S(2)}) %copy-start.3) | copy-done | bytes 1048600
  57.4 0.0 all-to-all-done.1.ends_ref
  57.4 0.0 copy-start.2
  57.4 0.0 copy-start.4
  57.4 2.0 %y_back.1 = f32[32,16,512]{2,1,0:T(8,128)} custom-call(f32[16,32,512]{2,1,0:T(8,128)S(1)} %get-tuple-element.36.t_ref, f32[16,32,512]{2,1,0:T(8,128)S(1)} %get-tuple-element.37.drive_ref, f32[8,2,16,128]{3,2,1,0:T(8,128)S(1)} %all-to-all-done.1.ends_ref), custom_call_target="tpu_custom_call" | custom-call | flops 1310720 | bytes 3145728 | tf_op jit(solution)/shard_map/y_back/pallas_call | solution.py:425
  59.3 0.0 collective-permute-done.5.other_ref
  59.4 0.0 copy-done.2
  59.4 0.0 copy-done.4
  59.4 1.8 %x_back.1 = f32[32,16,512]{2,1,0:T(8,128)} custom-call(s32[4]{0:T(128)S(1)} %add_convert_fusion.low_ref, f32[32,16,512]{2,1,0:T(8,128)S(1)} %copy-done.2, f32[32,16,512]{2,1,0:T(8,128)S(1)} %copy-done.4, f32[13,16,512]{2,1,0:T(8,128)S(1)} %get-tuple-element.47.kept_ref, f32[2,16,512]{2,1,0:T(8,128)S(1)} %get-tuple-element.44._.side_ref, ...), custom_call_target="tpu_custom_call" | custom-call | flops 1310720 | bytes 3145728 | tf_op jit(solution)/shard_map/x_back/pallas_call | solution.py:416
  (2 shorter events, 0.0 us)
Async XLA Ops:
  1.6 6.8 %collective-permute-start = (f32[32,16,128]{2,1,0:T(8,128)S(1)}, f32[32,16,128]{2,1,0:T(8,128)S(1)}, u32[]{:S(2)}, u32[]{:S(2)}) collective-permute-start(f32[32,16,128]{2,1,0:T(8,128)S(1)} %slice.6), channel_id=1, source_target_pairs={{0,1},{2,3},{4,5},{6,7},{8,9},{10,11},{12,13},{14,15},{16,17},{18,... | collective-permute-start | bytes 786440 | tf_op jit(solution)/shard_map/ppermute | solution.py:324
  4.5 3.8 %copy-start.5 = (f32[16]{0:T(128)S(1)}, f32[16]{0:T(128)}, u32[]{:S(2)}) copy-start(f32[16]{0:T(128)} %param.13) | copy-start | bytes 196
  4.5 10.5 %collective-permute-start.1 = (f32[32,512]{1,0:T(8,128)S(1)}, f32[32,512]{1,0:T(8,128)S(1)}, u32[]{:S(2)}, u32[]{:S(2)}) collective-permute-start(f32[32,512]{1,0:T(8,128)S(1)} %bitcast.9), channel_id=1, source_target_pairs={{0,2},{2,4},{4,6},{6,8},{8,10},{10,12},{12,14},{1,3},{3,5},{5,7},{... | collective-permute-start | bytes 196616 | tf_op jit(solution)/shard_map/ppermute | solution.py:324
  15.0 18.8 %all-to-all-start = ((f32[8,5,16,128]{3,2,1,0:T(8,128)}), f32[8,5,16,128]{3,2,1,0:T(8,128)S(1)}, u32[]{:S(2)}, u32[]{:S(2)}) async-start(f32[8,5,16,128]{3,2,1,0:T(8,128)} %get-tuple-element.34), calls=%async_computation | async-start | bytes 655360 | tf_op jit(solution)/shard_map/all_to_all | solution.py:380
  22.7 5.4 %collective-permute-start.2 = (f32[5,16,512]{2,1,0:T(8,128)S(1)}, f32[5,16,512]{2,1,0:T(8,128)S(1)}, u32[]{:S(2)}, u32[]{:S(2)}) collective-permute-start(f32[5,16,512]{2,1,0:T(8,128)S(1)} %get-tuple-element.31.own_ref), channel_id=1, source_target_pairs={{0,16},{16,0},{32,48},{48,32},{64,80},{80,64},{96,112},{112,96},{1... | collective-permute-start | bytes 491528 | tf_op jit(solution)/shard_map/ppermute | solution.py:275
  28.7 6.6 %collective-permute-start.3 = (f32[5,16,512]{2,1,0:T(8,128)S(1)}, f32[5,16,512]{2,1,0:T(8,128)S(1)}, u32[]{:S(2)}, u32[]{:S(2)}) collective-permute-start(f32[5,16,512]{2,1,0:T(8,128)S(1)} %get-tuple-element.33.own_ref), channel_id=1, source_target_pairs={{0,48},{16,32},{32,16},{48,0},{64,112},{80,96},{96,80},{112,64},{1... | collective-permute-start | bytes 491528 | tf_op jit(solution)/shard_map/ppermute | solution.py:275
  35.4 22.0 %all-to-all-start.1 = ((f32[8,2,16,128]{3,2,1,0:T(8,128)}), f32[8,2,16,128]{3,2,1,0:T(8,128)S(1)}, u32[]{:S(2)}, u32[]{:S(2)}) async-start(f32[8,2,16,128]{3,2,1,0:T(8,128)} %y_reduced.1._), calls=%async_computation.1 | async-start | bytes 262144 | tf_op jit(solution)/shard_map/all_to_all | solution.py:414
  43.1 5.4 %collective-permute-start.4 = (f32[5,16,512]{2,1,0:T(8,128)S(1)}, f32[5,16,512]{2,1,0:T(8,128)S(1)}, u32[]{:S(2)}, u32[]{:S(2)}) collective-permute-start(f32[5,16,512]{2,1,0:T(8,128)S(1)} %get-tuple-element.42.own_ref), channel_id=1, source_target_pairs={{0,64},{16,80},{32,96},{48,112},{64,0},{80,16},{96,32},{112,48},{1... | collective-permute-start | bytes 491528 | tf_op jit(solution)/shard_map/ppermute | solution.py:275
  48.6 3.7 %copy-start = (f32[8,2,16,128]{3,2,1,0:T(8,128)S(1)}, f32[8,2,16,128]{3,2,1,0:T(8,128)}, u32[]{:S(2)}) copy-start(f32[8,2,16,128]{3,2,1,0:T(8,128)} %y_reduced.1._) | copy-start | bytes 393220
  49.2 10.2 %collective-permute-start.5 = (f32[2,16,512]{2,1,0:T(8,128)S(1)}, f32[2,16,512]{2,1,0:T(8,128)S(1)}, u32[]{:S(2)}, u32[]{:S(2)}) collective-permute-start(f32[2,16,512]{2,1,0:T(8,128)S(1)} %get-tuple-element.44._.side_ref), channel_id=1, source_target_pairs={{0,192},{16,208},{32,224},{48,240},{64,128},{80,144},{96,160},{112... | collective-permute-start | bytes 196616 | tf_op jit(solution)/shard_map/ppermute | solution.py:275
  55.4 1.0 %copy-start.1 = (f32[32,16,512]{2,1,0:T(8,128)}, f32[32,16,512]{2,1,0:T(8,128)S(1)}, u32[]{:S(2)}) copy-start(f32[32,16,512]{2,1,0:T(8,128)S(1)} %get-tuple-element.45.t_ref) | copy-start | bytes 3145732
  56.4 1.0 %copy-start.3 = (f32[32,16,512]{2,1,0:T(8,128)}, f32[32,16,512]{2,1,0:T(8,128)S(1)}, u32[]{:S(2)}) copy-start(f32[32,16,512]{2,1,0:T(8,128)S(1)} %get-tuple-element.46.drive_ref) | copy-start | bytes 3145732
  57.4 2.0 %copy-start.2 = (f32[32,16,512]{2,1,0:T(8,128)S(1)}, f32[32,16,512]{2,1,0:T(8,128)}, u32[]{:S(2)}) copy-start(f32[32,16,512]{2,1,0:T(8,128)} %copy-done.1) | copy-start | bytes 3145732
  57.4 2.0 %copy-start.4 = (f32[32,16,512]{2,1,0:T(8,128)S(1)}, f32[32,16,512]{2,1,0:T(8,128)}, u32[]{:S(2)}) copy-start(f32[32,16,512]{2,1,0:T(8,128)} %copy-done.3) | copy-start | bytes 3145732

commit v3 on v2

v3 whole, which is shorter than its diff:
```python
import functools

import jax
import jax.numpy as jnp
from jax import lax
from jax.experimental import pallas as pl
from jax.experimental.pallas import tpu as pltpu
from jax.sharding import PartitionSpec as P

ground_scale = 1.0 / 1600.0
drive_scale = 1.0 / 40.0
lane = 128
rows = 8
f32 = jnp.float32
vmem_spec = pl.BlockSpec(memory_space=pltpu.VMEM)
smem_spec = pl.BlockSpec(memory_space=pltpu.SMEM)
hbm_spec = pl.BlockSpec(memory_space=pltpu.HBM)


def inverse(x):
    return pltpu.reciprocal(x, approx=True)


def eliminate(state, ground, drive):
    link, left, here, left_drive, here_drive = state
    t = inverse(link + here + 1.0)
    next_link = link * t
    return (
        next_link,
        left + next_link * here,
        ground + here * t,
        left_drive + next_link * here_drive,
        drive + here_drive * t,
    ), t


def close_block(state, rim):
    link, left, here, left_drive, here_drive = state
    return (
        link,
        left,
        here,
        left_drive + link * rim,
        here_drive - (link + here + 1.0) * rim,
    )


def forward_kernel(
    table_hbm, material_hbm, ex_hbm, ez_hbm, mx_hbm, my_hbm, mz_hbm,
    yt_ref, ydrive_ref, yreduced_ref, xt_hbm, xdrive_hbm, xreduced_ref,
    yt_edge_ref, my_edge_ref, xt_edge_ref, mx_edge_ref,
    table_s, material_s, ex_s, ez_s, mx_s, my_s, mz_s, xt_s, xjs_s, ground_s, ydrive_s, xdrive_s, turn_s,
    state_s, last_my_s, table_sem, sems, out_sems,
):
    xs, ys, zs = material_s.shape
    tiles = zs // lane
    chunks = xs // rows
    flat = (rows * ys, lane)
    cube = (rows, ys, lane)
    arrays = (
        (material_hbm, material_s), (my_hbm, my_s), (mz_hbm, mz_s),
        (ex_hbm, ex_s), (ez_hbm, ez_s), (mx_hbm, mx_s),
    )

    def chunk_copies(c):
        part = pl.ds(pl.multiple_of(c * rows, rows), rows)
        return [
            pltpu.make_async_copy(source.at[part], target.at[part], sems.at[a, c])
            for a, (source, target) in enumerate(arrays)
        ]

    def chunk_stores(c):
        part = pl.ds(pl.multiple_of(c * rows, rows), rows)
        return [
            pltpu.make_async_copy(source.at[part], target.at[part], out_sems.at[a, c])
            for a, (source, target) in enumerate(((xt_s, xt_hbm), (xjs_s, xdrive_hbm)))
        ]

    table_copy = pltpu.make_async_copy(table_hbm, table_s, table_sem)
    table_copy.start()
    for c in range(chunks):
        for copy in chunk_copies(c):
            copy.start()
    lanes = lax.broadcasted_iota(jnp.int32, flat, 1)
    first_lane = lanes == 0
    first_y = lax.broadcasted_iota(jnp.int32, cube, 1) == 0
    edge_lanes = lax.broadcasted_iota(jnp.int32, (rows, lane), 1)
    my_edge_ref[...] = jnp.zeros_like(my_edge_ref)
    state_s[...] = jnp.zeros_like(state_s)
    last_my_s[...] = jnp.zeros_like(last_my_s)
    table_copy.wait()
    table = jnp.zeros((1, lane), f32)
    for m in range(table_s.shape[0]):
        table = jnp.where(lax.broadcasted_iota(jnp.int32, (1, lane), 1) == m, table_s[m], table)
    table = table * ground_scale

    def chunk(c, _):
        for copy in chunk_copies(c):
            copy.wait()
        part = pl.ds(pl.multiple_of(c * rows, rows), rows)
        before = jnp.zeros(flat, f32)
        for k in range(tiles):
            cut = pl.ds(k * lane, lane)
            ground = jnp.take_along_axis(
                jnp.broadcast_to(table, flat), material_s[part, :, cut].reshape(flat), axis=1, mode="promise_in_bounds"
            )
            my = my_s[part, :, cut]
            rolled = pltpu.roll(my.reshape(flat), 1, 1)
            my_step = my.reshape(flat) - jnp.where(first_lane, before, rolled)
            before = rolled
            mz = mz_s[part, :, cut]
            mz_step = (mz - jnp.where(first_y, 0.0, pltpu.roll(mz, 1, 1))).reshape(flat)
            mx = mx_s[part, :, cut]
            mx_step = (mx - jnp.where(first_y, 0.0, pltpu.roll(mx, 1, 1))).reshape(flat)
            my_up = (my - jnp.concatenate([last_my_s[:, cut][None], my[:-1]], axis=0)).reshape(flat)
            last_my_s[:, cut] = my[rows - 1]
            ground_s[k] = ground
            ydrive_s[k] = ground * ex_s[part, :, cut].reshape(flat) + drive_scale * (mz_step - my_step)
            xdrive_s[k] = ground * ez_s[part, :, cut].reshape(flat) + drive_scale * (my_up - mx_step)
            mx_edge_ref[part, cut] = mx_s[part, ys - 1, cut]
            if k == tiles - 1:
                turn_s[...] = my.reshape(flat)

        states = [tuple(state_s[v, :, pl.ds(k * lane, lane)] for v in range(5)) for k in range(tiles)]
        for i in range(rows):
            line = pl.ds(i * ys, ys)
            for k in range(tiles):
                cut = pl.ds(k * lane, lane)
                state, t = eliminate(states[k], ground_s[k, line, :], xdrive_s[k, line, :])
                if i == 0:
                    state = (jnp.where(c == 0, 1.0, state[0]),) + state[1:]
                states[k] = state
                xt_s[c * rows + i, :, cut] = t
                js = state[4]
                if i == rows - 1:
                    js = jnp.where(c == chunks - 1, drive_scale * last_my_s[:, cut], js)
                xjs_s[c * rows + i, :, cut] = js
                xt_edge_ref[c * rows + i, :, cut] = t[0:1]
        for k in range(tiles):
            for v in range(5):
                state_s[v, :, pl.ds(k * lane, lane)] = states[k][v]
        for copy in chunk_stores(c):
            copy.start()

        for first in range(0, tiles, 2):
            pair = (first, first + 1)
            states = [None, None]
            for j in range(ys):
                pick = pl.ds(j, rows, stride=ys)
                for n, k in enumerate(pair):
                    cut = pl.ds(k * lane, lane)
                    ground = ground_s[k, pick, :]
                    drive = ydrive_s[k, pick, :]
                    if j == 0:
                        zero = jnp.zeros_like(ground)
                        states[n] = (jnp.ones_like(ground), zero, ground, zero, drive)
                    else:
                        states[n], t = eliminate(states[n], ground, drive)
                        yt_ref[j - 1, part, cut] = t
                        if k == 0:
                            yt_edge_ref[j - 1, part, :] = t
                    if j < ys - 1:
                        ydrive_ref[j, part, cut] = states[n][4]
            for n, k in enumerate(pair):
                cut = pl.ds(k * lane, lane)
                rim = drive_scale * mz_s[part, ys - 1, cut]
                ydrive_ref[ys - 1, part, cut] = rim
                for v, value in enumerate(close_block(states[n], rim)):
                    yreduced_ref[2 * c + k // 2, v, pl.ds((k % 2) * rows, rows), :] = value
        packed = my_edge_ref[...]
        for j in range(ys):
            place = j * chunks + c
            turned = pltpu.roll(turn_s[pl.ds(j, rows, stride=ys), :], place + 1, 1)
            packed = jnp.where(edge_lanes == place, turned, packed)
        my_edge_ref[...] = packed
        return _

    lax.fori_loop(0, chunks, chunk, 0)
    rim = drive_scale * last_my_s[...]
    for v, value in enumerate(close_block(tuple(state_s[v] for v in range(5)), rim)):
        xreduced_ref[v] = value
    for c in range(chunks):
        for copy in chunk_stores(c):
            copy.wait()


def y_edge_kernel(edge_ref, t_ref, reduced_ref, drive_ref, reduced_out, drive_out):
    ys, xs, _ = t_ref.shape
    reduced_out[...] = reduced_ref[...]
    first_lane = lax.broadcasted_iota(jnp.int32, (rows, lane), 1) == 0
    for c in range(xs // rows):
        part = pl.ds(c * rows, rows)

        def rim(j, c=c):
            place = j * (xs // rows) + c
            turned = pltpu.roll(edge_ref[...], (lane - place) % lane, 1)
            return jnp.where(first_lane, drive_scale * turned, 0.0)

        here = rim(0)
        link = jnp.ones_like(here)
        left = jnp.zeros_like(here)
        for j in range(ys):
            if j > 0:
                t = t_ref[j - 1, part, :]
                link = link * t
                left = left + link * here
                here = rim(j) + here * t
            if j < ys - 1:
                drive_out[j, part, pl.ds(0, lane)] = drive_ref[j, part, pl.ds(0, lane)] + here
        reduced_out[2 * c, 3, pl.ds(0, rows), :] = reduced_ref[2 * c, 3, pl.ds(0, rows), :] + left
        reduced_out[2 * c, 4, pl.ds(0, rows), :] = reduced_ref[2 * c, 4, pl.ds(0, rows), :] + here


kept_count = 13


def x_edge_kernel(edge_ref, t_ref, reduced_ref, reduced_out, kept_ref):
    xs = t_ref.shape[0]
    ys = reduced_ref.shape[1]
    row = pl.ds(0, 1)
    here = drive_scale * edge_ref[row, :]
    link = jnp.ones_like(here)
    left = jnp.zeros_like(here)
    kept_ref[11, row, :] = here
    for i in range(1, xs):
        t = t_ref[i]
        link = link * t
        left = left + link * here
        here = drive_scale * edge_ref[pl.ds(i, 1), :] + here * t
        kept_ref[11 + i // ys, pl.ds(i % ys, 1), :] = here
    for v in range(5):
        reduced_out[v] = reduced_ref[v]
    reduced_out[3, row, :] = reduced_ref[3, row, :] + left
    reduced_out[4, row, :] = reduced_ref[4, row, :] + here


def y_reduced_kernel(blocks_ref, ends_ref):
    count = blocks_ref.shape[0]
    block = [[blocks_ref[b, v] for v in range(5)] for b in range(count)]
    here = block[0][2] + block[0][0]
    drive = block[0][4]
    kept = []
    for b in range(1, count):
        link, left, right, left_drive, right_drive = block[b]
        total = here + left
        t = inverse(total + link)
        pull = link * t
        push = drive + left_drive
        kept.append((pull, push * t))
        here = right + pull * total
        drive = right_drive + pull * push
    value = drive * inverse(here + 1.0)
    ends_ref[count - 1, 1] = value
    for b in range(count - 1, 0, -1):
        pull, push = kept[b - 1]
        value = push + pull * value
        ends_ref[b, 0] = value
        ends_ref[b - 1, 1] = value
    ends_ref[0, 0] = jnp.zeros_like(value)


def merge(low, own_ref, other_ref, kept_ref, slot):
    own = [own_ref[v] for v in range(5)]
    other = [other_ref[v] for v in range(5)]
    a = [jnp.where(low, p, q) for p, q in zip(own, other)]
    b = [jnp.where(low, q, p) for p, q in zip(own, other)]
    total = a[2] + b[1]
    t = inverse(total + a[0] + b[0])
    a_link, b_link = a[0] * t, b[0] * t
    push = a[4] + b[3]
    kept_ref[slot] = push * t
    kept_ref[slot + 1] = a_link
    kept_ref[slot + 2] = b_link
    return (
        a[0] * b_link,
        a[1] + a_link * total,
        b[2] + b_link * total,
        a[3] + a_link * push,
        b[4] + b_link * push,
    )


def is_low(level):
    return (lax.axis_index("gx") >> level) & 1 == 0


def merge_kernel(level, own_ref, other_ref, _, merged_ref, kept_ref):
    merged = merge(is_low(level), own_ref, other_ref, kept_ref, 3 * level)
    for v in range(5):
        merged_ref[v] = merged[v]


def last_merge_kernel(level, own_ref, other_ref, _, side_ref, kept_ref):
    link, left, right, left_drive, right_drive = merge(is_low(level), own_ref, other_ref, kept_ref, 3 * level)
    closed = inverse(right + link + 1.0)
    share = link * closed
    top = is_low(level + 1)
    side_ref[0] = jnp.where(top, right + link, left + share * (right + 1.0))
    side_ref[1] = jnp.where(top, right_drive, left_drive + share * right_drive)
    kept_ref[9] = closed * right_drive
    kept_ref[10] = share


def y_back_kernel(
    t_ref, drive_ref, ends_ref, xt_hbm, xdrive_hbm, out_hbm, xt_ref, xdrive_ref, turn_s, out_s, sems, load_sems
):
    loads = [
        pltpu.make_async_copy(xt_hbm, xt_ref, load_sems.at[0]),
        pltpu.make_async_copy(xdrive_hbm, xdrive_ref, load_sems.at[1]),
    ]
    for load in loads:
        load.start()
    ys, xs, zs = t_ref.shape
    copies = []
    for c in range(xs // rows):
        part = pl.ds(c * rows, rows)
        for k in range(zs // lane):
            cut = pl.ds(k * lane, lane)
            half = pl.ds((k % 2) * rows, rows)
            reach = ends_ref[2 * c + k // 2, 0, half, :]
            value = ends_ref[2 * c + k // 2, 1, half, :] + drive_ref[ys - 1, part, cut]
            parts = []
            for j in range(ys - 1):
                t = t_ref[j, part, cut]
                reach = reach * t
                parts.append((t, drive_ref[j, part, cut] * t + reach))
            turn_s[k, pl.ds(ys - 1, rows, stride=ys), :] = value
            for j in range(ys - 2, -1, -1):
                t, share = parts[j]
                value = share + t * value
                turn_s[k, pl.ds(j, rows, stride=ys), :] = value
            out_s[part, :, cut] = turn_s[k].reshape(rows, ys, lane)
        copies.append(pltpu.make_async_copy(out_s.at[part], out_hbm.at[part], sems.at[c]))
        copies[-1].start()
    for copy in copies + loads:
        copy.wait()


def x_back_kernel(t_ref, drive_ref, kept_ref, side_ref, other_ref, out_ref):
    xs, ys, zs = t_ref.shape
    top = is_low(3)
    middle = (side_ref[1] + other_ref[1]) * inverse(side_ref[0] + other_ref[0])
    before = jnp.where(top, 0.0, middle)
    here = jnp.where(top, middle, kept_ref[9] + kept_ref[10] * middle)
    for level in (2, 1, 0):
        low = is_low(level)
        middle = kept_ref[3 * level] + kept_ref[3 * level + 1] * before + kept_ref[3 * level + 2] * here
        before, here = jnp.where(low, before, middle), jnp.where(low, middle, here)
    first_y = lax.broadcasted_iota(jnp.int32, (ys, zs), 0) == 0
    reach = before
    for i in range(xs - 1):
        t = t_ref[i + 1]
        reach = reach * t
        edge = jnp.where(first_y, kept_ref[11 + i // ys, pl.ds(i % ys, 1), :], 0.0)
        out_ref[i] = (drive_ref[i] + edge) * t + reach
    value = here + drive_ref[xs - 1]
    out_ref[xs - 1] = value
    for i in range(xs - 2, -1, -1):
        value = out_ref[i] + t_ref[i + 1] * value
        out_ref[i] = value


def cost(elements, ops, arrays):
    return pl.CostEstimate(flops=elements * ops, bytes_accessed=elements * 4 * arrays, transcendentals=0)


def call(kernel, name, inputs, outs, carried=(), limit=16, work=None, scratch=()):
    specs = [spec for spec, _ in inputs] + [vmem_spec] * len(carried)
    arrays = []
    for spec, array in inputs:
        if spec is hbm_spec:
            array = pltpu.with_memory_space_constraint(array, pltpu.HBM)
        elif spec is vmem_spec:
            array = pltpu.with_memory_space_constraint(array, pltpu.VMEM)
        arrays.append(array)
    arrays += [pltpu.with_memory_space_constraint(a, pltpu.VMEM) for a in carried]
    out_specs = [spec for spec, _ in outs] + [vmem_spec] * len(carried)
    out_shape = [shape for _, shape in outs] + [pltpu.VMEM(a.shape, a.dtype) for a in carried]
    return pl.pallas_call(
        kernel,
        in_specs=specs,
        out_specs=out_specs,
        out_shape=out_shape,
        scratch_shapes=list(scratch),
        input_output_aliases={len(inputs) + n: len(outs) + n for n in range(len(carried))},
        compiler_params=pltpu.CompilerParams(vmem_limit_bytes=limit * 2**20),
        cost_estimate=work,
        name=name,
    )(*arrays)


def shift_up(x, axis):
    return lax.ppermute(x, axis, [(i, i + 1) for i in range(lax.axis_size(axis) - 1)])


def exchange(x, axis, mask):
    return lax.ppermute(x, axis, [(i, i ^ mask) for i in range(lax.axis_size(axis))])


def per_device(electric_x, electric_z, magnetic_x, magnetic_y, magnetic_z, material, perm_table):
    xs, ys, zs = material.shape
    chunks = xs // rows
    cells = xs * ys * zs
    V, H = pltpu.VMEM, pltpu.HBM
    fields = (electric_x, electric_z, magnetic_x, magnetic_y, magnetic_z)
    block = (2 * chunks, 5, 2 * rows, lane)

    y_t, y_drive, y_reduced, x_t, x_drive, x_reduced, yt_edge, my_edge, xt_edge, mx_edge = call(
        forward_kernel,
        "forward",
        [(hbm_spec, a) for a in (perm_table, material) + fields],
        [
            (vmem_spec, V((ys, xs, zs), f32)),
            (vmem_spec, V((ys, xs, zs), f32)),
            (vmem_spec, V(block, f32)),
            (hbm_spec, H((xs, ys, zs), f32)),
            (hbm_spec, H((xs, ys, zs), f32)),
            (vmem_spec, V((5, ys, zs), f32)),
            (vmem_spec, V((ys, xs, lane), f32)),
            (vmem_spec, V((rows, lane), f32)),
            (vmem_spec, V((xs, 1, zs), f32)),
            (vmem_spec, V((xs, zs), f32)),
        ],
        scratch=[pltpu.SMEM(perm_table.shape, f32), V((xs, ys, zs), jnp.int32)]
        + [V((xs, ys, zs), f32)] * 7
        + [V((zs // lane, rows * ys, lane), f32)] * 3
        + [V((rows * ys, lane), f32), V((5, ys, zs), f32), V((ys, zs), f32)]
        + [pltpu.SemaphoreType.DMA, pltpu.SemaphoreType.DMA((6, chunks)), pltpu.SemaphoreType.DMA((2, chunks))],
        limit=24,
        work=cost(cells, 60, 10),
    )

    edge_z = shift_up(my_edge, "gz")
    edge_y = shift_up(mx_edge, "gy")
    y_reduced, y_drive = pl.pallas_call(
        y_edge_kernel,
        in_specs=[vmem_spec] * 4,
        out_specs=[vmem_spec] * 2,
        out_shape=[H(block, f32), V((ys, xs, zs), f32)],
        input_output_aliases={3: 1},
        compiler_params=pltpu.CompilerParams(vmem_limit_bytes=8 * 2**20),
        cost_estimate=cost(cells // 4, 10, 3),
        name="y_edge",
    )(*(pltpu.with_memory_space_constraint(a, V) for a in (edge_z, yt_edge, y_reduced, y_drive)))
    y_reduced, edge_y = lax.optimization_barrier((y_reduced, edge_y))
    y_blocks = lax.all_to_all(y_reduced, "gy", 0, 0, tiled=True)

    x_reduced, kept = call(
        x_edge_kernel,
        "x_edge",
        [(vmem_spec, a) for a in (edge_y, xt_edge, x_reduced)],
        [(vmem_spec, V((5, ys, zs), f32)), (vmem_spec, V((kept_count, ys, zs), f32))],
        limit=8,
        work=cost(cells // ys, 10, 3),
    )

    (y_ends,) = pl.pallas_call(
        y_reduced_kernel,
        in_specs=[vmem_spec],
        out_specs=[vmem_spec],
        out_shape=[H((2 * chunks, 2, 2 * rows, lane), f32)],
        compiler_params=pltpu.CompilerParams(vmem_limit_bytes=8 * 2**20),
        cost_estimate=cost(y_blocks.size // 5, 20, 7),
        name="y_reduced",
    )(y_blocks)

    own = x_reduced
    for level, mask in enumerate((1, 3, 4)):
        other = exchange(own, "gx", mask)
        if level == 1:
            other, y_ends = lax.optimization_barrier((other, y_ends))
        kernel = functools.partial(merge_kernel if level < 2 else last_merge_kernel, level)

        def body(own_ref, other_ref, kept_in, *refs, kernel=kernel):
            merged_ref, kept_ref = refs[2], refs[3]
            kernel(own_ref, other_ref, kept_in, merged_ref, kept_ref)

        own, kept, y_t, y_drive = call(
            body,
            "x_merge",
            [(vmem_spec, own), (vmem_spec, other)],
            [(vmem_spec, V((5 if level < 2 else 2, ys, zs), f32))],
            carried=(kept, y_t, y_drive),
            limit=8,
            work=cost(own.size, 10, 3),
        )
    side_other = exchange(own, "gx", 12)
    y_ends = lax.all_to_all(y_ends, "gy", 0, 0, tiled=True)

    electric_x_half, x_t, x_drive = call(
        y_back_kernel,
        "y_back",
        [(vmem_spec, a) for a in (y_t, y_drive, y_ends)] + [(hbm_spec, a) for a in (x_t, x_drive)],
        [(hbm_spec, H((xs, ys, zs), f32))] + [(vmem_spec, V((xs, ys, zs), f32))] * 2,
        scratch=[V((zs // lane, rows * ys, lane), f32), V((xs, ys, zs), f32)]
        + [pltpu.SemaphoreType.DMA((chunks,)), pltpu.SemaphoreType.DMA((2,))],
        work=cost(cells, 5, 3),
    )
    (electric_z_half,) = call(
        x_back_kernel,
        "x_back",
        [(vmem_spec, a) for a in (x_t, x_drive, kept, own, side_other)],
        [(vmem_spec, H((xs, ys, zs), f32))],
        work=cost(cells, 5, 3),
    )
    return (electric_x_half, electric_z_half)


def solution(mesh):
    field = P("gx", "gy", "gz")
    return jax.shard_map(
        per_device,
        mesh=mesh,
        in_specs=(field,) * 6 + (P(),),
        out_specs=(field, field),
        check_vma=False,
    )
```

time: 61.7 us -> 53.5 us (0.87)
  Pallas kernels: 16.1 us -> 9.99 us
  local copies, waits for them, and re-layouts: 4.07 us -> 0 us
  waiting for transfers between devices: 10.5 us -> 11.9 us
  starting transfers between devices: 29.7 us -> 30.6 us
    pallas_call x10 -> x9, Pallas kernels: 16.1 us -> 9.99 us  [the longest x7 8.31 us: call(): pl.pallas_call(kernel, in_specs=specs, out_specs=out_specs, out_shape=out...]
    slice x2 -> x0, local copies, waits for them, and re-layouts: 2.08 us -> none  [the longest x1 1.11 us: per_device(): edge_y = shift_up(magnetic_x[:, ys - 1], 'gy')]
    unnamed x13 -> x0, local copies, waits for them, and re-layouts: 1.99 us -> none
    all_to_all x1, starting transfers between devices: 7.68 us -> 8.91 us  [per_device(): y_blocks = lax.all_to_all(y_reduced, 'gy', 0, 0, tiled=True)]
    ppermute x2, waiting for transfers between devices: 0.01 us -> 0.81 us  [shift_up(): lax.ppermute(x, axis, [(i, i + 1) for i in range(lax.axis_size(axis) - 1)])]
  transfers between devices with their start and end apart: 8 -> 8, of which waited for: 4 -> 6; matrix products, arithmetic and copies ran while one was open for 2% -> 0% of each run, Pallas kernels for 23% -> 7%
where the time goes in v3:
time: 53.5 us; the launch traced here: 53.1 us
  starting transfers between devices  30.6 us (57%)
  waiting for transfers between devices  11.9 us (22%)
  Pallas kernels  9.99 us (19%)
  between operations  0.68 us (1%)
    ppermute x4, starting transfers between devices, exchange(): lax.ppermute(x, axis, [(i, i ^ mask) for i in range(lax.axis_size(axis))])  9.18 us
    all_to_all x1, starting transfers between devices, per_device(): y_blocks = lax.all_to_all(y_reduced, 'gy', 0, 0, tiled=True)  8.91 us
    ppermute x4, waiting for transfers between devices, exchange(): lax.ppermute(x, axis, [(i, i ^ mask) for i in range(lax.axis_size(axis))])  8.33 us
    pallas_call x7, Pallas kernels, call(): pl.pallas_call(kernel, in_specs=specs, out_specs=out_specs, out_shape=out...  8.31 us
    all_to_all x1, starting transfers between devices, per_device(): y_ends = lax.all_to_all(y_ends, 'gy', 0, 0, tiled=True)  7.21 us
    ppermute x2, starting transfers between devices, shift_up(): lax.ppermute(x, axis, [(i, i + 1) for i in range(lax.axis_size(axis) - 1)])  5.28 us
    all_to_all x1, waiting for transfers between devices, per_device(): y_blocks = lax.all_to_all(y_reduced, 'gy', 0, 0, tiled=True)  2.73 us
  transfers between devices with their start and end apart: 8, of which 6 were waited for; matrix products, arithmetic and copies ran while one was open for 0% of the time, Pallas kernels for 7%

profile of v3, /device:TPU:32, one launch (start us, length us, event | category | flops | bytes accessed | tf_op | source)
XLA Modules:
  0.0 53.1 jit_solution(15867891143967227577)
XLA Ops:
  0.6 4.9 %forward.1 = (f32[16,32,512]{2,1,0:T(8,128)S(1)}, f32[16,32,512]{2,1,0:T(8,128)S(1)}, f32[8,5,16,128]{3,2,1,0:T(8,128)S(1)}, f32[32,16,512]{2,1,0:T(8,128)}, f32...) custom-call(f32[16]{0:T(128)} %table_hbm.1, ...), custom_call_target="tpu_custom_call" | custom-call | flops 15728640 | bytes 10485760 | tf_op jit(solution)/shard_map/forward/pallas_call | solution.py:379
  5.5 3.8 %collective-permute-start.1 = (f32[32,512]{1,0:T(8,128)S(1)}, f32[32,512]{1,0:T(8,128)S(1)}, u32[]{:S(2)}, u32[]{:S(2)}) collective-permute-start(f32[32,512]{1,0:T(8,128)S(1)} %get-tuple-element.40), channel_id=1, source_target_pairs={{0,2},{2,4},{4,6},{6,8},{8,10},{10,12},{12,14},{1,3},{3,5},{5,7},{... | collective-permute-start | bytes 196616 | tf_op jit(solution)/shard_map/ppermute | solution.py:393
  9.3 1.5 %collective-permute-start = (f32[8,128]{1,0:T(8,128)S(1)}, f32[8,128]{1,0:T(8,128)S(1)}, u32[]{:S(2)}, u32[]{:S(2)}) collective-permute-start(f32[8,128]{1,0:T(8,128)S(1)} %get-tuple-element.35), channel_id=1, source_target_pairs={{0,1},{2,3},{4,5},{6,7},{8,9},{10,11},{12,13},{14,15},{16,17},{18,... | collective-permute-start | bytes 12296 | tf_op jit(solution)/shard_map/ppermute | solution.py:393
  10.8 0.8 %collective-permute-done.edge_ref = f32[8,128]{1,0:T(8,128)S(1)} collective-permute-done((f32[8,128]{1,0:T(8,128)S(1)}, f32[8,128]{1,0:T(8,128)S(1)}, u32[]{:S(2)}, u32[]{:S(2)}) %collective-permute-start) | collective-permute-done | bytes 4128 | tf_op jit(solution)/shard_map/ppermute | solution.py:393
  11.6 0.9 %y_edge.1 = (f32[8,5,16,128]{3,2,1,0:T(8,128)}, f32[16,32,512]{2,1,0:T(8,128)S(1)}) custom-call(f32[8,128]{1,0:T(8,128)S(1)} %collective-permute-done.edge_ref, f32[16,32,128]{2,1,0:T(8,128)S(1)} %get-tuple-element.36.t_ref, f32[8,5,16,128]{3,2,1,0:T(8,128)S(1)} %get-tuple-element.37.reduced_ref, ...), custom_call_target="tpu_custom_call", output_to_operand_aliasing={{1}: (3, {})} | custom-call | flops 655360 | bytes 786432 | tf_op jit(solution)/shard_map/y_edge/pallas_call | solution.py:435
  12.5 0.0 collective-permute-done.1.edge_ref
  12.5 8.9 %all-to-all-start = ((f32[8,5,16,128]{3,2,1,0:T(8,128)}), f32[8,5,16,128]{3,2,1,0:T(8,128)S(1)}, u32[]{:S(2)}, u32[]{:S(2)}) async-start(f32[8,5,16,128]{3,2,1,0:T(8,128)} %get-tuple-element.49), calls=%async_computation | async-start | bytes 655360 | tf_op jit(solution)/shard_map/all_to_all | solution.py:446
  21.5 0.1 x_edge.1
  21.5 1.6 %collective-permute-start.2 = (f32[5,16,512]{2,1,0:T(8,128)S(1)}, f32[5,16,512]{2,1,0:T(8,128)S(1)}, u32[]{:S(2)}, u32[]{:S(2)}) collective-permute-start(f32[5,16,512]{2,1,0:T(8,128)S(1)} %get-tuple-element.44.own_ref), channel_id=1, source_target_pairs={{0,16},{16,0},{32,48},{48,32},{64,80},{80,64},{96,112},{112,96},{1... | collective-permute-start | bytes 491528 | tf_op jit(solution)/shard_map/ppermute | solution.py:397
  23.1 3.8 %collective-permute-done.2.other_ref = f32[5,16,512]{2,1,0:T(8,128)S(1)} collective-permute-done((f32[5,16,512]{2,1,0:T(8,128)S(1)}, f32[5,16,512]{2,1,0:T(8,128)S(1)}, u32[]{:S(2)}, u32[]{:S(2)}) %collective-permute-start.2) | collective-permute-done | bytes 163872 | tf_op jit(solution)/shard_map/ppermute | solution.py:397
  27.0 2.8 %collective-permute-start.3 = (f32[5,16,512]{2,1,0:T(8,128)S(1)}, f32[5,16,512]{2,1,0:T(8,128)S(1)}, u32[]{:S(2)}, u32[]{:S(2)}) collective-permute-start(f32[5,16,512]{2,1,0:T(8,128)S(1)} %get-tuple-element.48.own_ref), channel_id=1, source_target_pairs={{0,48},{16,32},{32,16},{48,0},{64,112},{80,96},{96,80},{112,64},{1... | collective-permute-start | bytes 491528 | tf_op jit(solution)/shard_map/ppermute | solution.py:397
  29.8 2.7 %all-to-all-done.blocks_ref = f32[8,5,16,128]{3,2,1,0:T(8,128)S(1)} async-done(((f32[8,5,16,128]{3,2,1,0:T(8,128)}), f32[8,5,16,128]{3,2,1,0:T(8,128)S(1)}, u32[]{:S(2)}, u32[]{:S(2)}) %all-to-all-start) | async-done | bytes 327712 | tf_op jit(solution)/shard_map/all_to_all | solution.py:446
  32.6 0.8 %y_reduced.1 = f32[8,2,16,128]{3,2,1,0:T(8,128)} custom-call(f32[8,5,16,128]{3,2,1,0:T(8,128)S(1)} %all-to-all-done.blocks_ref), custom_call_target="tpu_custom_call" | custom-call | flops 327680 | bytes 458752 | tf_op jit(solution)/shard_map/y_reduced/pallas_call | solution.py:457
  33.3 0.3 collective-permute-done.3.other_ref
  33.6 7.2 %all-to-all-start.1 = ((f32[8,2,16,128]{3,2,1,0:T(8,128)}), f32[8,2,16,128]{3,2,1,0:T(8,128)S(1)}, u32[]{:S(2)}, u32[]{:S(2)}) async-start(f32[8,2,16,128]{3,2,1,0:T(8,128)} %y_reduced.1), calls=%async_computation.1 | async-start | bytes 262144 | tf_op jit(solution)/shard_map/all_to_all | solution.py:488
  40.9 1.7 %collective-permute-start.4 = (f32[5,16,512]{2,1,0:T(8,128)S(1)}, f32[5,16,512]{2,1,0:T(8,128)S(1)}, u32[]{:S(2)}, u32[]{:S(2)}) collective-permute-start(f32[5,16,512]{2,1,0:T(8,128)S(1)} %get-tuple-element.54.own_ref), channel_id=1, source_target_pairs={{0,64},{16,80},{32,96},{48,112},{64,0},{80,16},{96,32},{112,48},{1... | collective-permute-start | bytes 491528 | tf_op jit(solution)/shard_map/ppermute | solution.py:397
  42.5 3.7 %collective-permute-done.4.other_ref = f32[5,16,512]{2,1,0:T(8,128)S(1)} collective-permute-done((f32[5,16,512]{2,1,0:T(8,128)S(1)}, f32[5,16,512]{2,1,0:T(8,128)S(1)}, u32[]{:S(2)}, u32[]{:S(2)}) %collective-permute-start.4) | collective-permute-done | bytes 163872 | tf_op jit(solution)/shard_map/ppermute | solution.py:397
  46.3 0.1 x_merge.5
  46.3 3.1 %collective-permute-start.5 = (f32[2,16,512]{2,1,0:T(8,128)S(1)}, f32[2,16,512]{2,1,0:T(8,128)S(1)}, u32[]{:S(2)}, u32[]{:S(2)}) collective-permute-start(f32[2,16,512]{2,1,0:T(8,128)S(1)} %get-tuple-element.67.side_ref), channel_id=1, source_target_pairs={{0,192},{16,208},{32,224},{48,240},{64,128},{80,144},{96,160},{112... | collective-permute-start | bytes 196616 | tf_op jit(solution)/shard_map/ppermute | solution.py:397
  49.4 0.0 all-to-all-done.1.ends_ref
  49.4 2.0 %y_back.1 = (f32[32,16,512]{2,1,0:T(8,128)}, f32[32,16,512]{2,1,0:T(8,128)S(1)}, f32[32,16,512]{2,1,0:T(8,128)S(1)}) custom-call(f32[16,32,512]{2,1,0:T(8,128)S(1)} %get-tuple-element.58.t_ref, f32[16,32,512]{2,1,0:T(8,128)S(1)} %get-tuple-element.59.drive_ref, f32[8,2,16,128]{3,2,1,0:T(8,128)S(1)} %all-to-all-done.1.ends_ref, ...), custom_call_target="tpu_custom_call" | custom-call | flops 1310720 | bytes 3145728 | tf_op jit(solution)/shard_map/y_back/pallas_call | solution.py:379
  51.4 0.5 collective-permute-done.5.other_ref
  51.9 1.2 %x_back.1 = f32[32,16,512]{2,1,0:T(8,128)} custom-call(f32[32,16,512]{2,1,0:T(8,128)S(1)} %get-tuple-element.64.t_ref, f32[32,16,512]{2,1,0:T(8,128)S(1)} %get-tuple-element.65.drive_ref, f32[13,16,512]{2,1,0:T(8,128)S(1)} %get-tuple-element.66.kept_ref, f32[2,16,512]{2,1,0:T(8,128)S(1)} %get-tuple-element.67.side_ref, ...), custom_call_target="tpu_custom_call" | custom-call | flops 1310720 | bytes 3145728 | tf_op jit(solution)/shard_map/x_back/pallas_call | solution.py:379
  (2 shorter events, 0.1 us)
Async XLA Ops:
  5.5 7.0 %collective-permute-start.1 = (f32[32,512]{1,0:T(8,128)S(1)}, f32[32,512]{1,0:T(8,128)S(1)}, u32[]{:S(2)}, u32[]{:S(2)}) collective-permute-start(f32[32,512]{1,0:T(8,128)S(1)} %get-tuple-element.40), channel_id=1, source_target_pairs={{0,2},{2,4},{4,6},{6,8},{8,10},{10,12},{12,14},{1,3},{3,5},{5,7},{... | collective-permute-start | bytes 196616 | tf_op jit(solution)/shard_map/ppermute | solution.py:393
  9.3 2.3 %collective-permute-start = (f32[8,128]{1,0:T(8,128)S(1)}, f32[8,128]{1,0:T(8,128)S(1)}, u32[]{:S(2)}, u32[]{:S(2)}) collective-permute-start(f32[8,128]{1,0:T(8,128)S(1)} %get-tuple-element.35), channel_id=1, source_target_pairs={{0,1},{2,3},{4,5},{6,7},{8,9},{10,11},{12,13},{14,15},{16,17},{18,... | collective-permute-start | bytes 12296 | tf_op jit(solution)/shard_map/ppermute | solution.py:393
  12.5 20.0 %all-to-all-start = ((f32[8,5,16,128]{3,2,1,0:T(8,128)}), f32[8,5,16,128]{3,2,1,0:T(8,128)S(1)}, u32[]{:S(2)}, u32[]{:S(2)}) async-start(f32[8,5,16,128]{3,2,1,0:T(8,128)} %get-tuple-element.49), calls=%async_computation | async-start | bytes 655360 | tf_op jit(solution)/shard_map/all_to_all | solution.py:446
  21.5 5.4 %collective-permute-start.2 = (f32[5,16,512]{2,1,0:T(8,128)S(1)}, f32[5,16,512]{2,1,0:T(8,128)S(1)}, u32[]{:S(2)}, u32[]{:S(2)}) collective-permute-start(f32[5,16,512]{2,1,0:T(8,128)S(1)} %get-tuple-element.44.own_ref), channel_id=1, source_target_pairs={{0,16},{16,0},{32,48},{48,32},{64,80},{80,64},{96,112},{112,96},{1... | collective-permute-start | bytes 491528 | tf_op jit(solution)/shard_map/ppermute | solution.py:397
  27.0 6.6 %collective-permute-start.3 = (f32[5,16,512]{2,1,0:T(8,128)S(1)}, f32[5,16,512]{2,1,0:T(8,128)S(1)}, u32[]{:S(2)}, u32[]{:S(2)}) collective-permute-start(f32[5,16,512]{2,1,0:T(8,128)S(1)} %get-tuple-element.48.own_ref), channel_id=1, source_target_pairs={{0,48},{16,32},{32,16},{48,0},{64,112},{80,96},{96,80},{112,64},{1... | collective-permute-start | bytes 491528 | tf_op jit(solution)/shard_map/ppermute | solution.py:397
  33.6 15.8 %all-to-all-start.1 = ((f32[8,2,16,128]{3,2,1,0:T(8,128)}), f32[8,2,16,128]{3,2,1,0:T(8,128)S(1)}, u32[]{:S(2)}, u32[]{:S(2)}) async-start(f32[8,2,16,128]{3,2,1,0:T(8,128)} %y_reduced.1), calls=%async_computation.1 | async-start | bytes 262144 | tf_op jit(solution)/shard_map/all_to_all | solution.py:488
  40.9 5.4 %collective-permute-start.4 = (f32[5,16,512]{2,1,0:T(8,128)S(1)}, f32[5,16,512]{2,1,0:T(8,128)S(1)}, u32[]{:S(2)}, u32[]{:S(2)}) collective-permute-start(f32[5,16,512]{2,1,0:T(8,128)S(1)} %get-tuple-element.54.own_ref), channel_id=1, source_target_pairs={{0,64},{16,80},{32,96},{48,112},{64,0},{80,16},{96,32},{112,48},{1... | collective-permute-start | bytes 491528 | tf_op jit(solution)/shard_map/ppermute | solution.py:397
  46.3 5.6 %collective-permute-start.5 = (f32[2,16,512]{2,1,0:T(8,128)S(1)}, f32[2,16,512]{2,1,0:T(8,128)S(1)}, u32[]{:S(2)}, u32[]{:S(2)}) collective-permute-start(f32[2,16,512]{2,1,0:T(8,128)S(1)} %get-tuple-element.67.side_ref), channel_id=1, source_target_pairs={{0,192},{16,208},{32,224},{48,240},{64,128},{80,144},{96,160},{112... | collective-permute-start | bytes 196616 | tf_op jit(solution)/shard_map/ppermute | solution.py:397

commit v4 on v3

--- a/solution.py
+++ b/solution.py
@@ -13,7 +13,7 @@
 rows = 8
 f32 = jnp.float32
 vmem_spec = pl.BlockSpec(memory_space=pltpu.VMEM)
-smem_spec = pl.BlockSpec(memory_space=pltpu.SMEM)
+any_spec = pl.BlockSpec(memory_space=pl.ANY)
 hbm_spec = pl.BlockSpec(memory_space=pltpu.HBM)
 
 
@@ -188,6 +188,7 @@
     ys, xs, _ = t_ref.shape
     reduced_out[...] = reduced_ref[...]
     first_lane = lax.broadcasted_iota(jnp.int32, (rows, lane), 1) == 0
+    first_lane = first_lane & (lax.axis_index("gz") == 1)
     for c in range(xs // rows):
         part = pl.ds(c * rows, rows)
 
@@ -214,11 +215,15 @@
 kept_count = 13
 
 
-def x_edge_kernel(edge_ref, t_ref, reduced_ref, reduced_out, kept_ref):
+def x_edge_kernel(odd_ref, even_ref, t_ref, reduced_ref, reduced_out, kept_ref):
     xs = t_ref.shape[0]
     ys = reduced_ref.shape[1]
     row = pl.ds(0, 1)
-    here = drive_scale * edge_ref[row, :]
+    place = lax.axis_index("gy")
+    scale_odd = jnp.where(place % 2 == 1, drive_scale, 0.0)
+    scale_even = jnp.where((place % 2 == 0) & (place > 0), drive_scale, 0.0)
+    edge = scale_odd * odd_ref[...] + scale_even * even_ref[...]
+    here = edge[0:1]
     link = jnp.ones_like(here)
     left = jnp.zeros_like(here)
     kept_ref[11, row, :] = here
@@ -226,7 +231,7 @@
         t = t_ref[i]
         link = link * t
         left = left + link * here
-        here = drive_scale * edge_ref[pl.ds(i, 1), :] + here * t
+        here = edge[i:i + 1] + here * t
         kept_ref[11 + i // ys, pl.ds(i % ys, 1), :] = here
     for v in range(5):
         reduced_out[v] = reduced_ref[v]
@@ -389,10 +394,6 @@
     )(*arrays)
 
 
-def shift_up(x, axis):
-    return lax.ppermute(x, axis, [(i, i + 1) for i in range(lax.axis_size(axis) - 1)])
-
-
 def exchange(x, axis, mask):
     return lax.ppermute(x, axis, [(i, i ^ mask) for i in range(lax.axis_size(axis))])
 
@@ -430,8 +431,9 @@
         work=cost(cells, 60, 10),
     )
 
-    edge_z = shift_up(my_edge, "gz")
-    edge_y = shift_up(mx_edge, "gy")
+    edge_z = exchange(my_edge, "gz", 1)
+    edge_odd = exchange(mx_edge, "gy", 1)
+    edge_even = lax.ppermute(mx_edge, "gy", [(i, (i + (1 if i % 2 else -1)) % lax.axis_size("gy")) for i in range(lax.axis_size("gy"))])
     y_reduced, y_drive = pl.pallas_call(
         y_edge_kernel,
         in_specs=[vmem_spec] * 4,
@@ -442,13 +444,13 @@
         cost_estimate=cost(cells // 4, 10, 3),
         name="y_edge",
     )(*(pltpu.with_memory_space_constraint(a, V) for a in (edge_z, yt_edge, y_reduced, y_drive)))
-    y_reduced, edge_y = lax.optimization_barrier((y_reduced, edge_y))
+    y_reduced, edge_odd, edge_even = lax.optimization_barrier((y_reduced, edge_odd, edge_even))
     y_blocks = lax.all_to_all(y_reduced, "gy", 0, 0, tiled=True)
 
     x_reduced, kept = call(
         x_edge_kernel,
         "x_edge",
-        [(vmem_spec, a) for a in (edge_y, xt_edge, x_reduced)],
+        [(vmem_spec, a) for a in (edge_odd, edge_even, xt_edge, x_reduced)],
         [(vmem_spec, V((5, ys, zs), f32)), (vmem_spec, V((kept_count, ys, zs), f32))],
         limit=8,
         work=cost(cells // ys, 10, 3),
@@ -467,18 +469,16 @@
     own = x_reduced
     for level, mask in enumerate((1, 3, 4)):
         other = exchange(own, "gx", mask)
-        if level == 1:
-            other, y_ends = lax.optimization_barrier((other, y_ends))
         kernel = functools.partial(merge_kernel if level < 2 else last_merge_kernel, level)
 
-        def body(own_ref, other_ref, kept_in, *refs, kernel=kernel):
-            merged_ref, kept_ref = refs[2], refs[3]
-            kernel(own_ref, other_ref, kept_in, merged_ref, kept_ref)
+        def body(own_ref, other_ref, *refs, kernel=kernel):
+            merged_ref, kept_ref = refs[-4:-2]
+            kernel(own_ref, other_ref, None, merged_ref, kept_ref)
 
         own, kept, y_t, y_drive = call(
             body,
             "x_merge",
-            [(vmem_spec, own), (vmem_spec, other)],
+            [(vmem_spec, own), (vmem_spec, other)] + ([(any_spec, y_ends)] if level == 1 else []),
             [(vmem_spec, V((5 if level < 2 else 2, ys, zs), f32))],
             carried=(kept, y_t, y_drive),
             limit=8,

time: 53.5 us -> 48.8 us (0.912)
  starting transfers between devices: 30.6 us -> 26 us
    ppermute x4 -> x6, starting transfers between devices: 9.18 us -> 13.2 us  [exchange(): lax.ppermute(x, axis, [(i, i ^ mask) for i in range(lax.axis_size(axis))])]
    ppermute x2 -> x1, starting transfers between devices: 5.28 us -> 2 us  [per_device(): lax.ppermute(mx_edge, 'gy', [(i, (i + (1 if i % 2 else -1)) % lax.axis_si...]
    all_to_all x1, starting transfers between devices: 8.91 us -> 5.84 us  [per_device(): y_blocks = lax.all_to_all(y_reduced, 'gy', 0, 0, tiled=True)]
    all_to_all x1, starting transfers between devices: 7.21 us -> 4.96 us  [per_device(): y_ends = lax.all_to_all(y_ends, 'gy', 0, 0, tiled=True)]
    ppermute x4 -> x6, waiting for transfers between devices: 8.33 us -> 9.36 us  [exchange(): lax.ppermute(x, axis, [(i, i ^ mask) for i in range(lax.axis_size(axis))])]
    ppermute x2 -> x1, waiting for transfers between devices: 0.81 us -> 0.01 us  [per_device(): lax.ppermute(mx_edge, 'gy', [(i, (i + (1 if i % 2 else -1)) % lax.axis_si...]
  transfers between devices with their start and end apart: 8 -> 9, of which waited for: 6 -> 6; matrix products, arithmetic and copies ran while one was open for 0% -> 0% of each run, Pallas kernels for 7% -> 8%
where the time goes in v4:
time: 48.8 us; the launch traced here: 48.5 us
  starting transfers between devices  26 us (53%)
  waiting for transfers between devices  11.7 us (24%)
  Pallas kernels  10 us (20%)
  between operations  0.68 us (1%)
    ppermute x6, starting transfers between devices, exchange(): lax.ppermute(x, axis, [(i, i ^ mask) for i in range(lax.axis_size(axis))])  13.2 us
    ppermute x6, waiting for transfers between devices, exchange(): lax.ppermute(x, axis, [(i, i ^ mask) for i in range(lax.axis_size(axis))])  9.36 us
    pallas_call x7, Pallas kernels, call(): pl.pallas_call(kernel, in_specs=specs, out_specs=out_specs, out_shape=out...  8.36 us
    all_to_all x1, starting transfers between devices, per_device(): y_blocks = lax.all_to_all(y_reduced, 'gy', 0, 0, tiled=True)  5.84 us
    all_to_all x1, starting transfers between devices, per_device(): y_ends = lax.all_to_all(y_ends, 'gy', 0, 0, tiled=True)  4.96 us
    all_to_all x1, waiting for transfers between devices, per_device(): y_blocks = lax.all_to_all(y_reduced, 'gy', 0, 0, tiled=True)  2.38 us
    ppermute x1, starting transfers between devices, per_device(): lax.ppermute(mx_edge, 'gy', [(i, (i + (1 if i % 2 else -1)) % lax.axis_si...  2 us
  transfers between devices with their start and end apart: 9, of which 6 were waited for; matrix products, arithmetic and copies ran while one was open for 0% of the time, Pallas kernels for 8%

profile of v4, /device:TPU:32, one launch (start us, length us, event | category | flops | bytes accessed | tf_op | source)
XLA Modules:
  0.0 48.5 jit_solution(14778931140561712475)
XLA Ops:
  0.6 4.9 %forward.1 = (f32[16,32,512]{2,1,0:T(8,128)S(1)}, f32[16,32,512]{2,1,0:T(8,128)S(1)}, f32[8,5,16,128]{3,2,1,0:T(8,128)S(1)}, f32[32,16,512]{2,1,0:T(8,128)}, f32...) custom-call(f32[16]{0:T(128)} %table_hbm.1, ...), custom_call_target="tpu_custom_call" | custom-call | flops 15728640 | bytes 10485760 | tf_op jit(solution)/shard_map/forward/pallas_call | solution.py:384
  5.5 2.0 %collective-permute-start.2 = (f32[32,512]{1,0:T(8,128)S(1)}, f32[32,512]{1,0:T(8,128)S(1)}, u32[]{:S(2)}, u32[]{:S(2)}) collective-permute-start(f32[32,512]{1,0:T(8,128)S(1)} %get-tuple-element.39), channel_id=1, source_target_pairs={{0,14},{2,4},{4,2},{6,8},{8,6},{10,12},{12,10},{14,0},{1,15},{3,5}... | collective-permute-start | bytes 196616 | tf_op jit(solution)/shard_map/ppermute | solution.py:436
  7.5 4.0 %collective-permute-start.1 = (f32[32,512]{1,0:T(8,128)S(1)}, f32[32,512]{1,0:T(8,128)S(1)}, u32[]{:S(2)}, u32[]{:S(2)}) collective-permute-start(f32[32,512]{1,0:T(8,128)S(1)} %get-tuple-element.39), channel_id=1, source_target_pairs={{0,2},{2,0},{4,6},{6,4},{8,10},{10,8},{12,14},{14,12},{1,3},{3,1},... | collective-permute-start | bytes 196616 | tf_op jit(solution)/shard_map/ppermute | solution.py:398
  11.6 0.0 collective-permute-start
  11.6 1.2 %collective-permute-done.edge_ref = f32[8,128]{1,0:T(8,128)S(1)} collective-permute-done((f32[8,128]{1,0:T(8,128)S(1)}, f32[8,128]{1,0:T(8,128)S(1)}, u32[]{:S(2)}, u32[]{:S(2)}) %collective-permute-start) | collective-permute-done | bytes 4128 | tf_op jit(solution)/shard_map/ppermute | solution.py:398
  12.7 0.9 %y_edge.1 = (f32[8,5,16,128]{3,2,1,0:T(8,128)}, f32[16,32,512]{2,1,0:T(8,128)S(1)}) custom-call(f32[8,128]{1,0:T(8,128)S(1)} %collective-permute-done.edge_ref, f32[16,32,128]{2,1,0:T(8,128)S(1)} %get-tuple-element.35.t_ref, f32[8,5,16,128]{3,2,1,0:T(8,128)S(1)} %get-tuple-element.36.reduced_ref, ...), custom_call_target="tpu_custom_call", output_to_operand_aliasing={{1}: (3, {})} | custom-call | flops 655360 | bytes 786432 | tf_op jit(solution)/shard_map/y_edge/pallas_call | solution.py:437
  13.7 0.0 collective-permute-done.2.even_ref
  13.7 0.1 collective-permute-done.1.odd_ref
  13.8 5.8 %all-to-all-start = ((f32[8,5,16,128]{3,2,1,0:T(8,128)}), f32[8,5,16,128]{3,2,1,0:T(8,128)S(1)}, u32[]{:S(2)}, u32[]{:S(2)}) async-start(f32[8,5,16,128]{3,2,1,0:T(8,128)} %get-tuple-element.49), calls=%async_computation | async-start | bytes 655360 | tf_op jit(solution)/shard_map/all_to_all | solution.py:448
  19.7 0.1 x_edge.1
  19.8 1.6 %collective-permute-start.3 = (f32[5,16,512]{2,1,0:T(8,128)S(1)}, f32[5,16,512]{2,1,0:T(8,128)S(1)}, u32[]{:S(2)}, u32[]{:S(2)}) collective-permute-start(f32[5,16,512]{2,1,0:T(8,128)S(1)} %get-tuple-element.44.own_ref), channel_id=1, source_target_pairs={{0,16},{16,0},{32,48},{48,32},{64,80},{80,64},{96,112},{112,96},{1... | collective-permute-start | bytes 491528 | tf_op jit(solution)/shard_map/ppermute | solution.py:398
  21.4 3.8 %collective-permute-done.3.other_ref = f32[5,16,512]{2,1,0:T(8,128)S(1)} collective-permute-done((f32[5,16,512]{2,1,0:T(8,128)S(1)}, f32[5,16,512]{2,1,0:T(8,128)S(1)}, u32[]{:S(2)}, u32[]{:S(2)}) %collective-permute-start.3) | collective-permute-done | bytes 163872 | tf_op jit(solution)/shard_map/ppermute | solution.py:398
  25.2 2.8 %collective-permute-start.4 = (f32[5,16,512]{2,1,0:T(8,128)S(1)}, f32[5,16,512]{2,1,0:T(8,128)S(1)}, u32[]{:S(2)}, u32[]{:S(2)}) collective-permute-start(f32[5,16,512]{2,1,0:T(8,128)S(1)} %get-tuple-element.48.own_ref), channel_id=1, source_target_pairs={{0,48},{16,32},{32,16},{48,0},{64,112},{80,96},{96,80},{112,64},{1... | collective-permute-start | bytes 491528 | tf_op jit(solution)/shard_map/ppermute | solution.py:398
  28.1 2.4 %all-to-all-done.blocks_ref = f32[8,5,16,128]{3,2,1,0:T(8,128)S(1)} async-done(((f32[8,5,16,128]{3,2,1,0:T(8,128)}), f32[8,5,16,128]{3,2,1,0:T(8,128)S(1)}, u32[]{:S(2)}, u32[]{:S(2)}) %all-to-all-start) | async-done | bytes 327712 | tf_op jit(solution)/shard_map/all_to_all | solution.py:448
  30.5 0.8 %y_reduced.1.refs_0_ = f32[8,2,16,128]{3,2,1,0:T(8,128)} custom-call(f32[8,5,16,128]{3,2,1,0:T(8,128)S(1)} %all-to-all-done.blocks_ref), custom_call_target="tpu_custom_call" | custom-call | flops 327680 | bytes 458752 | tf_op jit(solution)/shard_map/y_reduced/pallas_call | solution.py:459
  31.2 0.0 copy-start
  31.2 5.0 %all-to-all-start.1 = ((f32[8,2,16,128]{3,2,1,0:T(8,128)}), f32[8,2,16,128]{3,2,1,0:T(8,128)S(1)}, u32[]{:S(2)}, u32[]{:S(2)}) async-start(f32[8,2,16,128]{3,2,1,0:T(8,128)} %y_reduced.1.refs_0_), calls=%async_computation.1 | async-start | bytes 262144 | tf_op jit(solution)/shard_map/all_to_all | solution.py:488
  36.2 0.0 collective-permute-done.4.other_ref
  36.2 0.0 copy-done
  36.3 1.7 %collective-permute-start.5 = (f32[5,16,512]{2,1,0:T(8,128)S(1)}, f32[5,16,512]{2,1,0:T(8,128)S(1)}, u32[]{:S(2)}, u32[]{:S(2)}) collective-permute-start(f32[5,16,512]{2,1,0:T(8,128)S(1)} %get-tuple-element.53.own_ref), channel_id=1, source_target_pairs={{0,64},{16,80},{32,96},{48,112},{64,0},{80,16},{96,32},{112,48},{1... | collective-permute-start | bytes 491528 | tf_op jit(solution)/shard_map/ppermute | solution.py:398
  37.9 3.7 %collective-permute-done.5.other_ref = f32[5,16,512]{2,1,0:T(8,128)S(1)} collective-permute-done((f32[5,16,512]{2,1,0:T(8,128)S(1)}, f32[5,16,512]{2,1,0:T(8,128)S(1)}, u32[]{:S(2)}, u32[]{:S(2)}) %collective-permute-start.5) | collective-permute-done | bytes 163872 | tf_op jit(solution)/shard_map/ppermute | solution.py:398
  41.7 0.1 x_merge.5
  41.7 3.1 %collective-permute-start.6 = (f32[2,16,512]{2,1,0:T(8,128)S(1)}, f32[2,16,512]{2,1,0:T(8,128)S(1)}, u32[]{:S(2)}, u32[]{:S(2)}) collective-permute-start(f32[2,16,512]{2,1,0:T(8,128)S(1)} %get-tuple-element.65.side_ref), channel_id=1, source_target_pairs={{0,192},{16,208},{32,224},{48,240},{64,128},{80,144},{96,160},{112... | collective-permute-start | bytes 196616 | tf_op jit(solution)/shard_map/ppermute | solution.py:398
  44.8 0.0 all-to-all-done.1.ends_ref
  44.8 2.0 %y_back.1 = (f32[32,16,512]{2,1,0:T(8,128)}, f32[32,16,512]{2,1,0:T(8,128)S(1)}, f32[32,16,512]{2,1,0:T(8,128)S(1)}) custom-call(f32[16,32,512]{2,1,0:T(8,128)S(1)} %get-tuple-element.57.t_ref, f32[16,32,512]{2,1,0:T(8,128)S(1)} %get-tuple-element.58.drive_ref, f32[8,2,16,128]{3,2,1,0:T(8,128)S(1)} %all-to-all-done.1.ends_ref, ...), custom_call_target="tpu_custom_call" | custom-call | flops 1310720 | bytes 3145728 | tf_op jit(solution)/shard_map/y_back/pallas_call | solution.py:384
  46.8 0.5 collective-permute-done.6.other_ref
  47.3 1.2 %x_back.1 = f32[32,16,512]{2,1,0:T(8,128)} custom-call(f32[32,16,512]{2,1,0:T(8,128)S(1)} %get-tuple-element.62.t_ref, f32[32,16,512]{2,1,0:T(8,128)S(1)} %get-tuple-element.63.drive_ref, f32[13,16,512]{2,1,0:T(8,128)S(1)} %get-tuple-element.64.kept_ref, f32[2,16,512]{2,1,0:T(8,128)S(1)} %get-tuple-element.65.side_ref, ...), custom_call_target="tpu_custom_call" | custom-call | flops 1310720 | bytes 3145728 | tf_op jit(solution)/shard_map/x_back/pallas_call | solution.py:384
  (2 shorter events, 0.1 us)
Async XLA Ops:
  5.5 8.1 %collective-permute-start.2 = (f32[32,512]{1,0:T(8,128)S(1)}, f32[32,512]{1,0:T(8,128)S(1)}, u32[]{:S(2)}, u32[]{:S(2)}) collective-permute-start(f32[32,512]{1,0:T(8,128)S(1)} %get-tuple-element.39), channel_id=1, source_target_pairs={{0,14},{2,4},{4,2},{6,8},{8,6},{10,12},{12,10},{14,0},{1,15},{3,5}... | collective-permute-start | bytes 196616 | tf_op jit(solution)/shard_map/ppermute | solution.py:436
  7.5 6.3 %collective-permute-start.1 = (f32[32,512]{1,0:T(8,128)S(1)}, f32[32,512]{1,0:T(8,128)S(1)}, u32[]{:S(2)}, u32[]{:S(2)}) collective-permute-start(f32[32,512]{1,0:T(8,128)S(1)} %get-tuple-element.39), channel_id=1, source_target_pairs={{0,2},{2,0},{4,6},{6,4},{8,10},{10,8},{12,14},{14,12},{1,3},{3,1},... | collective-permute-start | bytes 196616 | tf_op jit(solution)/shard_map/ppermute | solution.py:398
  11.6 1.2 %collective-permute-start = (f32[8,128]{1,0:T(8,128)S(1)}, f32[8,128]{1,0:T(8,128)S(1)}, u32[]{:S(2)}, u32[]{:S(2)}) collective-permute-start(f32[8,128]{1,0:T(8,128)S(1)} %get-tuple-element.34), channel_id=1, source_target_pairs={{0,1},{1,0},{2,3},{3,2},{4,5},{5,4},{6,7},{7,6},{8,9},{9,8},{10,11... | collective-permute-start | bytes 12296 | tf_op jit(solution)/shard_map/ppermute | solution.py:398
  13.8 16.7 %all-to-all-start = ((f32[8,5,16,128]{3,2,1,0:T(8,128)}), f32[8,5,16,128]{3,2,1,0:T(8,128)S(1)}, u32[]{:S(2)}, u32[]{:S(2)}) async-start(f32[8,5,16,128]{3,2,1,0:T(8,128)} %get-tuple-element.49), calls=%async_computation | async-start | bytes 655360 | tf_op jit(solution)/shard_map/all_to_all | solution.py:448
  19.8 5.4 %collective-permute-start.3 = (f32[5,16,512]{2,1,0:T(8,128)S(1)}, f32[5,16,512]{2,1,0:T(8,128)S(1)}, u32[]{:S(2)}, u32[]{:S(2)}) collective-permute-start(f32[5,16,512]{2,1,0:T(8,128)S(1)} %get-tuple-element.44.own_ref), channel_id=1, source_target_pairs={{0,16},{16,0},{32,48},{48,32},{64,80},{80,64},{96,112},{112,96},{1... | collective-permute-start | bytes 491528 | tf_op jit(solution)/shard_map/ppermute | solution.py:398
  25.2 11.0 %collective-permute-start.4 = (f32[5,16,512]{2,1,0:T(8,128)S(1)}, f32[5,16,512]{2,1,0:T(8,128)S(1)}, u32[]{:S(2)}, u32[]{:S(2)}) collective-permute-start(f32[5,16,512]{2,1,0:T(8,128)S(1)} %get-tuple-element.48.own_ref), channel_id=1, source_target_pairs={{0,48},{16,32},{32,16},{48,0},{64,112},{80,96},{96,80},{112,64},{1... | collective-permute-start | bytes 491528 | tf_op jit(solution)/shard_map/ppermute | solution.py:398
  31.2 5.0 %copy-start = (f32[8,2,16,128]{3,2,1,0:T(8,128)S(1)}, f32[8,2,16,128]{3,2,1,0:T(8,128)}, u32[]{:S(2)}) copy-start(f32[8,2,16,128]{3,2,1,0:T(8,128)} %y_reduced.1.refs_0_) | copy-start | bytes 393220
  31.2 13.6 %all-to-all-start.1 = ((f32[8,2,16,128]{3,2,1,0:T(8,128)}), f32[8,2,16,128]{3,2,1,0:T(8,128)S(1)}, u32[]{:S(2)}, u32[]{:S(2)}) async-start(f32[8,2,16,128]{3,2,1,0:T(8,128)} %y_reduced.1.refs_0_), calls=%async_computation.1 | async-start | bytes 262144 | tf_op jit(solution)/shard_map/all_to_all | solution.py:488
  36.3 5.4 %collective-permute-start.5 = (f32[5,16,512]{2,1,0:T(8,128)S(1)}, f32[5,16,512]{2,1,0:T(8,128)S(1)}, u32[]{:S(2)}, u32[]{:S(2)}) collective-permute-start(f32[5,16,512]{2,1,0:T(8,128)S(1)} %get-tuple-element.53.own_ref), channel_id=1, source_target_pairs={{0,64},{16,80},{32,96},{48,112},{64,0},{80,16},{96,32},{112,48},{1... | collective-permute-start | bytes 491528 | tf_op jit(solution)/shard_map/ppermute | solution.py:398
  41.7 5.6 %collective-permute-start.6 = (f32[2,16,512]{2,1,0:T(8,128)S(1)}, f32[2,16,512]{2,1,0:T(8,128)S(1)}, u32[]{:S(2)}, u32[]{:S(2)}) collective-permute-start(f32[2,16,512]{2,1,0:T(8,128)S(1)} %get-tuple-element.65.side_ref), channel_id=1, source_target_pairs={{0,192},{16,208},{32,224},{48,240},{64,128},{80,144},{96,160},{112... | collective-permute-start | bytes 196616 | tf_op jit(solution)/shard_map/ppermute | solution.py:398

commit v5 on v4

--- a/solution.py
+++ b/solution.py
@@ -47,10 +47,10 @@
 
 def forward_kernel(
     table_hbm, material_hbm, ex_hbm, ez_hbm, mx_hbm, my_hbm, mz_hbm,
-    yt_ref, ydrive_ref, yreduced_ref, xt_hbm, xdrive_hbm, xreduced_ref,
+    yt_ref, ydrive_ref, yreduced_ref, xt_ref, xdrive_ref, xreduced_ref,
     yt_edge_ref, my_edge_ref, xt_edge_ref, mx_edge_ref,
-    table_s, material_s, ex_s, ez_s, mx_s, my_s, mz_s, xt_s, xjs_s, ground_s, ydrive_s, xdrive_s, turn_s,
-    state_s, last_my_s, table_sem, sems, out_sems,
+    table_s, material_s, ex_s, ez_s, mx_s, my_s, mz_s, ground_s, yground_s, ydrive_s, xdrive_s, turn_s,
+    state_s, last_my_s, table_sem, sems,
 ):
     xs, ys, zs = material_s.shape
     tiles = zs // lane
@@ -67,13 +67,6 @@
         return [
             pltpu.make_async_copy(source.at[part], target.at[part], sems.at[a, c])
             for a, (source, target) in enumerate(arrays)
-        ]
-
-    def chunk_stores(c):
-        part = pl.ds(pl.multiple_of(c * rows, rows), rows)
-        return [
-            pltpu.make_async_copy(source.at[part], target.at[part], out_sems.at[a, c])
-            for a, (source, target) in enumerate(((xt_s, xt_hbm), (xjs_s, xdrive_hbm)))
         ]
 
     table_copy = pltpu.make_async_copy(table_hbm, table_s, table_sem)
@@ -115,7 +108,13 @@
             my_up = (my - jnp.concatenate([last_my_s[:, cut][None], my[:-1]], axis=0)).reshape(flat)
             last_my_s[:, cut] = my[rows - 1]
             ground_s[k] = ground
-            ydrive_s[k] = ground * ex_s[part, :, cut].reshape(flat) + drive_scale * (mz_step - my_step)
+            ydrive = ground * ex_s[part, :, cut].reshape(flat) + drive_scale * (mz_step - my_step)
+            for i in range(rows):
+                for h in range(0, ys, rows):
+                    turned = pl.ds(h * rows + i, rows, stride=rows)
+                    natural = slice(i * ys + h, i * ys + h + rows)
+                    yground_s[k, turned, :] = ground[natural]
+                    ydrive_s[k, turned, :] = ydrive[natural]
             xdrive_s[k] = ground * ez_s[part, :, cut].reshape(flat) + drive_scale * (my_up - mx_step)
             mx_edge_ref[part, cut] = mx_s[part, ys - 1, cut]
             if k == tiles - 1:
@@ -130,26 +129,24 @@
                 if i == 0:
                     state = (jnp.where(c == 0, 1.0, state[0]),) + state[1:]
                 states[k] = state
-                xt_s[c * rows + i, :, cut] = t
+                xt_ref[c * rows + i, :, cut] = t
                 js = state[4]
                 if i == rows - 1:
                     js = jnp.where(c == chunks - 1, drive_scale * last_my_s[:, cut], js)
-                xjs_s[c * rows + i, :, cut] = js
+                xdrive_ref[c * rows + i, :, cut] = js
                 xt_edge_ref[c * rows + i, :, cut] = t[0:1]
         for k in range(tiles):
             for v in range(5):
                 state_s[v, :, pl.ds(k * lane, lane)] = states[k][v]
-        for copy in chunk_stores(c):
-            copy.start()
 
         for first in range(0, tiles, 2):
             pair = (first, first + 1)
             states = [None, None]
             for j in range(ys):
-                pick = pl.ds(j, rows, stride=ys)
+                pick = pl.ds(j * rows, rows)
                 for n, k in enumerate(pair):
                     cut = pl.ds(k * lane, lane)
-                    ground = ground_s[k, pick, :]
+                    ground = yground_s[k, pick, :]
                     drive = ydrive_s[k, pick, :]
                     if j == 0:
                         zero = jnp.zeros_like(ground)
@@ -179,9 +176,6 @@
     rim = drive_scale * last_my_s[...]
     for v, value in enumerate(close_block(tuple(state_s[v] for v in range(5)), rim)):
         xreduced_ref[v] = value
-    for c in range(chunks):
-        for copy in chunk_stores(c):
-            copy.wait()
 
 
 def y_edge_kernel(edge_ref, t_ref, reduced_ref, drive_ref, reduced_out, drive_out):
@@ -215,14 +209,11 @@
 kept_count = 13
 
 
-def x_edge_kernel(odd_ref, even_ref, t_ref, reduced_ref, reduced_out, kept_ref):
+def x_edge_kernel(edge_ref, t_ref, reduced_ref, reduced_out, kept_ref):
     xs = t_ref.shape[0]
     ys = reduced_ref.shape[1]
     row = pl.ds(0, 1)
-    place = lax.axis_index("gy")
-    scale_odd = jnp.where(place % 2 == 1, drive_scale, 0.0)
-    scale_even = jnp.where((place % 2 == 0) & (place > 0), drive_scale, 0.0)
-    edge = scale_odd * odd_ref[...] + scale_even * even_ref[...]
+    edge = jnp.where(lax.axis_index("gy") > 0, drive_scale, 0.0) * edge_ref[...]
     here = edge[0:1]
     link = jnp.ones_like(here)
     left = jnp.zeros_like(here)
@@ -365,6 +356,17 @@
         out_ref[i] = value
 
 
+def store_kernel(t_ref, drive_ref, t_hbm, drive_hbm, sems):
+    copies = [
+        pltpu.make_async_copy(t_ref, t_hbm, sems.at[0]),
+        pltpu.make_async_copy(drive_ref, drive_hbm, sems.at[1]),
+    ]
+    for copy in copies:
+        copy.start()
+    for copy in copies:
+        copy.wait()
+
+
 def cost(elements, ops, arrays):
     return pl.CostEstimate(flops=elements * ops, bytes_accessed=elements * 4 * arrays, transcendentals=0)
 
@@ -414,8 +416,8 @@
             (vmem_spec, V((ys, xs, zs), f32)),
             (vmem_spec, V((ys, xs, zs), f32)),
             (vmem_spec, V(block, f32)),
-            (hbm_spec, H((xs, ys, zs), f32)),
-            (hbm_spec, H((xs, ys, zs), f32)),
+            (vmem_spec, V((xs, ys, zs), f32)),
+            (vmem_spec, V((xs, ys, zs), f32)),
             (vmem_spec, V((5, ys, zs), f32)),
             (vmem_spec, V((ys, xs, lane), f32)),
             (vmem_spec, V((rows, lane), f32)),
@@ -423,17 +425,17 @@
             (vmem_spec, V((xs, zs), f32)),
         ],
         scratch=[pltpu.SMEM(perm_table.shape, f32), V((xs, ys, zs), jnp.int32)]
-        + [V((xs, ys, zs), f32)] * 7
-        + [V((zs // lane, rows * ys, lane), f32)] * 3
+        + [V((xs, ys, zs), f32)] * 5
+        + [V((zs // lane, rows * ys, lane), f32)] * 4
         + [V((rows * ys, lane), f32), V((5, ys, zs), f32), V((ys, zs), f32)]
-        + [pltpu.SemaphoreType.DMA, pltpu.SemaphoreType.DMA((6, chunks)), pltpu.SemaphoreType.DMA((2, chunks))],
+        + [pltpu.SemaphoreType.DMA, pltpu.SemaphoreType.DMA((6, chunks))],
         limit=24,
         work=cost(cells, 60, 10),
     )
 
     edge_z = exchange(my_edge, "gz", 1)
-    edge_odd = exchange(mx_edge, "gy", 1)
-    edge_even = lax.ppermute(mx_edge, "gy", [(i, (i + (1 if i % 2 else -1)) % lax.axis_size("gy")) for i in range(lax.axis_size("gy"))])
+    count = lax.axis_size("gy")
+    edge_y = lax.ppermute(mx_edge, "gy", [(i, (i + 1) % count) for i in range(count)])
     y_reduced, y_drive = pl.pallas_call(
         y_edge_kernel,
         in_specs=[vmem_spec] * 4,
@@ -444,13 +446,24 @@
         cost_estimate=cost(cells // 4, 10, 3),
         name="y_edge",
     )(*(pltpu.with_memory_space_constraint(a, V) for a in (edge_z, yt_edge, y_reduced, y_drive)))
-    y_reduced, edge_odd, edge_even = lax.optimization_barrier((y_reduced, edge_odd, edge_even))
+    x_t, x_drive = call(
+        store_kernel,
+        "store",
+        [(vmem_spec, x_t), (vmem_spec, x_drive)],
+        [(hbm_spec, H((xs, ys, zs), f32))] * 2,
+        scratch=[pltpu.SemaphoreType.DMA((2,))],
+        limit=8,
+        work=cost(cells, 1, 4),
+    )
+    y_reduced, edge_y, x_t, x_drive = lax.optimization_barrier(
+        (y_reduced, edge_y, x_t, x_drive)
+    )
     y_blocks = lax.all_to_all(y_reduced, "gy", 0, 0, tiled=True)
 
     x_reduced, kept = call(
         x_edge_kernel,
         "x_edge",
-        [(vmem_spec, a) for a in (edge_odd, edge_even, xt_edge, x_reduced)],
+        [(vmem_spec, a) for a in (edge_y, xt_edge, x_reduced)],
         [(vmem_spec, V((5, ys, zs), f32)), (vmem_spec, V((kept_count, ys, zs), f32))],
         limit=8,
         work=cost(cells // ys, 10, 3),

time: 48.8 us -> 47.7 us (0.977)
  waiting for transfers between devices: 11.7 us -> 10.4 us
    ppermute x6 -> x5, starting transfers between devices: 13.2 us -> 9.19 us  [exchange(): lax.ppermute(x, axis, [(i, i ^ mask) for i in range(lax.axis_size(axis))])]
    all_to_all x1, starting transfers between devices: 5.84 us -> 9.78 us  [per_device(): y_blocks = lax.all_to_all(y_reduced, 'gy', 0, 0, tiled=True)]
    ppermute x6 -> x5, waiting for transfers between devices: 9.36 us -> 8.05 us  [exchange(): lax.ppermute(x, axis, [(i, i ^ mask) for i in range(lax.axis_size(axis))])]
    pallas_call x7 -> x8, Pallas kernels: 8.36 us -> 8.57 us  [call(): pl.pallas_call(kernel, in_specs=specs, out_specs=out_specs, out_shape=out...]
  transfers between devices with their start and end apart: 9 -> 8, of which waited for: 6 -> 5; matrix products, arithmetic and copies ran while one was open for 0% -> 0% of each run, Pallas kernels for 8% -> 11%
where the time goes in v5:
time: 47.7 us; the launch traced here: 47.4 us
  starting transfers between devices  26.1 us (55%)
  waiting for transfers between devices  10.4 us (22%)
  Pallas kernels  10.3 us (22%)
  between operations  0.69 us (1%)
    all_to_all x1, starting transfers between devices, per_device(): y_blocks = lax.all_to_all(y_reduced, 'gy', 0, 0, tiled=True)  9.78 us
    ppermute x5, starting transfers between devices, exchange(): lax.ppermute(x, axis, [(i, i ^ mask) for i in range(lax.axis_size(axis))])  9.19 us
    pallas_call x8, Pallas kernels, call(): pl.pallas_call(kernel, in_specs=specs, out_specs=out_specs, out_shape=out...  8.57 us
    ppermute x5, waiting for transfers between devices, exchange(): lax.ppermute(x, axis, [(i, i ^ mask) for i in range(lax.axis_size(axis))])  8.05 us
    all_to_all x1, starting transfers between devices, per_device(): y_ends = lax.all_to_all(y_ends, 'gy', 0, 0, tiled=True)  5.09 us
    all_to_all x1, waiting for transfers between devices, per_device(): y_blocks = lax.all_to_all(y_reduced, 'gy', 0, 0, tiled=True)  2.25 us
    ppermute x1, starting transfers between devices, per_device(): lax.ppermute(mx_edge, 'gy', [(i, (i + 1) % count) for i in range(count)])  1.99 us
  transfers between devices with their start and end apart: 8, of which 5 were waited for; matrix products, arithmetic and copies ran while one was open for 0% of the time, Pallas kernels for 11%

profile of v5, /device:TPU:32, one launch (start us, length us, event | category | flops | bytes accessed | tf_op | source)
XLA Modules:
  0.0 47.4 jit_solution(13401661731063201660)
XLA Ops:
  0.6 3.7 %forward.1 = (f32[16,32,512]{2,1,0:T(8,128)S(1)}, f32[16,32,512]{2,1,0:T(8,128)S(1)}, f32[8,5,16,128]{3,2,1,0:T(8,128)S(1)}, f32[32,16,512]{2,1,0:T(8,128)S(1)},...) custom-call(f32[16]{0:T(128)} %table_hbm.1, ...), custom_call_target="tpu_custom_call" | custom-call | flops 15728640 | bytes 10485760 | tf_op jit(solution)/shard_map/forward/pallas_call | solution.py:386
  4.4 2.0 %collective-permute-start.1 = (f32[32,512]{1,0:T(8,128)S(1)}, f32[32,512]{1,0:T(8,128)S(1)}, u32[]{:S(2)}, u32[]{:S(2)}) collective-permute-start(f32[32,512]{1,0:T(8,128)S(1)} %get-tuple-element.42), channel_id=1, source_target_pairs={{0,2},{2,4},{4,6},{6,8},{8,10},{10,12},{12,14},{14,0},{1,3},{3,5},... | collective-permute-start | bytes 196616 | tf_op jit(solution)/shard_map/ppermute | solution.py:438
  6.4 0.0 collective-permute-start
  6.4 1.3 %store.1 = (f32[32,16,512]{2,1,0:T(8,128)}, f32[32,16,512]{2,1,0:T(8,128)}) custom-call(f32[32,16,512]{2,1,0:T(8,128)S(1)} %get-tuple-element.43.t_ref, f32[32,16,512]{2,1,0:T(8,128)S(1)} %get-tuple-element.44.drive_ref), custom_call_target="tpu_custom_call" | custom-call | flops 262144 | bytes 4194304 | tf_op jit(solution)/shard_map/store/pallas_call | solution.py:386
  7.7 0.0 collective-permute-done.edge_ref
  7.7 0.9 %y_edge.1 = (f32[8,5,16,128]{3,2,1,0:T(8,128)}, f32[16,32,512]{2,1,0:T(8,128)S(1)}) custom-call(f32[8,128]{1,0:T(8,128)S(1)} %collective-permute-done.edge_ref, f32[16,32,128]{2,1,0:T(8,128)S(1)} %get-tuple-element.38.t_ref, f32[8,5,16,128]{3,2,1,0:T(8,128)S(1)} %get-tuple-element.39.reduced_ref, ...), custom_call_target="tpu_custom_call", output_to_operand_aliasing={{1}: (3, {})} | custom-call | flops 655360 | bytes 786432 | tf_op jit(solution)/shard_map/y_edge/pallas_call | solution.py:439
  8.7 0.1 collective-permute-done.1.edge_ref
  8.7 9.8 %all-to-all-start = ((f32[8,5,16,128]{3,2,1,0:T(8,128)}), f32[8,5,16,128]{3,2,1,0:T(8,128)S(1)}, u32[]{:S(2)}, u32[]{:S(2)}) async-start(f32[8,5,16,128]{3,2,1,0:T(8,128)} %get-tuple-element.55), calls=%async_computation | async-start | bytes 655360 | tf_op jit(solution)/shard_map/all_to_all | solution.py:461
  18.5 0.1 x_edge.1
  18.6 1.6 %collective-permute-start.2 = (f32[5,16,512]{2,1,0:T(8,128)S(1)}, f32[5,16,512]{2,1,0:T(8,128)S(1)}, u32[]{:S(2)}, u32[]{:S(2)}) collective-permute-start(f32[5,16,512]{2,1,0:T(8,128)S(1)} %get-tuple-element.50.own_ref), channel_id=1, source_target_pairs={{0,16},{16,0},{32,48},{48,32},{64,80},{80,64},{96,112},{112,96},{1... | collective-permute-start | bytes 491528 | tf_op jit(solution)/shard_map/ppermute | solution.py:400
  20.2 3.8 %collective-permute-done.2.other_ref = f32[5,16,512]{2,1,0:T(8,128)S(1)} collective-permute-done((f32[5,16,512]{2,1,0:T(8,128)S(1)}, f32[5,16,512]{2,1,0:T(8,128)S(1)}, u32[]{:S(2)}, u32[]{:S(2)}) %collective-permute-start.2) | collective-permute-done | bytes 163872 | tf_op jit(solution)/shard_map/ppermute | solution.py:400
  24.1 2.8 %collective-permute-start.3 = (f32[5,16,512]{2,1,0:T(8,128)S(1)}, f32[5,16,512]{2,1,0:T(8,128)S(1)}, u32[]{:S(2)}, u32[]{:S(2)}) collective-permute-start(f32[5,16,512]{2,1,0:T(8,128)S(1)} %get-tuple-element.54.own_ref), channel_id=1, source_target_pairs={{0,48},{16,32},{32,16},{48,0},{64,112},{80,96},{96,80},{112,64},{1... | collective-permute-start | bytes 491528 | tf_op jit(solution)/shard_map/ppermute | solution.py:400
  26.9 2.3 %all-to-all-done.blocks_ref = f32[8,5,16,128]{3,2,1,0:T(8,128)S(1)} async-done(((f32[8,5,16,128]{3,2,1,0:T(8,128)}), f32[8,5,16,128]{3,2,1,0:T(8,128)S(1)}, u32[]{:S(2)}, u32[]{:S(2)}) %all-to-all-start) | async-done | bytes 327712 | tf_op jit(solution)/shard_map/all_to_all | solution.py:461
  29.2 0.8 %y_reduced.1.refs_0_ = f32[8,2,16,128]{3,2,1,0:T(8,128)} custom-call(f32[8,5,16,128]{3,2,1,0:T(8,128)S(1)} %all-to-all-done.blocks_ref), custom_call_target="tpu_custom_call" | custom-call | flops 327680 | bytes 458752 | tf_op jit(solution)/shard_map/y_reduced/pallas_call | solution.py:472
  29.9 0.0 copy-start
  30.0 5.1 %all-to-all-start.1 = ((f32[8,2,16,128]{3,2,1,0:T(8,128)}), f32[8,2,16,128]{3,2,1,0:T(8,128)S(1)}, u32[]{:S(2)}, u32[]{:S(2)}) async-start(f32[8,2,16,128]{3,2,1,0:T(8,128)} %y_reduced.1.refs_0_), calls=%async_computation.1 | async-start | bytes 262144 | tf_op jit(solution)/shard_map/all_to_all | solution.py:501
  35.0 0.0 collective-permute-done.3.other_ref
  35.0 0.0 copy-done
  35.1 1.7 %collective-permute-start.4 = (f32[5,16,512]{2,1,0:T(8,128)S(1)}, f32[5,16,512]{2,1,0:T(8,128)S(1)}, u32[]{:S(2)}, u32[]{:S(2)}) collective-permute-start(f32[5,16,512]{2,1,0:T(8,128)S(1)} %get-tuple-element.59.own_ref), channel_id=1, source_target_pairs={{0,64},{16,80},{32,96},{48,112},{64,0},{80,16},{96,32},{112,48},{1... | collective-permute-start | bytes 491528 | tf_op jit(solution)/shard_map/ppermute | solution.py:400
  36.8 3.7 %collective-permute-done.4.other_ref = f32[5,16,512]{2,1,0:T(8,128)S(1)} collective-permute-done((f32[5,16,512]{2,1,0:T(8,128)S(1)}, f32[5,16,512]{2,1,0:T(8,128)S(1)}, u32[]{:S(2)}, u32[]{:S(2)}) %collective-permute-start.4) | collective-permute-done | bytes 163872 | tf_op jit(solution)/shard_map/ppermute | solution.py:400
  40.5 0.1 x_merge.5
  40.6 3.1 %collective-permute-start.5 = (f32[2,16,512]{2,1,0:T(8,128)S(1)}, f32[2,16,512]{2,1,0:T(8,128)S(1)}, u32[]{:S(2)}, u32[]{:S(2)}) collective-permute-start(f32[2,16,512]{2,1,0:T(8,128)S(1)} %get-tuple-element.71.side_ref), channel_id=1, source_target_pairs={{0,192},{16,208},{32,224},{48,240},{64,128},{80,144},{96,160},{112... | collective-permute-start | bytes 196616 | tf_op jit(solution)/shard_map/ppermute | solution.py:400
  43.7 0.0 all-to-all-done.1.ends_ref
  43.7 2.0 %y_back.1 = (f32[32,16,512]{2,1,0:T(8,128)}, f32[32,16,512]{2,1,0:T(8,128)S(1)}, f32[32,16,512]{2,1,0:T(8,128)S(1)}) custom-call(f32[16,32,512]{2,1,0:T(8,128)S(1)} %get-tuple-element.63.t_ref, f32[16,32,512]{2,1,0:T(8,128)S(1)} %get-tuple-element.64.drive_ref, f32[8,2,16,128]{3,2,1,0:T(8,128)S(1)} %all-to-all-done.1.ends_ref, ...), custom_call_target="tpu_custom_call" | custom-call | flops 1310720 | bytes 3145728 | tf_op jit(solution)/shard_map/y_back/pallas_call | solution.py:386
  45.7 0.5 %collective-permute-done.5.other_ref = f32[2,16,512]{2,1,0:T(8,128)S(1)} collective-permute-done((f32[2,16,512]{2,1,0:T(8,128)S(1)}, f32[2,16,512]{2,1,0:T(8,128)S(1)}, u32[]{:S(2)}, u32[]{:S(2)}) %collective-permute-start.5) | collective-permute-done | bytes 65568 | tf_op jit(solution)/shard_map/ppermute | solution.py:400
  46.1 1.2 %x_back.1 = f32[32,16,512]{2,1,0:T(8,128)} custom-call(f32[32,16,512]{2,1,0:T(8,128)S(1)} %get-tuple-element.68.t_ref, f32[32,16,512]{2,1,0:T(8,128)S(1)} %get-tuple-element.69.drive_ref, f32[13,16,512]{2,1,0:T(8,128)S(1)} %get-tuple-element.70.kept_ref, f32[2,16,512]{2,1,0:T(8,128)S(1)} %get-tuple-element.71.side_ref, ...), custom_call_target="tpu_custom_call" | custom-call | flops 1310720 | bytes 3145728 | tf_op jit(solution)/shard_map/x_back/pallas_call | solution.py:386
  (2 shorter events, 0.1 us)
Async XLA Ops:
  4.4 4.3 %collective-permute-start.1 = (f32[32,512]{1,0:T(8,128)S(1)}, f32[32,512]{1,0:T(8,128)S(1)}, u32[]{:S(2)}, u32[]{:S(2)}) collective-permute-start(f32[32,512]{1,0:T(8,128)S(1)} %get-tuple-element.42), channel_id=1, source_target_pairs={{0,2},{2,4},{4,6},{6,8},{8,10},{10,12},{12,14},{14,0},{1,3},{3,5},... | collective-permute-start | bytes 196616 | tf_op jit(solution)/shard_map/ppermute | solution.py:438
  6.4 1.4 %collective-permute-start = (f32[8,128]{1,0:T(8,128)S(1)}, f32[8,128]{1,0:T(8,128)S(1)}, u32[]{:S(2)}, u32[]{:S(2)}) collective-permute-start(f32[8,128]{1,0:T(8,128)S(1)} %get-tuple-element.37), channel_id=1, source_target_pairs={{0,1},{1,0},{2,3},{3,2},{4,5},{5,4},{6,7},{7,6},{8,9},{9,8},{10,11... | collective-permute-start | bytes 12296 | tf_op jit(solution)/shard_map/ppermute | solution.py:400
  8.7 20.5 %all-to-all-start = ((f32[8,5,16,128]{3,2,1,0:T(8,128)}), f32[8,5,16,128]{3,2,1,0:T(8,128)S(1)}, u32[]{:S(2)}, u32[]{:S(2)}) async-start(f32[8,5,16,128]{3,2,1,0:T(8,128)} %get-tuple-element.55), calls=%async_computation | async-start | bytes 655360 | tf_op jit(solution)/shard_map/all_to_all | solution.py:461
  18.6 5.4 %collective-permute-start.2 = (f32[5,16,512]{2,1,0:T(8,128)S(1)}, f32[5,16,512]{2,1,0:T(8,128)S(1)}, u32[]{:S(2)}, u32[]{:S(2)}) collective-permute-start(f32[5,16,512]{2,1,0:T(8,128)S(1)} %get-tuple-element.50.own_ref), channel_id=1, source_target_pairs={{0,16},{16,0},{32,48},{48,32},{64,80},{80,64},{96,112},{112,96},{1... | collective-permute-start | bytes 491528 | tf_op jit(solution)/shard_map/ppermute | solution.py:400
  24.1 11.0 %collective-permute-start.3 = (f32[5,16,512]{2,1,0:T(8,128)S(1)}, f32[5,16,512]{2,1,0:T(8,128)S(1)}, u32[]{:S(2)}, u32[]{:S(2)}) collective-permute-start(f32[5,16,512]{2,1,0:T(8,128)S(1)} %get-tuple-element.54.own_ref), channel_id=1, source_target_pairs={{0,48},{16,32},{32,16},{48,0},{64,112},{80,96},{96,80},{112,64},{1... | collective-permute-start | bytes 491528 | tf_op jit(solution)/shard_map/ppermute | solution.py:400
  29.9 5.1 %copy-start = (f32[8,2,16,128]{3,2,1,0:T(8,128)S(1)}, f32[8,2,16,128]{3,2,1,0:T(8,128)}, u32[]{:S(2)}) copy-start(f32[8,2,16,128]{3,2,1,0:T(8,128)} %y_reduced.1.refs_0_) | copy-start | bytes 393220
  30.0 13.7 %all-to-all-start.1 = ((f32[8,2,16,128]{3,2,1,0:T(8,128)}), f32[8,2,16,128]{3,2,1,0:T(8,128)S(1)}, u32[]{:S(2)}, u32[]{:S(2)}) async-start(f32[8,2,16,128]{3,2,1,0:T(8,128)} %y_reduced.1.refs_0_), calls=%async_computation.1 | async-start | bytes 262144 | tf_op jit(solution)/shard_map/all_to_all | solution.py:501
  35.1 5.4 %collective-permute-start.4 = (f32[5,16,512]{2,1,0:T(8,128)S(1)}, f32[5,16,512]{2,1,0:T(8,128)S(1)}, u32[]{:S(2)}, u32[]{:S(2)}) collective-permute-start(f32[5,16,512]{2,1,0:T(8,128)S(1)} %get-tuple-element.59.own_ref), channel_id=1, source_target_pairs={{0,64},{16,80},{32,96},{48,112},{64,0},{80,16},{96,32},{112,48},{1... | collective-permute-start | bytes 491528 | tf_op jit(solution)/shard_map/ppermute | solution.py:400
  40.6 5.6 %collective-permute-start.5 = (f32[2,16,512]{2,1,0:T(8,128)S(1)}, f32[2,16,512]{2,1,0:T(8,128)S(1)}, u32[]{:S(2)}, u32[]{:S(2)}) collective-permute-start(f32[2,16,512]{2,1,0:T(8,128)S(1)} %get-tuple-element.71.side_ref), channel_id=1, source_target_pairs={{0,192},{16,208},{32,224},{48,240},{64,128},{80,144},{96,160},{112... | collective-permute-start | bytes 196616 | tf_op jit(solution)/shard_map/ppermute | solution.py:400

commit v6 on v5

--- a/solution.py
+++ b/solution.py
@@ -139,9 +139,9 @@
             for v in range(5):
                 state_s[v, :, pl.ds(k * lane, lane)] = states[k][v]
 
-        for first in range(0, tiles, 2):
-            pair = (first, first + 1)
-            states = [None, None]
+        for first in range(0, tiles, 4):
+            pair = tuple(range(first, first + 4))
+            states = [None] * 4
             for j in range(ys):
                 pick = pl.ds(j * rows, rows)
                 for n, k in enumerate(pair):

time: 47.7 us -> 47.7 us (level)
  no operation moved by 1% of the time
where the time goes in v6:
time: 47.7 us; the launch traced here: 47.4 us
  starting transfers between devices  26.1 us (55%)
  waiting for transfers between devices  10.4 us (22%)
  Pallas kernels  10.3 us (22%)
  between operations  0.69 us (1%)
    all_to_all x1, starting transfers between devices, per_device(): y_blocks = lax.all_to_all(y_reduced, 'gy', 0, 0, tiled=True)  9.78 us
    ppermute x5, starting transfers between devices, exchange(): lax.ppermute(x, axis, [(i, i ^ mask) for i in range(lax.axis_size(axis))])  9.19 us
    pallas_call x8, Pallas kernels, call(): pl.pallas_call(kernel, in_specs=specs, out_specs=out_specs, out_shape=out...  8.57 us
    ppermute x5, waiting for transfers between devices, exchange(): lax.ppermute(x, axis, [(i, i ^ mask) for i in range(lax.axis_size(axis))])  8.05 us
    all_to_all x1, starting transfers between devices, per_device(): y_ends = lax.all_to_all(y_ends, 'gy', 0, 0, tiled=True)  5.09 us
    all_to_all x1, waiting for transfers between devices, per_device(): y_blocks = lax.all_to_all(y_reduced, 'gy', 0, 0, tiled=True)  2.25 us
    ppermute x1, starting transfers between devices, per_device(): lax.ppermute(mx_edge, 'gy', [(i, (i + 1) % count) for i in range(count)])  1.99 us
  transfers between devices with their start and end apart: 8, of which 5 were waited for; matrix products, arithmetic and copies ran while one was open for 0% of the time, Pallas kernels for 11%

profile of v6, /device:TPU:32, one launch (start us, length us, event | category | flops | bytes accessed | tf_op | source)
XLA Modules:
  0.0 47.4 jit_solution(2815506210149579601)
XLA Ops:
  0.6 3.7 %forward.1 = (f32[16,32,512]{2,1,0:T(8,128)S(1)}, f32[16,32,512]{2,1,0:T(8,128)S(1)}, f32[8,5,16,128]{3,2,1,0:T(8,128)S(1)}, f32[32,16,512]{2,1,0:T(8,128)S(1)},...) custom-call(f32[16]{0:T(128)} %table_hbm.1, ...), custom_call_target="tpu_custom_call" | custom-call | flops 15728640 | bytes 10485760 | tf_op jit(solution)/shard_map/forward/pallas_call | solution.py:386
  4.4 2.0 %collective-permute-start.1 = (f32[32,512]{1,0:T(8,128)S(1)}, f32[32,512]{1,0:T(8,128)S(1)}, u32[]{:S(2)}, u32[]{:S(2)}) collective-permute-start(f32[32,512]{1,0:T(8,128)S(1)} %get-tuple-element.42), channel_id=1, source_target_pairs={{0,2},{2,4},{4,6},{6,8},{8,10},{10,12},{12,14},{14,0},{1,3},{3,5},... | collective-permute-start | bytes 196616 | tf_op jit(solution)/shard_map/ppermute | solution.py:438
  6.4 0.0 collective-permute-start
  6.4 1.3 %store.1 = (f32[32,16,512]{2,1,0:T(8,128)}, f32[32,16,512]{2,1,0:T(8,128)}) custom-call(f32[32,16,512]{2,1,0:T(8,128)S(1)} %get-tuple-element.43.t_ref, f32[32,16,512]{2,1,0:T(8,128)S(1)} %get-tuple-element.44.drive_ref), custom_call_target="tpu_custom_call" | custom-call | flops 262144 | bytes 4194304 | tf_op jit(solution)/shard_map/store/pallas_call | solution.py:386
  7.7 0.0 collective-permute-done.edge_ref
  7.7 0.9 %y_edge.1 = (f32[8,5,16,128]{3,2,1,0:T(8,128)}, f32[16,32,512]{2,1,0:T(8,128)S(1)}) custom-call(f32[8,128]{1,0:T(8,128)S(1)} %collective-permute-done.edge_ref, f32[16,32,128]{2,1,0:T(8,128)S(1)} %get-tuple-element.38.t_ref, f32[8,5,16,128]{3,2,1,0:T(8,128)S(1)} %get-tuple-element.39.reduced_ref, ...), custom_call_target="tpu_custom_call", output_to_operand_aliasing={{1}: (3, {})} | custom-call | flops 655360 | bytes 786432 | tf_op jit(solution)/shard_map/y_edge/pallas_call | solution.py:439
  8.7 0.1 collective-permute-done.1.edge_ref
  8.7 9.8 %all-to-all-start = ((f32[8,5,16,128]{3,2,1,0:T(8,128)}), f32[8,5,16,128]{3,2,1,0:T(8,128)S(1)}, u32[]{:S(2)}, u32[]{:S(2)}) async-start(f32[8,5,16,128]{3,2,1,0:T(8,128)} %get-tuple-element.55), calls=%async_computation | async-start | bytes 655360 | tf_op jit(solution)/shard_map/all_to_all | solution.py:461
  18.5 0.1 x_edge.1
  18.6 1.6 %collective-permute-start.2 = (f32[5,16,512]{2,1,0:T(8,128)S(1)}, f32[5,16,512]{2,1,0:T(8,128)S(1)}, u32[]{:S(2)}, u32[]{:S(2)}) collective-permute-start(f32[5,16,512]{2,1,0:T(8,128)S(1)} %get-tuple-element.50.own_ref), channel_id=1, source_target_pairs={{0,16},{16,0},{32,48},{48,32},{64,80},{80,64},{96,112},{112,96},{1... | collective-permute-start | bytes 491528 | tf_op jit(solution)/shard_map/ppermute | solution.py:400
  20.2 3.8 %collective-permute-done.2.other_ref = f32[5,16,512]{2,1,0:T(8,128)S(1)} collective-permute-done((f32[5,16,512]{2,1,0:T(8,128)S(1)}, f32[5,16,512]{2,1,0:T(8,128)S(1)}, u32[]{:S(2)}, u32[]{:S(2)}) %collective-permute-start.2) | collective-permute-done | bytes 163872 | tf_op jit(solution)/shard_map/ppermute | solution.py:400
  24.1 2.8 %collective-permute-start.3 = (f32[5,16,512]{2,1,0:T(8,128)S(1)}, f32[5,16,512]{2,1,0:T(8,128)S(1)}, u32[]{:S(2)}, u32[]{:S(2)}) collective-permute-start(f32[5,16,512]{2,1,0:T(8,128)S(1)} %get-tuple-element.54.own_ref), channel_id=1, source_target_pairs={{0,48},{16,32},{32,16},{48,0},{64,112},{80,96},{96,80},{112,64},{1... | collective-permute-start | bytes 491528 | tf_op jit(solution)/shard_map/ppermute | solution.py:400
  26.9 2.3 %all-to-all-done.blocks_ref = f32[8,5,16,128]{3,2,1,0:T(8,128)S(1)} async-done(((f32[8,5,16,128]{3,2,1,0:T(8,128)}), f32[8,5,16,128]{3,2,1,0:T(8,128)S(1)}, u32[]{:S(2)}, u32[]{:S(2)}) %all-to-all-start) | async-done | bytes 327712 | tf_op jit(solution)/shard_map/all_to_all | solution.py:461
  29.2 0.8 %y_reduced.1.refs_0_ = f32[8,2,16,128]{3,2,1,0:T(8,128)} custom-call(f32[8,5,16,128]{3,2,1,0:T(8,128)S(1)} %all-to-all-done.blocks_ref), custom_call_target="tpu_custom_call" | custom-call | flops 327680 | bytes 458752 | tf_op jit(solution)/shard_map/y_reduced/pallas_call | solution.py:472
  30.0 0.0 copy-start
  30.0 5.1 %all-to-all-start.1 = ((f32[8,2,16,128]{3,2,1,0:T(8,128)}), f32[8,2,16,128]{3,2,1,0:T(8,128)S(1)}, u32[]{:S(2)}, u32[]{:S(2)}) async-start(f32[8,2,16,128]{3,2,1,0:T(8,128)} %y_reduced.1.refs_0_), calls=%async_computation.1 | async-start | bytes 262144 | tf_op jit(solution)/shard_map/all_to_all | solution.py:501
  35.0 0.0 collective-permute-done.3.other_ref
  35.0 0.0 copy-done
  35.1 1.7 %collective-permute-start.4 = (f32[5,16,512]{2,1,0:T(8,128)S(1)}, f32[5,16,512]{2,1,0:T(8,128)S(1)}, u32[]{:S(2)}, u32[]{:S(2)}) collective-permute-start(f32[5,16,512]{2,1,0:T(8,128)S(1)} %get-tuple-element.59.own_ref), channel_id=1, source_target_pairs={{0,64},{16,80},{32,96},{48,112},{64,0},{80,16},{96,32},{112,48},{1... | collective-permute-start | bytes 491528 | tf_op jit(solution)/shard_map/ppermute | solution.py:400
  36.8 3.7 %collective-permute-done.4.other_ref = f32[5,16,512]{2,1,0:T(8,128)S(1)} collective-permute-done((f32[5,16,512]{2,1,0:T(8,128)S(1)}, f32[5,16,512]{2,1,0:T(8,128)S(1)}, u32[]{:S(2)}, u32[]{:S(2)}) %collective-permute-start.4) | collective-permute-done | bytes 163872 | tf_op jit(solution)/shard_map/ppermute | solution.py:400
  40.5 0.1 x_merge.5
  40.6 3.1 %collective-permute-start.5 = (f32[2,16,512]{2,1,0:T(8,128)S(1)}, f32[2,16,512]{2,1,0:T(8,128)S(1)}, u32[]{:S(2)}, u32[]{:S(2)}) collective-permute-start(f32[2,16,512]{2,1,0:T(8,128)S(1)} %get-tuple-element.71.side_ref), channel_id=1, source_target_pairs={{0,192},{16,208},{32,224},{48,240},{64,128},{80,144},{96,160},{112... | collective-permute-start | bytes 196616 | tf_op jit(solution)/shard_map/ppermute | solution.py:400
  43.7 0.0 all-to-all-done.1.ends_ref
  43.7 2.0 %y_back.1 = (f32[32,16,512]{2,1,0:T(8,128)}, f32[32,16,512]{2,1,0:T(8,128)S(1)}, f32[32,16,512]{2,1,0:T(8,128)S(1)}) custom-call(f32[16,32,512]{2,1,0:T(8,128)S(1)} %get-tuple-element.63.t_ref, f32[16,32,512]{2,1,0:T(8,128)S(1)} %get-tuple-element.64.drive_ref, f32[8,2,16,128]{3,2,1,0:T(8,128)S(1)} %all-to-all-done.1.ends_ref, ...), custom_call_target="tpu_custom_call" | custom-call | flops 1310720 | bytes 3145728 | tf_op jit(solution)/shard_map/y_back/pallas_call | solution.py:386
  45.7 0.5 %collective-permute-done.5.other_ref = f32[2,16,512]{2,1,0:T(8,128)S(1)} collective-permute-done((f32[2,16,512]{2,1,0:T(8,128)S(1)}, f32[2,16,512]{2,1,0:T(8,128)S(1)}, u32[]{:S(2)}, u32[]{:S(2)}) %collective-permute-start.5) | collective-permute-done | bytes 65568 | tf_op jit(solution)/shard_map/ppermute | solution.py:400
  46.1 1.2 %x_back.1 = f32[32,16,512]{2,1,0:T(8,128)} custom-call(f32[32,16,512]{2,1,0:T(8,128)S(1)} %get-tuple-element.68.t_ref, f32[32,16,512]{2,1,0:T(8,128)S(1)} %get-tuple-element.69.drive_ref, f32[13,16,512]{2,1,0:T(8,128)S(1)} %get-tuple-element.70.kept_ref, f32[2,16,512]{2,1,0:T(8,128)S(1)} %get-tuple-element.71.side_ref, ...), custom_call_target="tpu_custom_call" | custom-call | flops 1310720 | bytes 3145728 | tf_op jit(solution)/shard_map/x_back/pallas_call | solution.py:386
  (2 shorter events, 0.1 us)
Async XLA Ops:
  4.4 4.3 %collective-permute-start.1 = (f32[32,512]{1,0:T(8,128)S(1)}, f32[32,512]{1,0:T(8,128)S(1)}, u32[]{:S(2)}, u32[]{:S(2)}) collective-permute-start(f32[32,512]{1,0:T(8,128)S(1)} %get-tuple-element.42), channel_id=1, source_target_pairs={{0,2},{2,4},{4,6},{6,8},{8,10},{10,12},{12,14},{14,0},{1,3},{3,5},... | collective-permute-start | bytes 196616 | tf_op jit(solution)/shard_map/ppermute | solution.py:438
  6.4 1.4 %collective-permute-start = (f32[8,128]{1,0:T(8,128)S(1)}, f32[8,128]{1,0:T(8,128)S(1)}, u32[]{:S(2)}, u32[]{:S(2)}) collective-permute-start(f32[8,128]{1,0:T(8,128)S(1)} %get-tuple-element.37), channel_id=1, source_target_pairs={{0,1},{1,0},{2,3},{3,2},{4,5},{5,4},{6,7},{7,6},{8,9},{9,8},{10,11... | collective-permute-start | bytes 12296 | tf_op jit(solution)/shard_map/ppermute | solution.py:400
  8.7 20.5 %all-to-all-start = ((f32[8,5,16,128]{3,2,1,0:T(8,128)}), f32[8,5,16,128]{3,2,1,0:T(8,128)S(1)}, u32[]{:S(2)}, u32[]{:S(2)}) async-start(f32[8,5,16,128]{3,2,1,0:T(8,128)} %get-tuple-element.55), calls=%async_computation | async-start | bytes 655360 | tf_op jit(solution)/shard_map/all_to_all | solution.py:461
  18.6 5.4 %collective-permute-start.2 = (f32[5,16,512]{2,1,0:T(8,128)S(1)}, f32[5,16,512]{2,1,0:T(8,128)S(1)}, u32[]{:S(2)}, u32[]{:S(2)}) collective-permute-start(f32[5,16,512]{2,1,0:T(8,128)S(1)} %get-tuple-element.50.own_ref), channel_id=1, source_target_pairs={{0,16},{16,0},{32,48},{48,32},{64,80},{80,64},{96,112},{112,96},{1... | collective-permute-start | bytes 491528 | tf_op jit(solution)/shard_map/ppermute | solution.py:400
  24.1 11.0 %collective-permute-start.3 = (f32[5,16,512]{2,1,0:T(8,128)S(1)}, f32[5,16,512]{2,1,0:T(8,128)S(1)}, u32[]{:S(2)}, u32[]{:S(2)}) collective-permute-start(f32[5,16,512]{2,1,0:T(8,128)S(1)} %get-tuple-element.54.own_ref), channel_id=1, source_target_pairs={{0,48},{16,32},{32,16},{48,0},{64,112},{80,96},{96,80},{112,64},{1... | collective-permute-start | bytes 491528 | tf_op jit(solution)/shard_map/ppermute | solution.py:400
  30.0 5.1 %copy-start = (f32[8,2,16,128]{3,2,1,0:T(8,128)S(1)}, f32[8,2,16,128]{3,2,1,0:T(8,128)}, u32[]{:S(2)}) copy-start(f32[8,2,16,128]{3,2,1,0:T(8,128)} %y_reduced.1.refs_0_) | copy-start | bytes 393220
  30.0 13.7 %all-to-all-start.1 = ((f32[8,2,16,128]{3,2,1,0:T(8,128)}), f32[8,2,16,128]{3,2,1,0:T(8,128)S(1)}, u32[]{:S(2)}, u32[]{:S(2)}) async-start(f32[8,2,16,128]{3,2,1,0:T(8,128)} %y_reduced.1.refs_0_), calls=%async_computation.1 | async-start | bytes 262144 | tf_op jit(solution)/shard_map/all_to_all | solution.py:501
  35.1 5.4 %collective-permute-start.4 = (f32[5,16,512]{2,1,0:T(8,128)S(1)}, f32[5,16,512]{2,1,0:T(8,128)S(1)}, u32[]{:S(2)}, u32[]{:S(2)}) collective-permute-start(f32[5,16,512]{2,1,0:T(8,128)S(1)} %get-tuple-element.59.own_ref), channel_id=1, source_target_pairs={{0,64},{16,80},{32,96},{48,112},{64,0},{80,16},{96,32},{112,48},{1... | collective-permute-start | bytes 491528 | tf_op jit(solution)/shard_map/ppermute | solution.py:400
  40.6 5.6 %collective-permute-start.5 = (f32[2,16,512]{2,1,0:T(8,128)S(1)}, f32[2,16,512]{2,1,0:T(8,128)S(1)}, u32[]{:S(2)}, u32[]{:S(2)}) collective-permute-start(f32[2,16,512]{2,1,0:T(8,128)S(1)} %get-tuple-element.71.side_ref), channel_id=1, source_target_pairs={{0,192},{16,208},{32,224},{48,240},{64,128},{80,144},{96,160},{112... | collective-permute-start | bytes 196616 | tf_op jit(solution)/shard_map/ppermute | solution.py:400

commit v7 on v6

--- a/solution.py
+++ b/solution.py
@@ -13,6 +13,7 @@
 rows = 8
 f32 = jnp.float32
 vmem_spec = pl.BlockSpec(memory_space=pltpu.VMEM)
+free_spec = pl.BlockSpec(memory_space=pltpu.VMEM)
 any_spec = pl.BlockSpec(memory_space=pl.ANY)
 hbm_spec = pl.BlockSpec(memory_space=pltpu.HBM)
 
@@ -298,12 +299,9 @@
 
 
 def y_back_kernel(
-    t_ref, drive_ref, ends_ref, xt_hbm, xdrive_hbm, out_hbm, xt_ref, xdrive_ref, turn_s, out_s, sems, load_sems
+    t_ref, drive_ref, ends_ref, xt_hbm, out_hbm, xt_ref, turn_s, out_s, sems, load_sem
 ):
-    loads = [
-        pltpu.make_async_copy(xt_hbm, xt_ref, load_sems.at[0]),
-        pltpu.make_async_copy(xdrive_hbm, xdrive_ref, load_sems.at[1]),
-    ]
+    loads = [pltpu.make_async_copy(xt_hbm, xt_ref, load_sem)]
     for load in loads:
         load.start()
     ys, xs, zs = t_ref.shape
@@ -500,19 +498,19 @@
     side_other = exchange(own, "gx", 12)
     y_ends = lax.all_to_all(y_ends, "gy", 0, 0, tiled=True)
 
-    electric_x_half, x_t, x_drive = call(
+    electric_x_half, x_t = call(
         y_back_kernel,
         "y_back",
-        [(vmem_spec, a) for a in (y_t, y_drive, y_ends)] + [(hbm_spec, a) for a in (x_t, x_drive)],
-        [(hbm_spec, H((xs, ys, zs), f32))] + [(vmem_spec, V((xs, ys, zs), f32))] * 2,
+        [(vmem_spec, a) for a in (y_t, y_drive, y_ends)] + [(hbm_spec, x_t)],
+        [(hbm_spec, H((xs, ys, zs), f32)), (vmem_spec, V((xs, ys, zs), f32))],
         scratch=[V((zs // lane, rows * ys, lane), f32), V((xs, ys, zs), f32)]
-        + [pltpu.SemaphoreType.DMA((chunks,)), pltpu.SemaphoreType.DMA((2,))],
+        + [pltpu.SemaphoreType.DMA((chunks,)), pltpu.SemaphoreType.DMA],
         work=cost(cells, 5, 3),
     )
     (electric_z_half,) = call(
         x_back_kernel,
         "x_back",
-        [(vmem_spec, a) for a in (x_t, x_drive, kept, own, side_other)],
+        [(vmem_spec, x_t), (free_spec, x_drive)] + [(vmem_spec, a) for a in (kept, own, side_other)],
         [(vmem_spec, H((xs, ys, zs), f32))],
         work=cost(cells, 5, 3),
     )

time: 47.7 us -> 47.7 us (level)
  no operation moved by 1% of the time
where the time goes in v7:
time: 47.7 us; the launch traced here: 47.4 us
  starting transfers between devices  26.1 us (55%)
  waiting for transfers between devices  10.6 us (22%)
  Pallas kernels  10 us (21%)
  between operations  0.7 us (1%)
    all_to_all x1, starting transfers between devices, per_device(): y_blocks = lax.all_to_all(y_reduced, 'gy', 0, 0, tiled=True)  9.78 us
    ppermute x5, starting transfers between devices, exchange(): lax.ppermute(x, axis, [(i, i ^ mask) for i in range(lax.axis_size(axis))])  9.19 us
    pallas_call x8, Pallas kernels, call(): pl.pallas_call(kernel, in_specs=specs, out_specs=out_specs, out_shape=out...  8.34 us
    ppermute x5, waiting for transfers between devices, exchange(): lax.ppermute(x, axis, [(i, i ^ mask) for i in range(lax.axis_size(axis))])  8.29 us
    all_to_all x1, starting transfers between devices, per_device(): y_ends = lax.all_to_all(y_ends, 'gy', 0, 0, tiled=True)  5.09 us
    all_to_all x1, waiting for transfers between devices, per_device(): y_blocks = lax.all_to_all(y_reduced, 'gy', 0, 0, tiled=True)  2.25 us
    ppermute x1, starting transfers between devices, per_device(): lax.ppermute(mx_edge, 'gy', [(i, (i + 1) % count) for i in range(count)])  1.99 us
  transfers between devices with their start and end apart: 8, of which 5 were waited for; matrix products, arithmetic and copies ran while one was open for 0% of the time, Pallas kernels for 11%

profile of v7, /device:TPU:32, one launch (start us, length us, event | category | flops | bytes accessed | tf_op | source)
XLA Modules:
  0.0 47.4 jit_solution(865097425763011878)
XLA Ops:
  0.6 3.8 %forward.1 = (f32[16,32,512]{2,1,0:T(8,128)S(1)}, f32[16,32,512]{2,1,0:T(8,128)S(1)}, f32[8,5,16,128]{3,2,1,0:T(8,128)S(1)}, f32[32,16,512]{2,1,0:T(8,128)S(1)},...) custom-call(f32[16]{0:T(128)} %table_hbm.1, ...), custom_call_target="tpu_custom_call" | custom-call | flops 15728640 | bytes 10485760 | tf_op jit(solution)/shard_map/forward/pallas_call | solution.py:384
  4.4 2.0 %collective-permute-start.1 = (f32[32,512]{1,0:T(8,128)S(1)}, f32[32,512]{1,0:T(8,128)S(1)}, u32[]{:S(2)}, u32[]{:S(2)}) collective-permute-start(f32[32,512]{1,0:T(8,128)S(1)} %get-tuple-element.41), channel_id=1, source_target_pairs={{0,2},{2,4},{4,6},{6,8},{8,10},{10,12},{12,14},{14,0},{1,3},{3,5},... | collective-permute-start | bytes 196616 | tf_op jit(solution)/shard_map/ppermute | solution.py:436
  6.4 0.0 collective-permute-start
  6.4 1.3 %store.1 = (f32[32,16,512]{2,1,0:T(8,128)}, f32[32,16,512]{2,1,0:T(8,128)}) custom-call(f32[32,16,512]{2,1,0:T(8,128)S(1)} %get-tuple-element.42.t_ref, f32[32,16,512]{2,1,0:T(8,128)S(1)} %get-tuple-element.43.drive_ref), custom_call_target="tpu_custom_call" | custom-call | flops 262144 | bytes 4194304 | tf_op jit(solution)/shard_map/store/pallas_call | solution.py:384
  7.7 0.0 collective-permute-done.edge_ref
  7.8 0.9 %y_edge.1 = (f32[8,5,16,128]{3,2,1,0:T(8,128)}, f32[16,32,512]{2,1,0:T(8,128)S(1)}) custom-call(f32[8,128]{1,0:T(8,128)S(1)} %collective-permute-done.edge_ref, f32[16,32,128]{2,1,0:T(8,128)S(1)} %get-tuple-element.37.t_ref, f32[8,5,16,128]{3,2,1,0:T(8,128)S(1)} %get-tuple-element.38.reduced_ref, ...), custom_call_target="tpu_custom_call", output_to_operand_aliasing={{1}: (3, {})} | custom-call | flops 655360 | bytes 786432 | tf_op jit(solution)/shard_map/y_edge/pallas_call | solution.py:437
  8.7 0.1 collective-permute-done.1.edge_ref
  8.7 9.8 %all-to-all-start = ((f32[8,5,16,128]{3,2,1,0:T(8,128)}), f32[8,5,16,128]{3,2,1,0:T(8,128)S(1)}, u32[]{:S(2)}, u32[]{:S(2)}) async-start(f32[8,5,16,128]{3,2,1,0:T(8,128)} %get-tuple-element.54), calls=%async_computation | async-start | bytes 655360 | tf_op jit(solution)/shard_map/all_to_all | solution.py:459
  18.5 0.1 x_edge.1
  18.6 1.6 %collective-permute-start.2 = (f32[5,16,512]{2,1,0:T(8,128)S(1)}, f32[5,16,512]{2,1,0:T(8,128)S(1)}, u32[]{:S(2)}, u32[]{:S(2)}) collective-permute-start(f32[5,16,512]{2,1,0:T(8,128)S(1)} %get-tuple-element.49.own_ref), channel_id=1, source_target_pairs={{0,16},{16,0},{32,48},{48,32},{64,80},{80,64},{96,112},{112,96},{1... | collective-permute-start | bytes 491528 | tf_op jit(solution)/shard_map/ppermute | solution.py:398
  20.2 3.8 %collective-permute-done.2.other_ref = f32[5,16,512]{2,1,0:T(8,128)S(1)} collective-permute-done((f32[5,16,512]{2,1,0:T(8,128)S(1)}, f32[5,16,512]{2,1,0:T(8,128)S(1)}, u32[]{:S(2)}, u32[]{:S(2)}) %collective-permute-start.2) | collective-permute-done | bytes 163872 | tf_op jit(solution)/shard_map/ppermute | solution.py:398
  24.1 2.8 %collective-permute-start.3 = (f32[5,16,512]{2,1,0:T(8,128)S(1)}, f32[5,16,512]{2,1,0:T(8,128)S(1)}, u32[]{:S(2)}, u32[]{:S(2)}) collective-permute-start(f32[5,16,512]{2,1,0:T(8,128)S(1)} %get-tuple-element.53.own_ref), channel_id=1, source_target_pairs={{0,48},{16,32},{32,16},{48,0},{64,112},{80,96},{96,80},{112,64},{1... | collective-permute-start | bytes 491528 | tf_op jit(solution)/shard_map/ppermute | solution.py:398
  26.9 2.3 %all-to-all-done.blocks_ref = f32[8,5,16,128]{3,2,1,0:T(8,128)S(1)} async-done(((f32[8,5,16,128]{3,2,1,0:T(8,128)}), f32[8,5,16,128]{3,2,1,0:T(8,128)S(1)}, u32[]{:S(2)}, u32[]{:S(2)}) %all-to-all-start) | async-done | bytes 327712 | tf_op jit(solution)/shard_map/all_to_all | solution.py:459
  29.2 0.8 %y_reduced.1.refs_0_ = f32[8,2,16,128]{3,2,1,0:T(8,128)} custom-call(f32[8,5,16,128]{3,2,1,0:T(8,128)S(1)} %all-to-all-done.blocks_ref), custom_call_target="tpu_custom_call" | custom-call | flops 327680 | bytes 458752 | tf_op jit(solution)/shard_map/y_reduced/pallas_call | solution.py:470
  30.0 0.0 copy-start
  30.0 5.1 %all-to-all-start.1 = ((f32[8,2,16,128]{3,2,1,0:T(8,128)}), f32[8,2,16,128]{3,2,1,0:T(8,128)S(1)}, u32[]{:S(2)}, u32[]{:S(2)}) async-start(f32[8,2,16,128]{3,2,1,0:T(8,128)} %y_reduced.1.refs_0_), calls=%async_computation.1 | async-start | bytes 262144 | tf_op jit(solution)/shard_map/all_to_all | solution.py:499
  35.0 0.0 collective-permute-done.3.other_ref
  35.1 0.0 copy-done
  35.1 1.7 %collective-permute-start.4 = (f32[5,16,512]{2,1,0:T(8,128)S(1)}, f32[5,16,512]{2,1,0:T(8,128)S(1)}, u32[]{:S(2)}, u32[]{:S(2)}) collective-permute-start(f32[5,16,512]{2,1,0:T(8,128)S(1)} %get-tuple-element.58.own_ref), channel_id=1, source_target_pairs={{0,64},{16,80},{32,96},{48,112},{64,0},{80,16},{96,32},{112,48},{1... | collective-permute-start | bytes 491528 | tf_op jit(solution)/shard_map/ppermute | solution.py:398
  36.8 3.7 %collective-permute-done.4.other_ref = f32[5,16,512]{2,1,0:T(8,128)S(1)} collective-permute-done((f32[5,16,512]{2,1,0:T(8,128)S(1)}, f32[5,16,512]{2,1,0:T(8,128)S(1)}, u32[]{:S(2)}, u32[]{:S(2)}) %collective-permute-start.4) | collective-permute-done | bytes 163872 | tf_op jit(solution)/shard_map/ppermute | solution.py:398
  40.5 0.1 x_merge.5
  40.6 3.1 %collective-permute-start.5 = (f32[2,16,512]{2,1,0:T(8,128)S(1)}, f32[2,16,512]{2,1,0:T(8,128)S(1)}, u32[]{:S(2)}, u32[]{:S(2)}) collective-permute-start(f32[2,16,512]{2,1,0:T(8,128)S(1)} %get-tuple-element.69.side_ref), channel_id=1, source_target_pairs={{0,192},{16,208},{32,224},{48,240},{64,128},{80,144},{96,160},{112... | collective-permute-start | bytes 196616 | tf_op jit(solution)/shard_map/ppermute | solution.py:398
  43.7 0.0 all-to-all-done.1.ends_ref
  43.7 0.0 copy-start.1
  43.7 1.7 %y_back.1 = (f32[32,16,512]{2,1,0:T(8,128)}, f32[32,16,512]{2,1,0:T(8,128)S(1)}) custom-call(f32[16,32,512]{2,1,0:T(8,128)S(1)} %get-tuple-element.62.t_ref, f32[16,32,512]{2,1,0:T(8,128)S(1)} %get-tuple-element.63.drive_ref, f32[8,2,16,128]{3,2,1,0:T(8,128)S(1)} %all-to-all-done.1.ends_ref, f32[32,16,512]{2,1,0:T(8,128)} %get-tuple-element.64.xt_hbm), custom_call_target="tpu_custom_call" | custom-call | flops 1310720 | bytes 3145728 | tf_op jit(solution)/shard_map/y_back/pallas_call | solution.py:384
  45.4 0.7 %collective-permute-done.5.other_ref = f32[2,16,512]{2,1,0:T(8,128)S(1)} collective-permute-done((f32[2,16,512]{2,1,0:T(8,128)S(1)}, f32[2,16,512]{2,1,0:T(8,128)S(1)}, u32[]{:S(2)}, u32[]{:S(2)}) %collective-permute-start.5) | collective-permute-done | bytes 65568 | tf_op jit(solution)/shard_map/ppermute | solution.py:398
  46.1 0.0 copy-done.1
  46.1 1.2 %x_back.1 = f32[32,16,512]{2,1,0:T(8,128)} custom-call(f32[32,16,512]{2,1,0:T(8,128)S(1)} %get-tuple-element.66.t_ref, f32[32,16,512]{2,1,0:T(8,128)S(1)} %copy-done.1, f32[13,16,512]{2,1,0:T(8,128)S(1)} %get-tuple-element.68.kept_ref, f32[2,16,512]{2,1,0:T(8,128)S(1)} %get-tuple-element.69.side_ref, f32[2,16,512]{2,1,0:T(8,128)S(1)} %collective-permute-done.5.other_ref), custom_call_target="tpu_custom_call" | custom-call | flops 1310720 | bytes 3145728 | tf_op jit(solution)/shard_map/x_back/pallas_call | solution.py:384
  (2 shorter events, 0.1 us)
Async XLA Ops:
  4.4 4.3 %collective-permute-start.1 = (f32[32,512]{1,0:T(8,128)S(1)}, f32[32,512]{1,0:T(8,128)S(1)}, u32[]{:S(2)}, u32[]{:S(2)}) collective-permute-start(f32[32,512]{1,0:T(8,128)S(1)} %get-tuple-element.41), channel_id=1, source_target_pairs={{0,2},{2,4},{4,6},{6,8},{8,10},{10,12},{12,14},{14,0},{1,3},{3,5},... | collective-permute-start | bytes 196616 | tf_op jit(solution)/shard_map/ppermute | solution.py:436
  6.4 1.4 %collective-permute-start = (f32[8,128]{1,0:T(8,128)S(1)}, f32[8,128]{1,0:T(8,128)S(1)}, u32[]{:S(2)}, u32[]{:S(2)}) collective-permute-start(f32[8,128]{1,0:T(8,128)S(1)} %get-tuple-element.36), channel_id=1, source_target_pairs={{0,1},{1,0},{2,3},{3,2},{4,5},{5,4},{6,7},{7,6},{8,9},{9,8},{10,11... | collective-permute-start | bytes 12296 | tf_op jit(solution)/shard_map/ppermute | solution.py:398
  8.7 20.5 %all-to-all-start = ((f32[8,5,16,128]{3,2,1,0:T(8,128)}), f32[8,5,16,128]{3,2,1,0:T(8,128)S(1)}, u32[]{:S(2)}, u32[]{:S(2)}) async-start(f32[8,5,16,128]{3,2,1,0:T(8,128)} %get-tuple-element.54), calls=%async_computation | async-start | bytes 655360 | tf_op jit(solution)/shard_map/all_to_all | solution.py:459
  18.6 5.4 %collective-permute-start.2 = (f32[5,16,512]{2,1,0:T(8,128)S(1)}, f32[5,16,512]{2,1,0:T(8,128)S(1)}, u32[]{:S(2)}, u32[]{:S(2)}) collective-permute-start(f32[5,16,512]{2,1,0:T(8,128)S(1)} %get-tuple-element.49.own_ref), channel_id=1, source_target_pairs={{0,16},{16,0},{32,48},{48,32},{64,80},{80,64},{96,112},{112,96},{1... | collective-permute-start | bytes 491528 | tf_op jit(solution)/shard_map/ppermute | solution.py:398
  24.1 11.0 %collective-permute-start.3 = (f32[5,16,512]{2,1,0:T(8,128)S(1)}, f32[5,16,512]{2,1,0:T(8,128)S(1)}, u32[]{:S(2)}, u32[]{:S(2)}) collective-permute-start(f32[5,16,512]{2,1,0:T(8,128)S(1)} %get-tuple-element.53.own_ref), channel_id=1, source_target_pairs={{0,48},{16,32},{32,16},{48,0},{64,112},{80,96},{96,80},{112,64},{1... | collective-permute-start | bytes 491528 | tf_op jit(solution)/shard_map/ppermute | solution.py:398
  30.0 5.1 %copy-start = (f32[8,2,16,128]{3,2,1,0:T(8,128)S(1)}, f32[8,2,16,128]{3,2,1,0:T(8,128)}, u32[]{:S(2)}) copy-start(f32[8,2,16,128]{3,2,1,0:T(8,128)} %y_reduced.1.refs_0_) | copy-start | bytes 393220
  30.0 13.7 %all-to-all-start.1 = ((f32[8,2,16,128]{3,2,1,0:T(8,128)}), f32[8,2,16,128]{3,2,1,0:T(8,128)S(1)}, u32[]{:S(2)}, u32[]{:S(2)}) async-start(f32[8,2,16,128]{3,2,1,0:T(8,128)} %y_reduced.1.refs_0_), calls=%async_computation.1 | async-start | bytes 262144 | tf_op jit(solution)/shard_map/all_to_all | solution.py:499
  35.1 5.4 %collective-permute-start.4 = (f32[5,16,512]{2,1,0:T(8,128)S(1)}, f32[5,16,512]{2,1,0:T(8,128)S(1)}, u32[]{:S(2)}, u32[]{:S(2)}) collective-permute-start(f32[5,16,512]{2,1,0:T(8,128)S(1)} %get-tuple-element.58.own_ref), channel_id=1, source_target_pairs={{0,64},{16,80},{32,96},{48,112},{64,0},{80,16},{96,32},{112,48},{1... | collective-permute-start | bytes 491528 | tf_op jit(solution)/shard_map/ppermute | solution.py:398
  40.6 5.6 %collective-permute-start.5 = (f32[2,16,512]{2,1,0:T(8,128)S(1)}, f32[2,16,512]{2,1,0:T(8,128)S(1)}, u32[]{:S(2)}, u32[]{:S(2)}) collective-permute-start(f32[2,16,512]{2,1,0:T(8,128)S(1)} %get-tuple-element.69.side_ref), channel_id=1, source_target_pairs={{0,192},{16,208},{32,224},{48,240},{64,128},{80,144},{96,160},{112... | collective-permute-start | bytes 196616 | tf_op jit(solution)/shard_map/ppermute | solution.py:398
  43.7 2.5 %copy-start.1 = (f32[32,16,512]{2,1,0:T(8,128)S(1)}, f32[32,16,512]{2,1,0:T(8,128)}, u32[]{:S(2)}) copy-start(f32[32,16,512]{2,1,0:T(8,128)} %get-tuple-element.67.drive_ref) | copy-start | bytes 3145732
